TPU v7x, 32 devices: a whole 2x2x4 slice. The times are simulated.
32 devices in a mesh: line: 4 (over y, core), bus: 8 (over z, x).
Axes of the slice: x: 2, y: 2, z: 4, core: 2. Of those that a mesh axis runs over, the one named last changes fastest.
Arguments:
- site_values: float32 [512, 32768], P('line', 'bus'), may hold values from -6 to 6
- site_bus: int32 [32768], replicated, may hold values from 0 to 71679, as said below
- block_count: int32 [88, 8], P('line', 'bus'), may hold values from 0 to 3
- block_zone: int32 [88, 24], P('line', 'bus'), may hold values from 0 to 13, as said below
- ptdf_blocks: bfloat16 [88, 24, 512, 640], P('line', 'bus'), may hold values from -0.078125 to 0.078125
- rating: float32 [45056], P('line'), may hold values from 0.5 to 4
Outputs:
- loading: float32 [512, 45056], P('bus', 'line')
- worst: float32 [45056], P('line')
Inputs may be any that keep to these rules, and one draw needn't show every extreme that they name: `site_bus`: every aligned block of 4096 sites holds exactly 512 sites whose bus lies in each bus group, the range of 8960 consecutive buses; bus 0 and the last bus each carry a site. `block_zone`: for each line zone, the 3 slots of one bus group name distinct zones of that group.
All inputs are finite; a program needn't handle non-finite values.
Results may differ from a plain program's by a relative error of at most 0.015.
Values may be sent and summed in bfloat16 or wider, within the bound.
No kernel may reach another device: no remote copies, remote signals or barrier semaphores. Data moves between devices by JAX's collectives and lax.ppermute only.
A program may use at most 128 MiB of HBM per device.

v0:
```python
import jax
import jax.numpy as jnp
from jax import lax
from jax.sharding import PartitionSpec as P

NB = 71680


def body(site_values, site_bus, block_count, block_zone, ptdf_blocks, rating):
    here = lax.axis_index("bus")
    groups = lax.axis_size("bus")
    scen_part, site_dev = site_values.shape
    bus_dev = NB // groups
    own_ids = lax.dynamic_slice_in_dim(site_bus, here * site_dev, site_dev)
    order = jnp.argsort(own_ids // bus_dev, stable=True)
    outgoing = jnp.take(site_values, order, axis=1)
    sorted_offsets = (jnp.take(own_ids, order) % bus_dev).astype(jnp.float32)
    per_group = site_dev // groups
    grouped_vals = jnp.transpose(outgoing.reshape(scen_part, groups, per_group), (1, 0, 2))
    grouped_offs = sorted_offsets.reshape(groups, per_group)
    columns = jnp.arange(bus_dev).astype(jnp.float32)

    def one_group(carry, inputs):
        vals, offs = inputs
        table = (offs[:, None] == columns[None, :]).astype(jnp.float32)
        return (
            carry,
            jnp.dot(
                vals, table, precision=lax.Precision.HIGHEST, preferred_element_type=jnp.float32
            ),
        )

    _, spread = lax.scan(one_group, jnp.float32(0.0), (grouped_vals, grouped_offs))
    every_bus = jnp.transpose(spread, (1, 0, 2)).reshape(scen_part, groups * bus_dev)
    partial_value = lax.psum_scatter(
        every_bus.astype(jnp.bfloat16), "bus", scatter_dimension=1, tiled=True
    )
    injection = lax.all_gather(partial_value, "line", axis=0, tiled=True)
    zones_dev, slots_dev = block_zone.shape
    line_zone = ptdf_blocks.shape[2]
    zone_width = ptdf_blocks.shape[3]
    bus_zones = bus_dev // zone_width
    count_col = block_count[:, 0]
    scen_total = injection.shape[0]
    rows_here = injection.reshape(
        lax.axis_size("bus") * (scen_total // groups), bus_zones, zone_width
    )

    def one_zone(carry, inputs):
        live_count, zones, blocks = inputs
        total = jnp.zeros((lax.axis_size("bus") * (scen_total // groups), line_zone), jnp.float32)
        for slot in range(slots_dev):
            piece = lax.dynamic_index_in_dim(rows_here, zones[slot], 1, keepdims=False)
            block = blocks[slot]
            total = lax.cond(
                slot < live_count,
                lambda acc: acc
                + lax.dot_general(
                    piece, block, (((1,), (1,)), ((), ())), preferred_element_type=jnp.float32
                ),
                lambda acc: acc,
                total,
            )
        return (carry, total)

    _, stacked = lax.scan(one_zone, jnp.float32(0.0), (count_col, block_zone, ptdf_blocks))
    flow = lax.psum_scatter(
        jnp.transpose(stacked, (1, 0, 2))
        .reshape(lax.axis_size("bus") * (scen_total // groups), zones_dev * line_zone)
        .astype(jnp.bfloat16),
        "bus",
        scatter_dimension=0,
        tiled=True,
    ).astype(jnp.float32)
    loading = flow / rating[None, :]
    local_worst = jnp.max(jnp.abs(loading), axis=0)
    worst = lax.pmax(local_worst, "bus")
    return (loading, worst)


def solution(mesh):
    return jax.shard_map(
        body,
        mesh=mesh,
        in_specs=(
            P("line", "bus"),
            P(),
            P("line", "bus"),
            P("line", "bus"),
            P("line", "bus", None, None),
            P("line"),
        ),
        out_specs=(P("bus", "line"), P("line")),
        check_vma=False,
    )
```

profile of v0, /device:TPU:0, one launch (start us, length us, event | category | flops | bytes accessed | tf_op | source)
XLA Modules:
  0.0 1134.6 jit_solution(5057524608357216114)
XLA Ops:
  8.0 5.8 sort.17
  13.8 23.0 %gather_fusion.1 = s32[4096]{0:T(1024)S(1)} fusion(s32[4096]{0:T(1024)S(1)} %get-tuple-element.266, s32[4096]{0:T(1024)S(1)} %fusion.34), kind=kCustom, calls=%fused_computation.1 | custom fusion | bytes 49152 | tf_op jit(solution)/shard_map/jit(_take)/gather | solution.py:17
  36.8 1.9 copy.19
  38.8 14.2 %gather_fusion = f32[4096,128]{1,0:T(8,128)} fusion(f32[128,4096]{0,1:T(8,128)S(1)} %copy.19, s32[4096]{0:T(1024)S(1)} %fusion.34), kind=kCustom, calls=%fused_computation | custom fusion | bytes 4210688 | tf_op jit(solution)/shard_map/jit(_take)/gather | solution.py:16
  53.0 1.9 copy.20
  54.9 1.7 select_bitcast_fusion
  56.7 134.9 %while.22 = (s32[]{:T(128)}, bf16[8,128,8960]{1,2,0:T(8,128)(2,1)}, f32[8,128,512]{2,1,0:T(8,128)}, f32[8,512]{1,0:T(8,128)S(1)}, s32[]{:T(128)}) while((s32[]{:T(128)}, bf16[8,128,8960]{1,2,0:T(8,128)(2,1)}, f32[8,128,512]{2,1,0:T(8,128)}, f32[8,512]{1,0:T(8,128)S(1)}, s32[]{:T(128)}) %tuple.96), condition=%wide.region_2.3_spmd.clone, body=%wide.region_1.2_spmd.clone.sunk | while | flops 7051027456 | bytes 4928577 | solution.py:33
  56.7 16.9 %fusion.43 = bf16[8,128,8960]{1,2,0:T(8,128)(2,1)} fusion(bf16[8,128,8960]{1,2,0:T(8,128)(2,1)} %get-tuple-element.345, s32[]{:T(128)} %get-tuple-element.344, f32[8960]{0:T(1024)S(1)} %iota_convert_fusion.2, f32[512]{0:T(512)S(1)} %bitcast.71, f32[8,128,512]{2,1,0:T(8,128)} %get-tuple-element.351), kind=kOutput, calls=%fused_computation.28.clone.1 | convolution fusion | flops 7051018240 | bytes 4888576 | tf_op jit(solution)/shard_map/while/body/eval_jaxpr/dot_general | solution.py:28
  73.5 16.8 %fusion.43 = bf16[8,128,8960]{1,2,0:T(8,128)(2,1)} fusion(bf16[8,128,8960]{1,2,0:T(8,128)(2,1)} %get-tuple-element.345, s32[]{:T(128)} %get-tuple-element.344, f32[8960]{0:T(1024)S(1)} %iota_convert_fusion.2, f32[512]{0:T(512)S(1)} %bitcast.71, f32[8,128,512]{2,1,0:T(8,128)} %get-tuple-element.351), kind=kOutput, calls=%fused_computation.28.clone.1 | convolution fusion | flops 7051018240 | bytes 4888576 | tf_op jit(solution)/shard_map/while/body/eval_jaxpr/dot_general | solution.py:28
  90.4 16.9 %fusion.43 = bf16[8,128,8960]{1,2,0:T(8,128)(2,1)} fusion(bf16[8,128,8960]{1,2,0:T(8,128)(2,1)} %get-tuple-element.345, s32[]{:T(128)} %get-tuple-element.344, f32[8960]{0:T(1024)S(1)} %iota_convert_fusion.2, f32[512]{0:T(512)S(1)} %bitcast.71, f32[8,128,512]{2,1,0:T(8,128)} %get-tuple-element.351), kind=kOutput, calls=%fused_computation.28.clone.1 | convolution fusion | flops 7051018240 | bytes 4888576 | tf_op jit(solution)/shard_map/while/body/eval_jaxpr/dot_general | solution.py:28
  107.2 16.9 %fusion.43 = bf16[8,128,8960]{1,2,0:T(8,128)(2,1)} fusion(bf16[8,128,8960]{1,2,0:T(8,128)(2,1)} %get-tuple-element.345, s32[]{:T(128)} %get-tuple-element.344, f32[8960]{0:T(1024)S(1)} %iota_convert_fusion.2, f32[512]{0:T(512)S(1)} %bitcast.71, f32[8,128,512]{2,1,0:T(8,128)} %get-tuple-element.351), kind=kOutput, calls=%fused_computation.28.clone.1 | convolution fusion | flops 7051018240 | bytes 4888576 | tf_op jit(solution)/shard_map/while/body/eval_jaxpr/dot_general | solution.py:28
  124.1 16.8 %fusion.43 = bf16[8,128,8960]{1,2,0:T(8,128)(2,1)} fusion(bf16[8,128,8960]{1,2,0:T(8,128)(2,1)} %get-tuple-element.345, s32[]{:T(128)} %get-tuple-element.344, f32[8960]{0:T(1024)S(1)} %iota_convert_fusion.2, f32[512]{0:T(512)S(1)} %bitcast.71, f32[8,128,512]{2,1,0:T(8,128)} %get-tuple-element.351), kind=kOutput, calls=%fused_computation.28.clone.1 | convolution fusion | flops 7051018240 | bytes 4888576 | tf_op jit(solution)/shard_map/while/body/eval_jaxpr/dot_general | solution.py:28
  141.0 16.9 %fusion.43 = bf16[8,128,8960]{1,2,0:T(8,128)(2,1)} fusion(bf16[8,128,8960]{1,2,0:T(8,128)(2,1)} %get-tuple-element.345, s32[]{:T(128)} %get-tuple-element.344, f32[8960]{0:T(1024)S(1)} %iota_convert_fusion.2, f32[512]{0:T(512)S(1)} %bitcast.71, f32[8,128,512]{2,1,0:T(8,128)} %get-tuple-element.351), kind=kOutput, calls=%fused_computation.28.clone.1 | convolution fusion | flops 7051018240 | bytes 4888576 | tf_op jit(solution)/shard_map/while/body/eval_jaxpr/dot_general | solution.py:28
  157.9 16.8 %fusion.43 = bf16[8,128,8960]{1,2,0:T(8,128)(2,1)} fusion(bf16[8,128,8960]{1,2,0:T(8,128)(2,1)} %get-tuple-element.345, s32[]{:T(128)} %get-tuple-element.344, f32[8960]{0:T(1024)S(1)} %iota_convert_fusion.2, f32[512]{0:T(512)S(1)} %bitcast.71, f32[8,128,512]{2,1,0:T(8,128)} %get-tuple-element.351), kind=kOutput, calls=%fused_computation.28.clone.1 | convolution fusion | flops 7051018240 | bytes 4888576 | tf_op jit(solution)/shard_map/while/body/eval_jaxpr/dot_general | solution.py:28
  174.7 16.8 %fusion.43 = bf16[8,128,8960]{1,2,0:T(8,128)(2,1)} fusion(bf16[8,128,8960]{1,2,0:T(8,128)(2,1)} %get-tuple-element.345, s32[]{:T(128)} %get-tuple-element.344, f32[8960]{0:T(1024)S(1)} %iota_convert_fusion.2, f32[512]{0:T(512)S(1)} %bitcast.71, f32[8,128,512]{2,1,0:T(8,128)} %get-tuple-element.351), kind=kOutput, calls=%fused_computation.28.clone.1 | convolution fusion | flops 7051018240 | bytes 4888576 | tf_op jit(solution)/shard_map/while/body/eval_jaxpr/dot_general | solution.py:28
  191.6 308.6 %reduce-scatter.5.cloned.1.call-done = bf16[128,8960]{0,1:T(8,128)(2,1)} async-done(((bf16[128,71680]{0,1:T(8,128)(2,1)}), bf16[128,8960]{0,1:T(8,128)(2,1)}) %reduce-scatter.5.cloned.1.call-update) | async-done | bytes 2293776 | tf_op jit(solution)/shard_map/reduce_scatter | solution.py:35
  500.6 64.4 %all-gather.2.cloned.1.call-done = bf16[512,8960]{0,1:T(8,128)(2,1)} async-done(((bf16[128,8960]{0,1:T(8,128)(2,1)}), bf16[512,8960]{0,1:T(8,128)(2,1)}) %all-gather.2.cloned.1.call-update) | async-done | bytes 9175056 | tf_op jit(solution)/shard_map/all_gather | solution.py:38
  565.0 12.7 %copy.23 = bf16[512,14,640]{2,0,1:T(8,128)(2,1)} copy(bf16[512,14,640]{0,2,1:T(8,128)(2,1)} %bitcast.69) | data formatting | bytes 18350080 | tf_op jit(solution)/shard_map/while | solution.py:66
  577.7 270.1 %while.21 = (s32[]{:T(128)}, bf16[22,512,512]{1,2,0:T(8,128)(2,1)}, s32[22]{0:T(128)S(1)}, s32[22,3]{1,0:T(8,128)S(1)}, bf16[512,14,640]{2,0,1:T(8,128)(2,1)}, /...) while((s32[]{:T(128)}, bf16[22,512,512]{1,2,0:T(8,128)(2,1)}, ...), condition=%wide.region_11.12_spmd, body=%wide.region_4.11_spmd.sunk | while | flops 1007157248 | bytes 15729669 | solution.py:66
  581.3 3.4 conditional.6
  585.4 3.6 conditional.7
  587.3 1.7 convolution_add_fusion.1
  589.6 4.2 conditional.8
  598.5 3.4 conditional.6
  607.9 3.4 conditional.6
  629.5 3.4 conditional.6
  633.5 3.6 conditional.7
  642.5 3.4 conditional.6
  646.5 3.6 conditional.7
  655.4 3.4 conditional.6
  659.5 3.6 conditional.7
  663.7 4.2 conditional.8
  672.6 3.4 conditional.6
  676.7 3.6 conditional.7
  685.6 3.4 conditional.6
  689.7 3.6 conditional.7
  710.8 3.4 conditional.6
  714.9 3.6 conditional.7
  719.2 4.2 conditional.8
  734.2 3.4 conditional.6
  743.5 3.4 conditional.6
  747.6 3.6 conditional.7
  751.8 4.2 conditional.8
  760.8 3.4 conditional.6
  764.8 3.6 conditional.7
  773.8 3.4 conditional.6
  777.8 3.6 conditional.7
  782.1 4.2 conditional.8
  791.0 3.4 conditional.6
  795.1 3.6 conditional.7
  799.4 4.2 conditional.8
  808.2 3.4 conditional.6
  812.3 3.6 conditional.7
  821.2 3.4 conditional.6
  825.2 3.6 conditional.7
  829.5 4.2 conditional.8
  838.4 3.4 conditional.6
  842.5 3.6 conditional.7
  847.8 15.0 %copy.26 = bf16[512,11264]{1,0:T(8,128)(2,1)} copy(bf16[512,11264]{0,1:T(8,128)(2,1)} %bitcast.68) | data formatting | bytes 23068672
  862.8 212.3 %reduce-scatter.7.cloned.1.call-done = bf16[64,11264]{1,0:T(8,128)(2,1)} async-done(((bf16[512,11264]{1,0:T(8,128)(2,1)}), bf16[64,11264]{1,0:T(8,128)(2,1)}) %reduce-scatter.7.cloned.1.call-update) | async-done | bytes 1441808
  1075.2 3.3 copy.27
  1078.5 7.6 abs_reduce_fusion
  1086.1 5.8 copy.25
  1091.9 36.1 %pmax.7 = f32[11264]{0:T(1024)} all-reduce(f32[11264]{0:T(1024)S(1)} %get-tuple-element.263), channel_id=1, replica_groups=mesh['line'=4,'bus'=8] {'bus'}, use_global_device_ids=true, to_apply=%region_14.15 | all-reduce | flops 11264 | bytes 90112 | tf_op jit(solution)/shard_map/pmax | solution.py:77
  (247 shorter events, 157.6 us)
Async XLA Ops:
  7.2 493.0 %reduce-scatter.5.cloned.1.call-start = ((), (), s32[]{:S(2)}) async-start(), calls=%async_computation.2 | async-start | bytes 20643840 | tf_op jit(solution)/shard_map/reduce_scatter | solution.py:35
  191.6 308.9 %copy-start.1 = (s32[22,3]{0,1:T(4,128)S(1)}, s32[22,3]{0,1:T(4,128)}, u32[]{:S(2)}) copy-start(s32[22,3]{0,1:T(4,128)} %param.19) | copy-start | bytes 796
  191.6 373.4 %all-gather.2.cloned.1.call-start = ((), (), s32[]{:S(2)}) async-start(), calls=%async_computation.3 | async-start | bytes 11468800 | tf_op jit(solution)/shard_map/all_gather | solution.py:38
  500.2 575.0 %reduce-scatter.7.cloned.1.call-start = ((), (), s32[]{:S(2)}) async-start(), calls=%async_computation.4 | async-start | bytes 12976128
  565.0 12.7 %copy-start.2 = (s32[22,1]{0,1:T(1,128)S(1)}, s32[22,1]{0,1:T(1,128)}, u32[]{:S(2)}) copy-start(s32[22,1]{0,1:T(1,128)} %param.18) | copy-start | bytes 268
  862.8 215.7 %copy-start = (f32[11264]{0:T(1024)S(1)}, f32[11264]{0:T(1024)}, u32[]{:S(2)}) copy-start(f32[11264]{0:T(1024)} %param.21) | copy-start | bytes 135172
Sparse Core Ops, SparseCore 0:
  191.7 308.4 reduce-scatter.4
  501.8 63.1 all-gather.1
  863.0 212.1 reduce-scatter.6
where the time goes:
time: 1140 us; the launch traced here: 1130 us
  waiting for transfers between devices  585 us (51%)
  matrix products  200 us (18%)
  local copies, waits for them, and re-layouts  170 us (15%)
  loops' own time  113 us (10%)
  blocking collectives  36.1 us (3%)
  other arithmetic  15.9 us (1%)
  between operations  13.9 us (1%)
    reduce_scatter x1, waiting for transfers between devices, body(): lax.psum_scatter(every_bus.astype(jnp.bfloat16), 'bus', scatter_dimension...  309 us
    unnamed x4, waiting for transfers between devices  212 us
    dot_general x8, matrix products, one_group(): jnp.dot(vals, table, precision=lax.Precision.HIGHEST, preferred_element_t...  135 us
    another operation x66, loops' own time, one_zone(): lax.cond(slot < live_count, lambda acc: acc + lax.dot_general(piece, bloc...  69 us
    dot_general x38, matrix products, one_zone(): lax.dot_general(piece, block, (((1,), (1,)), ((), ())), preferred_element...  64.8 us
    all_gather x1, waiting for transfers between devices, body(): injection = lax.all_gather(partial_value, 'line', axis=0, tiled=True)  64.4 us
    dynamic_slice x66, local copies, waits for them, and re-layouts, body(): lax.scan(one_zone, jnp.float32(0.0), (count_col, block_zone, ptdf_blocks))  50.8 us
    another operation x1, loops' own time, body(): lax.scan(one_zone, jnp.float32(0.0), (count_col, block_zone, ptdf_blocks))  43.9 us
  transfers between devices with their start and end apart: 3, of which 3 were waited for; matrix products, arithmetic and copies ran while one was open for 0% of the time, Pallas kernels for 0%

commit v1 on v0

v1 whole, which is shorter than its diff:
```python
import functools

import jax
import jax.numpy as jnp
from jax import lax
from jax.experimental import pallas as pl
from jax.experimental.pallas import tpu as pltpu
from jax.sharding import PartitionSpec as P

NB = 71680
TILE = 256
VMEM = 48 * 1024 * 1024
F32 = jnp.float32
BF16 = jnp.bfloat16


def params(n):
    return pltpu.CompilerParams(dimension_semantics=("arbitrary",) * n, vmem_limit_bytes=VMEM)


def cost(flops, nbytes):
    return pl.CostEstimate(flops=int(flops), bytes_accessed=int(nbytes), transcendentals=0)


def hot(ids, first, rows):
    at = lax.broadcasted_iota(jnp.int32, (rows, ids.shape[1]), 0) + first
    return (at == ids).astype(F32).astype(BF16)


def route_kernel(order_ref, values_ref, out_ref, rounded):
    @pl.when(pl.program_id(0) == 0)
    def _():
        rounded[...] = values_ref[...].astype(BF16)

    depth = values_ref.shape[1]
    step = 512
    ids = order_ref[0]
    total = jnp.zeros(out_ref.shape[1:], F32)
    for at in range(0, depth, step):
        total += jnp.dot(
            rounded[:, at : at + step], hot(ids, at, step), preferred_element_type=F32
        )
    out_ref[0] = total.astype(BF16)


def route(order, values):
    groups, _, width = order.shape
    rows, depth = values.shape
    return pl.pallas_call(
        route_kernel,
        grid=(groups,),
        in_specs=[
            pl.BlockSpec((1, 1, width), lambda g: (g, 0, 0)),
            pl.BlockSpec((rows, depth), lambda g: (0, 0)),
        ],
        out_specs=pl.BlockSpec((1, rows, width), lambda g: (g, 0, 0)),
        out_shape=jax.ShapeDtypeStruct((groups, rows, width), BF16),
        scratch_shapes=[pltpu.VMEM((rows, depth), BF16)],
        compiler_params=params(1),
        cost_estimate=cost(4 * rows * depth * groups * width, 4 * rows * depth),
        name="route",
    )(order, values)


def merge_kernel(order_ref, runs_ref, out_ref):
    runs, rows, width = runs_ref.shape
    ids = order_ref[0]
    total = jnp.zeros((rows, ids.shape[1]), F32)
    for run in range(runs):
        total += jnp.dot(runs_ref[run], hot(ids, run * width, width), preferred_element_type=F32)
    total = total.astype(BF16)
    for part in range(out_ref.shape[0]):
        out_ref[part] = total[:, part * TILE : (part + 1) * TILE]


def merge(order, runs):
    count, rows, width = runs.shape
    sites = count * width
    step = 2 * TILE
    return pl.pallas_call(
        merge_kernel,
        grid=(sites // step,),
        in_specs=[
            pl.BlockSpec((1, 1, step), lambda t: (t, 0, 0)),
            pl.BlockSpec((count, rows, width), lambda t: (0, 0, 0)),
        ],
        out_specs=pl.BlockSpec((step // TILE, rows, TILE), lambda t: (t, 0, 0)),
        out_shape=jax.ShapeDtypeStruct((sites // TILE, rows, TILE), BF16),
        compiler_params=params(1),
        cost_estimate=cost(4 * rows * sites * sites, 4 * rows * sites),
        name="merge",
    )(order.reshape(sites // step, 1, step), runs)


def inject_kernel(first_ref, last_ref, rows_ref, ids_ref, *refs):
    pieces, out_ref, total = refs[:-2], refs[-2], refs[-1]
    zone = pl.program_id(0)
    scen, width = total.shape
    total[...] = jnp.zeros_like(total)

    @pl.loop(first_ref[zone], last_ref[zone])
    def _(t):
        at = lax.broadcasted_iota(jnp.int32, (width, TILE), 0) + zone * width
        table = (at == ids_ref[t]).astype(F32).astype(BF16)
        part = jnp.concatenate([piece[t] for piece in pieces], axis=0)
        total[...] += lax.dot_general(
            part, table, (((1,), (1,)), ((), ())), preferred_element_type=F32
        )

    blocks = rows_ref.shape[0]
    high = scen // blocks
    for j in range(blocks):
        rows = pl.ds(pl.multiple_of(rows_ref[j] * high, high), high)
        out_ref[0, j * high : (j + 1) * high] = total[rows, :].astype(BF16)


def inject(first, last, row_blocks, ids, pieces, zones, width):
    tiles, rows, _ = pieces[0].shape
    scen = rows * len(pieces)
    whole = pl.BlockSpec((tiles, rows, TILE), lambda z, *_: (0, 0, 0))
    return pl.pallas_call(
        inject_kernel,
        grid_spec=pltpu.PrefetchScalarGridSpec(
            num_scalar_prefetch=3,
            grid=(zones,),
            in_specs=[pl.BlockSpec((tiles, 1, TILE), lambda z, *_: (0, 0, 0))]
            + [whole] * len(pieces),
            out_specs=pl.BlockSpec((1, scen, width), lambda z, *_: (z, 0, 0)),
            scratch_shapes=[pltpu.VMEM((scen, width), F32)],
        ),
        out_shape=jax.ShapeDtypeStruct((zones, scen, width), BF16),
        compiler_params=params(1),
        cost_estimate=cost(4 * scen * width * TILE * (tiles + zones), 2 * zones * scen * width),
        name="inject",
    )(first, last, row_blocks, ids, *pieces)


def flow_kernel(count_ref, zone_ref, inj_ref, block_ref, *refs, base):
    outs, total = refs[:-1], refs[-1]
    z, k = pl.program_id(0), pl.program_id(1)
    live = k < count_ref[z + base]

    @pl.when(k == 0)
    def _():
        total[...] = jnp.zeros_like(total)

    @pl.when(live)
    def _():
        total[...] += lax.dot_general(
            inj_ref[0], block_ref[0, 0], (((1,), (1,)), ((), ())), preferred_element_type=F32
        )

    @pl.when(k == pl.num_programs(1) - 1)
    def _():
        row = 0
        for out in outs:
            out[...] = total[row : row + out.shape[0], :].astype(BF16)
            row += out.shape[0]


def partial_flow(count, zone, inj, blocks, base, zones, splits):
    _, slots, lines, width = blocks.shape
    scen = inj.shape[1]

    def slot(z, k, count):
        return jnp.minimum(k, jnp.maximum(count[z + base] - 1, 0))

    return pl.pallas_call(
        functools.partial(flow_kernel, base=base),
        grid_spec=pltpu.PrefetchScalarGridSpec(
            num_scalar_prefetch=2,
            grid=(zones, slots),
            in_specs=[
                pl.BlockSpec(
                    (1, scen, width),
                    lambda z, k, count, zone: (
                        zone[(z + base) * slots + slot(z, k, count)],
                        0,
                        0,
                    ),
                ),
                pl.BlockSpec(
                    (1, 1, lines, width),
                    lambda z, k, count, zone: (z + base, slot(z, k, count), 0, 0),
                ),
            ],
            out_specs=[pl.BlockSpec((rows, lines), lambda z, k, *_: (0, z)) for rows in splits],
            scratch_shapes=[pltpu.VMEM((scen, lines), F32)],
        ),
        out_shape=[jax.ShapeDtypeStruct((rows, zones * lines), BF16) for rows in splits],
        compiler_params=params(2),
        cost_estimate=cost(
            zones * slots * scen * lines * width, zones * slots * (scen + lines) * width
        ),
        name="partial_flow",
    )(count, zone.reshape(-1), inj, blocks)


def chunks_of(zones):
    sizes = []
    for size in (1, 2):
        if zones - sum(sizes) > size:
            sizes.insert(0, size)
    left = zones - sum(sizes)
    while left > 0:
        sizes.insert(0, min(4, left))
        left -= sizes[0]
    return sizes


def add(*terms):
    return sum(term.astype(F32) for term in terms)


def body(site_values, site_bus, block_count, block_zone, ptdf_blocks, rating):
    here = lax.axis_index("bus")
    groups = lax.axis_size("bus")
    lines_size = lax.axis_size("line")
    scen_part, site_dev = site_values.shape
    bus_dev = NB // groups
    per_group = site_dev // groups
    group_sites = groups * per_group
    zones_dev, slots_dev, line_zone, zone_width = ptdf_blocks.shape
    bus_zones = bus_dev // zone_width
    scen = scen_part * lines_size
    high = scen // groups

    own_ids = lax.dynamic_slice_in_dim(site_bus, here * site_dev, site_dev)
    keys = lax.sort(own_ids * site_dev + jnp.arange(site_dev, dtype=jnp.int32))
    order = (keys % site_dev).reshape(groups, 1, per_group)
    sorted_bus = (keys // site_dev).reshape(groups, per_group)
    got_bus = lax.all_to_all(sorted_bus, "bus", 0, 0, tiled=True)
    got = lax.all_to_all(route(order, site_values), "bus", 0, 0, tiled=True)

    local = (got_bus - here * bus_dev).reshape(group_sites)
    keys = lax.sort(local * group_sites + jnp.arange(group_sites, dtype=jnp.int32))
    local = keys // group_sites
    sites = merge(keys % group_sites, got)
    edges = jnp.arange(bus_zones + 1, dtype=jnp.int32) * zone_width
    starts = jnp.sum((local[None, :] < edges[:, None]).astype(jnp.int32), axis=1)
    first = starts[:-1] // TILE
    last = (starts[1:] + TILE - 1) // TILE
    ids = local.reshape(group_sites // TILE, 1, TILE)

    tuned = groups == 8 and lines_size == 4 and scen_part == 2 * high
    if tuned:
        me = lax.axis_index("line")
        by_core = [(i, i ^ 1) for i in range(lines_size)]
        by_y = [(i, i ^ 2) for i in range(lines_size)]
        across = lax.ppermute(sites, "line", by_y)
        pieces = [
            sites,
            lax.ppermute(sites, "line", by_core),
            across,
            lax.ppermute(across, "line", by_core),
        ]
        x, z = here % 2, here // 2
        slots = jnp.arange(4, dtype=jnp.int32)
        z_dest = jnp.where(z < 2, slots, 3 - slots)
        piece_at = (z_dest ^ me) * 2
        row_blocks = jnp.concatenate([piece_at + (1 - x), piece_at + x])
        splits = (scen // 2, scen // 2)
    else:
        gathered = lax.all_gather(sites, "line", axis=0)
        pieces = [gathered[i] for i in range(lines_size)]
        row_blocks = jnp.arange(groups, dtype=jnp.int32)
        splits = (scen,)

    inj = inject(first, last, row_blocks.astype(jnp.int32), ids, pieces, bus_zones, zone_width)
    count = block_count[:, 0]

    if tuned:
        swap_x = [(i, i ^ 1) for i in range(8)]
        inward = [(0, 2), (1, 3), (6, 4), (7, 5)]
        middle = [(2, 4), (3, 5), (4, 2), (5, 3)]
        outward = [(2, 0), (3, 1), (4, 6), (5, 7)]
        inner = (z == 1) | (z == 2)
        flows = []
        base = 0
        for zones in chunks_of(zones_dev):
            send, keep = partial_flow(
                count, block_zone, inj, ptdf_blocks, base, zones, splits
            )
            base += zones
            summed = add(keep, lax.ppermute(send, "bus", swap_x)).astype(BF16)
            own0, own1, own23 = summed[:high], summed[high : 2 * high], summed[2 * high :]
            from1 = lax.ppermute(own1, "bus", inward)
            from23 = lax.ppermute(own23, "bus", inward)
            mid = lax.ppermute(add(own23, from23).astype(BF16), "bus", middle)
            end = lax.ppermute(add(own0, mid[high:]).astype(BF16), "bus", outward)
            flows.append(
                jnp.where(inner, add(own1, from1, mid[:high]), add(own0, end))
            )
        flow = jnp.concatenate(flows, axis=1)
    else:
        (whole,) = partial_flow(
            count, block_zone, inj, ptdf_blocks, 0, zones_dev, splits
        )
        flow = lax.psum_scatter(whole, "bus", scatter_dimension=0, tiled=True).astype(F32)

    loading = flow / rating[None, :]
    worst = jnp.max(jnp.abs(loading), axis=0)
    if groups & (groups - 1) == 0:
        step = 1
        while step < groups:
            pairs = [(i, i ^ step) for i in range(groups)]
            worst = jnp.maximum(worst, lax.ppermute(worst, "bus", pairs))
            step *= 2
    else:
        worst = lax.pmax(worst, "bus")
    return loading, worst


def solution(mesh):
    return jax.shard_map(
        body,
        mesh=mesh,
        in_specs=(
            P("line", "bus"),
            P(),
            P("line", "bus"),
            P("line", "bus"),
            P("line", "bus", None, None),
            P("line"),
        ),
        out_specs=(P("bus", "line"), P("line")),
        check_vma=False,
    )
```

time: 1140 us -> 427 us (0.37)
  waiting for transfers between devices: 585 us -> 189 us
  matrix products: 200 us -> 0 us
  local copies, waits for them, and re-layouts: 170 us -> 2.13 us
  starting transfers between devices: 0.3 us -> 131 us
  loops' own time: 113 us -> 0 us
  Pallas kernels: 0 us -> 83.8 us
  blocking collectives: 36.1 us -> 0 us
  between operations: 13.9 us -> 1.45 us
    reduce_scatter x1 -> x0, waiting for transfers between devices: 309 us -> none  [body(): lax.psum_scatter(every_bus.astype(jnp.bfloat16), 'bus', scatter_dimension...]
    unnamed x4 -> x0, waiting for transfers between devices: 212 us -> none
    dot_general x46 -> x0, matrix products: 200 us -> none  [the longest x8 135 us: one_group(): jnp.dot(vals, table, precision=lax.Precision.HIGHEST, preferred_element_t...]
    ppermute x0 -> x41, waiting for transfers between devices: none -> 169 us  [the longest x7 69.3 us: body(): summed = add(keep, lax.ppermute(send, 'bus', swap_x)).astype(BF16)]
    ppermute x0 -> x41, starting transfers between devices: none -> 118 us  [the longest x7 51.3 us: body(): from1 = lax.ppermute(own1, 'bus', inward)]
    another operation x68 -> x0, loops' own time: 113 us -> none  [the longest x66 69 us: one_zone(): lax.cond(slot < live_count, lambda acc: acc + lax.dot_general(piece, bloc...]
    pallas_call x0 -> x10, Pallas kernels: none -> 83.8 us  [the longest x7 54.1 us: partial_flow(): pl.pallas_call(functools.partial(flow_kernel, base=base), grid_spec=pltpu...]
    all_gather x1 -> x0, waiting for transfers between devices: 64.4 us -> none  [body(): injection = lax.all_gather(partial_value, 'line', axis=0, tiled=True)]
  transfers between devices with their start and end apart: 3 -> 43, of which waited for: 3 -> 25; matrix products, arithmetic and copies ran while one was open for 0% -> 3% of each run, Pallas kernels for 0% -> 7%
where the time goes in v1:
time: 427 us
  waiting for transfers between devices  189 us (44%)
  starting transfers between devices  131 us (31%)
  Pallas kernels  83.8 us (20%)
  other arithmetic  19.8 us (5%)
    ppermute x7, waiting for transfers between devices, body(): summed = add(keep, lax.ppermute(send, 'bus', swap_x)).astype(BF16)  69.3 us
    pallas_call x7, Pallas kernels, partial_flow(): pl.pallas_call(functools.partial(flow_kernel, base=base), grid_spec=pltpu...  54.1 us
    ppermute x7, starting transfers between devices, body(): from1 = lax.ppermute(own1, 'bus', inward)  51.3 us
    ppermute x7, starting transfers between devices, body(): from23 = lax.ppermute(own23, 'bus', inward)  36 us
    ppermute x7, waiting for transfers between devices, body(): from23 = lax.ppermute(own23, 'bus', inward)  35.3 us
    ppermute x7, waiting for transfers between devices, body(): end = lax.ppermute(add(own0, mid[high:]).astype(BF16), 'bus', outward)  23.2 us
    ppermute x1, waiting for transfers between devices, body(): across = lax.ppermute(sites, 'line', by_y)  21.6 us
    all_to_all x1, waiting for transfers between devices, body(): got = lax.all_to_all(route(order, site_values), 'bus', 0, 0, tiled=True)  19.6 us
  transfers between devices with their start and end apart: 43, of which 25 were waited for; matrix products, arithmetic and copies ran while one was open for 3% of the time, Pallas kernels for 7%

profile of v1, /device:TPU:0, one launch (start us, length us, event | category | flops | bytes accessed | tf_op | source)
XLA Modules:
  0.0 426.8 jit_solution(4579467409819593141)
XLA Ops:
  1.4 5.8 %sort.28 = (s32[4096]{0:T(1024)S(1)}, s32[4096]{0:T(1024)}) sort(s32[4096]{0:T(1024)S(1)} %iota_add_fusion.1, s32[4096]{0:T(1024)S(1)} %iota.23), dimensions={0}, to_apply=%region_0.0 | sort | flops 49152 | bytes 65536 | tf_op jit(solution)/shard_map/sort | solution.py:229
  7.8 7.3 %all-to-all-start = ((s32[8,1,512]{2,1,0:T(1,128)}), s32[8,1,512]{2,1,0:T(1,128)S(1)}, u32[]{:S(2)}, u32[]{:S(2)}) async-start(s32[8,1,512]{2,1,0:T(1,128)} %bitcast.1), calls=%async_computation | async-start | bytes 32768 | tf_op jit(solution)/shard_map/all_to_all | solution.py:232
  15.0 1.6 copy-done.1
  16.6 6.6 %route.1 = bf16[8,128,512]{2,1,0:T(8,128)(2,1)} custom-call(s32[8,1,512]{2,1,0:T(1,128)S(1)} %bitcast.15, f32[128,4096]{1,0:T(8,128)S(1)} %copy-done.1), custom_call_target="tpu_custom_call" | custom-call | flops 8589934592 | bytes 2097152 | tf_op jit(solution)/shard_map/route/pallas_call | solution.py:49
  23.2 6.0 %all-to-all-start.1 = ((bf16[8,128,512]{2,1,0:T(8,128)(2,1)}), bf16[8,128,512]{2,1,0:T(8,128)(2,1)S(1)}, u32[]{:S(2)}, u32[]{:S(2)}) async-start(bf16[8,128,512]{2,1,0:T(8,128)(2,1)} %route.1), calls=%async_computation.1 | async-start | bytes 2097152 | tf_op jit(solution)/shard_map/all_to_all | solution.py:233
  29.3 5.8 %sort.29 = (s32[4096]{0:T(1024)S(1)}, s32[4096]{0:T(1024)}) sort(s32[4096]{0:T(1024)S(1)} %iota_add_fusion, s32[4096]{0:T(1024)S(1)} %iota.25), dimensions={0}, to_apply=%region_1.2 | sort | flops 49152 | bytes 65536 | tf_op jit(solution)/shard_map/sort | solution.py:236
  35.1 19.6 %all-to-all-done.1.runs_ref = bf16[8,128,512]{2,1,0:T(8,128)(2,1)S(1)} async-done(((bf16[8,128,512]{2,1,0:T(8,128)(2,1)}), bf16[8,128,512]{2,1,0:T(8,128)(2,1)S(1)}, u32[]{:S(2)}, u32[]{:S(2)}) %all-to-all-start.1) | async-done | bytes 1048608 | tf_op jit(solution)/shard_map/all_to_all | solution.py:233
  54.7 5.8 %merge.1.refs_0_ = bf16[16,128,256]{2,1,0:T(8,128)(2,1)S(1)} custom-call(s32[8,1,512]{2,1,0:T(1,128)S(1)} %bitcast.14, bf16[8,128,512]{2,1,0:T(8,128)(2,1)S(1)} %all-to-all-done.1.runs_ref), custom_call_target="tpu_custom_call" | custom-call | flops 8589934592 | bytes 2097152 | tf_op jit(solution)/shard_map/merge/pallas_call | solution.py:80
  60.5 1.6 collective-permute-start.1
  62.1 21.6 %collective-permute-done.1.refs_2_ = bf16[16,128,256]{2,1,0:T(8,128)(2,1)S(1)} collective-permute-done((bf16[16,128,256]{2,1,0:T(8,128)(2,1)S(1)}, bf16[16,128,256]{2,1,0:T(8,128)(2,1)S(1)}, u32[]{:S(2)}, u32[]{:S(2)}) %collective-permute-start.1) | collective-permute-done | bytes 1048608 | tf_op jit(solution)/shard_map/ppermute | solution.py:250
  84.3 2.2 collective-permute-done.2.refs_3_
  86.4 17.2 %inject.1.inj_ref = bf16[14,512,640]{2,1,0:T(8,128)(2,1)} custom-call(s32[14]{0:T(128)S(1)} %get-tuple-element.43.first_ref, s32[14]{0:T(128)S(1)} %get-tuple-element.42.last_ref, s32[8]{0:T(128)S(1)} %pad_add_fusion.rows_ref, s32[16,1,256]{2,1,0:T(1,128)S(1)} %bitcast.6, bf16[16,128,256]{2,1,0:T(8,128)(2,1)S(1)} %merge.1.refs_0_, ...), custom_call_target="tpu_custom_call" | custom-call | flops 10066329600 | bytes 9175040 | tf_op jit(solution)/shard_map/inject/pallas_call | solution.py:121
  103.7 7.5 %partial_flow.7 = (bf16[256,1536]{1,0:T(8,128)(2,1)S(1)}, bf16[256,1536]{1,0:T(8,128)(2,1)S(1)}) custom-call(s32[22]{0:T(128)S(1)} %bitcast.7, s32[66]{0:T(128)S(1)} %reshape.38.zone_ref, bf16[14,512,640]{2,1,0:T(8,128)(2,1)} %inject.1.inj_ref, bf16[22,3,512,640]{3,2,1,0:T(8,128)(2,1)} %block_ref.13), custom_call_target="tpu_custom_call" | custom-call | flops 1509949440 | bytes 5898240 | tf_op jit(solution)/shard_map/partial_flow/pallas_call | solution.py:168
  111.2 9.2 %partial_flow.8 = (bf16[256,2048]{1,0:T(8,128)(2,1)S(1)}, bf16[256,2048]{1,0:T(8,128)(2,1)S(1)}) custom-call(s32[22]{0:T(128)S(1)} %bitcast.8, s32[66]{0:T(128)S(1)} %reshape.38.zone_ref, bf16[14,512,640]{2,1,0:T(8,128)(2,1)} %inject.1.inj_ref, bf16[22,3,512,640]{3,2,1,0:T(8,128)(2,1)} %block_ref.13), custom_call_target="tpu_custom_call" | custom-call | flops 2013265920 | bytes 7864320 | tf_op jit(solution)/shard_map/partial_flow/pallas_call | solution.py:168
  120.3 10.1 %partial_flow.9 = (bf16[256,2048]{1,0:T(8,128)(2,1)S(1)}, bf16[256,2048]{1,0:T(8,128)(2,1)S(1)}) custom-call(s32[22]{0:T(128)S(1)} %bitcast.9, s32[66]{0:T(128)S(1)} %reshape.38.zone_ref, bf16[14,512,640]{2,1,0:T(8,128)(2,1)} %inject.1.inj_ref, bf16[22,3,512,640]{3,2,1,0:T(8,128)(2,1)} %block_ref.13), custom_call_target="tpu_custom_call" | custom-call | flops 2013265920 | bytes 7864320 | tf_op jit(solution)/shard_map/partial_flow/pallas_call | solution.py:168
  130.5 2.7 partial_flow.13
  133.2 2.9 collective-permute-start.3
  136.1 5.0 %partial_flow.12 = (bf16[256,1024]{1,0:T(8,128)(2,1)S(1)}, bf16[256,1024]{1,0:T(8,128)(2,1)S(1)}) custom-call(s32[22]{0:T(128)S(1)} %bitcast.11, s32[66]{0:T(128)S(1)} %reshape.38.zone_ref, bf16[14,512,640]{2,1,0:T(8,128)(2,1)} %inject.1.inj_ref, bf16[22,3,512,640]{3,2,1,0:T(8,128)(2,1)} %block_ref.13), custom_call_target="tpu_custom_call" | custom-call | flops 1006632960 | bytes 3932160 | tf_op jit(solution)/shard_map/partial_flow/pallas_call | solution.py:168
  141.1 3.8 collective-permute-start.28
  144.9 8.6 %partial_flow.10 = (bf16[256,2048]{1,0:T(8,128)(2,1)S(1)}, bf16[256,2048]{1,0:T(8,128)(2,1)S(1)}) custom-call(s32[22]{0:T(128)S(1)} %bitcast.12, s32[66]{0:T(128)S(1)} %reshape.38.zone_ref, bf16[14,512,640]{2,1,0:T(8,128)(2,1)} %inject.1.inj_ref, bf16[22,3,512,640]{3,2,1,0:T(8,128)(2,1)} %block_ref.13), custom_call_target="tpu_custom_call" | custom-call | flops 2013265920 | bytes 7864320 | tf_op jit(solution)/shard_map/partial_flow/pallas_call | solution.py:168
  153.5 6.0 %collective-permute-done.33 = bf16[256,512]{1,0:T(8,128)(2,1)S(1)} collective-permute-done((bf16[256,512]{1,0:T(8,128)(2,1)S(1)}, bf16[256,512]{1,0:T(8,128)(2,1)S(1)}, u32[]{:S(2)}, u32[]{:S(2)}) %collective-permute-start.33) | collective-permute-done | bytes 262176 | tf_op jit(solution)/shard_map/ppermute | solution.py:285
  159.7 5.8 %collective-permute-start.35 = (bf16[128,512]{1,0:T(8,128)(2,1)S(1)}, bf16[128,512]{1,0:T(8,128)(2,1)S(1)}, u32[]{:S(2)}, u32[]{:S(2)}) collective-permute-start(bf16[128,512]{1,0:T(8,128)(2,1)S(1)} %slice.179), channel_id=1, source_target_pairs={{0,2},{1,3},{6,4},{7,5},{8,10},{9,11},{14,12},{15,13},{16,18},{17,... | collective-permute-start | bytes 393224 | tf_op jit(solution)/shard_map/ppermute | solution.py:288
  165.5 11.0 %partial_flow.11 = (bf16[256,2048]{1,0:T(8,128)(2,1)S(1)}, bf16[256,2048]{1,0:T(8,128)(2,1)S(1)}) custom-call(s32[22]{0:T(128)S(1)} %bitcast.13, s32[66]{0:T(128)S(1)} %reshape.38.zone_ref, bf16[14,512,640]{2,1,0:T(8,128)(2,1)} %inject.1.inj_ref, bf16[22,3,512,640]{3,2,1,0:T(8,128)(2,1)} %block_ref.13), custom_call_target="tpu_custom_call" | custom-call | flops 2013265920 | bytes 7864320 | tf_op jit(solution)/shard_map/partial_flow/pallas_call | solution.py:168
  176.6 2.0 collective-permute-start.13
  179.8 2.0 collective-permute-start.23
  181.8 7.8 %collective-permute-start.30 = (bf16[128,1024]{1,0:T(8,128)(2,1)S(1)}, bf16[128,1024]{1,0:T(8,128)(2,1)S(1)}, u32[]{:S(2)}, u32[]{:S(2)}) collective-permute-start(bf16[128,1024]{1,0:T(8,128)(2,1)S(1)} %slice.174), channel_id=1, source_target_pairs={{0,2},{1,3},{6,4},{7,5},{8,10},{9,11},{14,12},{15,13},{16,18},{17,... | collective-permute-start | bytes 786440 | tf_op jit(solution)/shard_map/ppermute | solution.py:288
  189.9 4.5 %collective-permute-done.30 = bf16[128,1024]{1,0:T(8,128)(2,1)S(1)} collective-permute-done((bf16[128,1024]{1,0:T(8,128)(2,1)S(1)}, bf16[128,1024]{1,0:T(8,128)(2,1)S(1)}, u32[]{:S(2)}, u32[]{:S(2)}) %collective-permute-start.30) | collective-permute-done | bytes 262176 | tf_op jit(solution)/shard_map/ppermute | solution.py:288
  194.4 4.4 %collective-permute-start.34 = (bf16[64,512]{1,0:T(8,128)(2,1)S(1)}, bf16[64,512]{1,0:T(8,128)(2,1)S(1)}, u32[]{:S(2)}, u32[]{:S(2)}) collective-permute-start(bf16[64,512]{1,0:T(8,128)(2,1)S(1)} %slice.178), channel_id=1, source_target_pairs={{0,2},{1,3},{6,4},{7,5},{8,10},{9,11},{14,12},{15,13},{16,18},{17,... | collective-permute-start | bytes 196616 | tf_op jit(solution)/shard_map/ppermute | solution.py:287
  198.9 3.9 collective-permute-done.8
  202.7 1.7 collective-permute-start.29
  204.8 20.4 %collective-permute-done.13 = bf16[256,2048]{1,0:T(8,128)(2,1)S(1)} collective-permute-done((bf16[256,2048]{1,0:T(8,128)(2,1)S(1)}, bf16[256,2048]{1,0:T(8,128)(2,1)S(1)}, u32[]{:S(2)}, u32[]{:S(2)}) %collective-permute-start.13) | collective-permute-done | bytes 1048608 | tf_op jit(solution)/shard_map/ppermute | solution.py:285
  225.2 1.7 collective-permute-start.5
  227.3 20.4 %collective-permute-done.18 = bf16[256,2048]{1,0:T(8,128)(2,1)S(1)} collective-permute-done((bf16[256,2048]{1,0:T(8,128)(2,1)S(1)}, bf16[256,2048]{1,0:T(8,128)(2,1)S(1)}, u32[]{:S(2)}, u32[]{:S(2)}) %collective-permute-start.18) | collective-permute-done | bytes 1048608 | tf_op jit(solution)/shard_map/ppermute | solution.py:285
  247.7 1.7 collective-permute-start.4
  249.8 18.7 %collective-permute-done.23 = bf16[256,2048]{1,0:T(8,128)(2,1)S(1)} collective-permute-done((bf16[256,2048]{1,0:T(8,128)(2,1)S(1)}, bf16[256,2048]{1,0:T(8,128)(2,1)S(1)}, u32[]{:S(2)}, u32[]{:S(2)}) %collective-permute-start.23) | collective-permute-done | bytes 1048608 | tf_op jit(solution)/shard_map/ppermute | solution.py:285
  269.6 10.5 %collective-permute-start.10 = (bf16[128,2048]{1,0:T(8,128)(2,1)S(1)}, bf16[128,2048]{1,0:T(8,128)(2,1)S(1)}, u32[]{:S(2)}, u32[]{:S(2)}) collective-permute-start(bf16[128,2048]{1,0:T(8,128)(2,1)S(1)} %slice.154), channel_id=1, source_target_pairs={{0,2},{1,3},{6,4},{7,5},{8,10},{9,11},{14,12},{15,13},{16,18},{17,... | collective-permute-start | bytes 1572872 | tf_op jit(solution)/shard_map/ppermute | solution.py:288
  280.4 1.3 collective-permute-start.15
  281.8 10.6 %collective-permute-done.10 = bf16[128,2048]{1,0:T(8,128)(2,1)S(1)} collective-permute-done((bf16[128,2048]{1,0:T(8,128)(2,1)S(1)}, bf16[128,2048]{1,0:T(8,128)(2,1)S(1)}, u32[]{:S(2)}, u32[]{:S(2)}) %collective-permute-start.10) | collective-permute-done | bytes 524320 | tf_op jit(solution)/shard_map/ppermute | solution.py:288
  292.4 4.4 %collective-permute-start.20 = (bf16[128,2048]{1,0:T(8,128)(2,1)S(1)}, bf16[128,2048]{1,0:T(8,128)(2,1)S(1)}, u32[]{:S(2)}, u32[]{:S(2)}) collective-permute-start(bf16[128,2048]{1,0:T(8,128)(2,1)S(1)} %slice.164), channel_id=1, source_target_pairs={{0,2},{1,3},{6,4},{7,5},{8,10},{9,11},{14,12},{15,13},{16,18},{17,... | collective-permute-start | bytes 1572872 | tf_op jit(solution)/shard_map/ppermute | solution.py:288
  297.0 6.7 %collective-permute-done.15 = bf16[128,2048]{1,0:T(8,128)(2,1)S(1)} collective-permute-done((bf16[128,2048]{1,0:T(8,128)(2,1)S(1)}, bf16[128,2048]{1,0:T(8,128)(2,1)S(1)}, u32[]{:S(2)}, u32[]{:S(2)}) %collective-permute-start.15) | collective-permute-done | bytes 524320 | tf_op jit(solution)/shard_map/ppermute | solution.py:288
  303.7 4.4 %collective-permute-start.25 = (bf16[128,2048]{1,0:T(8,128)(2,1)S(1)}, bf16[128,2048]{1,0:T(8,128)(2,1)S(1)}, u32[]{:S(2)}, u32[]{:S(2)}) collective-permute-start(bf16[128,2048]{1,0:T(8,128)(2,1)S(1)} %slice.169), channel_id=1, source_target_pairs={{0,2},{1,3},{6,4},{7,5},{8,10},{9,11},{14,12},{15,13},{16,18},{17,... | collective-permute-start | bytes 1572872 | tf_op jit(solution)/shard_map/ppermute | solution.py:288
  308.2 6.7 %collective-permute-done.20 = bf16[128,2048]{1,0:T(8,128)(2,1)S(1)} collective-permute-done((bf16[128,2048]{1,0:T(8,128)(2,1)S(1)}, bf16[128,2048]{1,0:T(8,128)(2,1)S(1)}, u32[]{:S(2)}, u32[]{:S(2)}) %collective-permute-start.20) | collective-permute-done | bytes 524320 | tf_op jit(solution)/shard_map/ppermute | solution.py:288
  316.5 6.8 %collective-permute-done.25 = bf16[128,2048]{1,0:T(8,128)(2,1)S(1)} collective-permute-done((bf16[128,2048]{1,0:T(8,128)(2,1)S(1)}, bf16[128,2048]{1,0:T(8,128)(2,1)S(1)}, u32[]{:S(2)}, u32[]{:S(2)}) %collective-permute-start.25) | collective-permute-done | bytes 524320 | tf_op jit(solution)/shard_map/ppermute | solution.py:288
  324.7 1.3 collective-permute-start.37
  326.0 9.5 %collective-permute-done.7 = bf16[64,1536]{1,0:T(8,128)(2,1)S(1)} collective-permute-done((bf16[64,1536]{1,0:T(8,128)(2,1)S(1)}, bf16[64,1536]{1,0:T(8,128)(2,1)S(1)}, u32[]{:S(2)}, u32[]{:S(2)}) %collective-permute-start.7) | collective-permute-done | bytes 196640 | tf_op jit(solution)/shard_map/ppermute | solution.py:290
  337.9 30.4 %collective-permute-start.9 = (bf16[64,2048]{1,0:T(8,128)(2,1)S(1)}, bf16[64,2048]{1,0:T(8,128)(2,1)S(1)}, u32[]{:S(2)}, u32[]{:S(2)}) collective-permute-start(bf16[64,2048]{1,0:T(8,128)(2,1)S(1)} %slice.153), channel_id=1, source_target_pairs={{0,2},{1,3},{6,4},{7,5},{8,10},{9,11},{14,12},{15,13},{16,18},{17,... | collective-permute-start | bytes 786440 | tf_op jit(solution)/shard_map/ppermute | solution.py:287
  368.4 1.3 collective-permute-start.12
  369.8 4.3 %collective-permute-done.9 = bf16[64,2048]{1,0:T(8,128)(2,1)S(1)} collective-permute-done((bf16[64,2048]{1,0:T(8,128)(2,1)S(1)}, bf16[64,2048]{1,0:T(8,128)(2,1)S(1)}, u32[]{:S(2)}, u32[]{:S(2)}) %collective-permute-start.9) | collective-permute-done | bytes 262176 | tf_op jit(solution)/shard_map/ppermute | solution.py:287
  374.1 4.4 %collective-permute-start.14 = (bf16[64,2048]{1,0:T(8,128)(2,1)S(1)}, bf16[64,2048]{1,0:T(8,128)(2,1)S(1)}, u32[]{:S(2)}, u32[]{:S(2)}) collective-permute-start(bf16[64,2048]{1,0:T(8,128)(2,1)S(1)} %slice.158), channel_id=1, source_target_pairs={{0,2},{1,3},{6,4},{7,5},{8,10},{9,11},{14,12},{15,13},{16,18},{17,... | collective-permute-start | bytes 786440 | tf_op jit(solution)/shard_map/ppermute | solution.py:287
  378.5 1.4 collective-permute-done.12
  379.9 1.3 collective-permute-start.17
  381.4 2.1 collective-permute-done.14
  383.5 4.4 %collective-permute-start.19 = (bf16[64,2048]{1,0:T(8,128)(2,1)S(1)}, bf16[64,2048]{1,0:T(8,128)(2,1)S(1)}, u32[]{:S(2)}, u32[]{:S(2)}) collective-permute-start(bf16[64,2048]{1,0:T(8,128)(2,1)S(1)} %slice.163), channel_id=1, source_target_pairs={{0,2},{1,3},{6,4},{7,5},{8,10},{9,11},{14,12},{15,13},{16,18},{17,... | collective-permute-start | bytes 786440 | tf_op jit(solution)/shard_map/ppermute | solution.py:287
  387.9 1.9 collective-permute-done.17
  389.7 1.3 collective-permute-start.22
  391.9 4.4 %collective-permute-start.24 = (bf16[64,2048]{1,0:T(8,128)(2,1)S(1)}, bf16[64,2048]{1,0:T(8,128)(2,1)S(1)}, u32[]{:S(2)}, u32[]{:S(2)}) collective-permute-start(bf16[64,2048]{1,0:T(8,128)(2,1)S(1)} %slice.168), channel_id=1, source_target_pairs={{0,2},{1,3},{6,4},{7,5},{8,10},{9,11},{14,12},{15,13},{16,18},{17,... | collective-permute-start | bytes 786440 | tf_op jit(solution)/shard_map/ppermute | solution.py:287
  396.3 3.7 collective-permute-done.22
  401.5 1.3 collective-permute-start.32
  402.8 5.5 %collective-permute-done.27 = bf16[64,2048]{1,0:T(8,128)(2,1)S(1)} collective-permute-done((bf16[64,2048]{1,0:T(8,128)(2,1)S(1)}, bf16[64,2048]{1,0:T(8,128)(2,1)S(1)}, u32[]{:S(2)}, u32[]{:S(2)}) %collective-permute-start.27) | collective-permute-done | bytes 262176 | tf_op jit(solution)/shard_map/ppermute | solution.py:290
  409.8 1.8 abs_reduce_fusion
  411.7 3.3 collective-permute-start.38
  415.0 2.0 collective-permute-done.38
  417.1 4.0 collective-permute-done.39
  421.7 4.4 %collective-permute-done.40 = f32[11264]{0:T(1024)S(1)} collective-permute-done((f32[11264]{0:T(1024)S(1)}, f32[11264]{0:T(1024)S(1)}, u32[]{:S(2)}, u32[]{:S(2)}) %collective-permute-start.40) | collective-permute-done | bytes 45088 | tf_op jit(solution)/shard_map/ppermute | solution.py:307
  (102 shorter events, 17.3 us)
Async XLA Ops:
  7.8 15.5 %all-to-all-start = ((s32[8,1,512]{2,1,0:T(1,128)}), s32[8,1,512]{2,1,0:T(1,128)S(1)}, u32[]{:S(2)}, u32[]{:S(2)}) async-start(s32[8,1,512]{2,1,0:T(1,128)} %bitcast.1), calls=%async_computation | async-start | bytes 32768 | tf_op jit(solution)/shard_map/all_to_all | solution.py:232
  15.0 1.6 copy-start.1
  23.2 31.4 %all-to-all-start.1 = ((bf16[8,128,512]{2,1,0:T(8,128)(2,1)}), bf16[8,128,512]{2,1,0:T(8,128)(2,1)S(1)}, u32[]{:S(2)}, u32[]{:S(2)}) async-start(bf16[8,128,512]{2,1,0:T(8,128)(2,1)} %route.1), calls=%async_computation.1 | async-start | bytes 2097152 | tf_op jit(solution)/shard_map/all_to_all | solution.py:233
  54.7 29.0 %copy-start.3 = (s32[22,3]{0,1:T(4,128)S(1)}, s32[22,3]{0,1:T(4,128)}, u32[]{:S(2)}) copy-start(s32[22,3]{0,1:T(4,128)} %param.9) | copy-start | bytes 796
  60.5 23.2 %collective-permute-start.1 = (bf16[16,128,256]{2,1,0:T(8,128)(2,1)S(1)}, bf16[16,128,256]{2,1,0:T(8,128)(2,1)S(1)}, u32[]{:S(2)}, u32[]{:S(2)}) collective-permute-start(bf16[16,128,256]{2,1,0:T(8,128)(2,1)S(1)} %merge.1.refs_0_), channel_id=1, source_target_pairs={{0,16},{8,24},{16,0},{24,8},{1,17},{9,25},{17,1},{25,9},{2,18},{10... | collective-permute-start | bytes 3145736 | tf_op jit(solution)/shard_map/ppermute | solution.py:250
  62.1 22.2 %collective-permute-start = (bf16[16,128,256]{2,1,0:T(8,128)(2,1)S(1)}, bf16[16,128,256]{2,1,0:T(8,128)(2,1)}, u32[]{:S(2)}, u32[]{:S(2)}) collective-permute-start(bf16[16,128,256]{2,1,0:T(8,128)(2,1)S(1)} %merge.1.refs_0_), channel_id=1, source_target_pairs={{0,8},{8,0},{16,24},{24,16},{1,9},{9,1},{17,25},{25,17},{2,10},{10... | collective-permute-start | bytes 3145736 | tf_op jit(solution)/shard_map/ppermute | solution.py:253
  83.7 2.8 collective-permute-start.2
  86.4 17.2 %copy-start = (s32[22,1]{0,1:T(1,128)S(1)}, s32[22,1]{0,1:T(1,128)}, u32[]{:S(2)}) copy-start(s32[22,1]{0,1:T(1,128)} %param.8) | copy-start | bytes 268
  133.2 48.7 %collective-permute-start.3 = (bf16[256,1536]{1,0:T(8,128)(2,1)S(1)}, bf16[256,1536]{1,0:T(8,128)(2,1)S(1)}, u32[]{:S(2)}, u32[]{:S(2)}) collective-permute-start(bf16[256,1536]{1,0:T(8,128)(2,1)S(1)} %get-tuple-element.23), channel_id=1, source_target_pairs={{0,1},{1,0},{2,3},{3,2},{4,5},{5,4},{6,7},{7,6},{8,9},{9,8},{10,11... | collective-permute-start | bytes 2359304 | tf_op jit(solution)/shard_map/ppermute | solution.py:285
  136.0 23.5 %collective-permute-start.33 = (bf16[256,512]{1,0:T(8,128)(2,1)S(1)}, bf16[256,512]{1,0:T(8,128)(2,1)S(1)}, u32[]{:S(2)}, u32[]{:S(2)}) collective-permute-start(bf16[256,512]{1,0:T(8,128)(2,1)S(1)} %get-tuple-element.35), channel_id=1, source_target_pairs={{0,1},{1,0},{2,3},{3,2},{4,5},{5,4},{6,7},{7,6},{8,9},{9,8},{10,11... | collective-permute-start | bytes 786440 | tf_op jit(solution)/shard_map/ppermute | solution.py:285
  141.1 37.8 %collective-permute-start.28 = (bf16[256,1024]{1,0:T(8,128)(2,1)S(1)}, bf16[256,1024]{1,0:T(8,128)(2,1)S(1)}, u32[]{:S(2)}, u32[]{:S(2)}) collective-permute-start(bf16[256,1024]{1,0:T(8,128)(2,1)S(1)} %get-tuple-element.33), channel_id=1, source_target_pairs={{0,1},{1,0},{2,3},{3,2},{4,5},{5,4},{6,7},{7,6},{8,9},{9,8},{10,11... | collective-permute-start | bytes 1572872 | tf_op jit(solution)/shard_map/ppermute | solution.py:285
  159.7 19.0 %collective-permute-start.35 = (bf16[128,512]{1,0:T(8,128)(2,1)S(1)}, bf16[128,512]{1,0:T(8,128)(2,1)S(1)}, u32[]{:S(2)}, u32[]{:S(2)}) collective-permute-start(bf16[128,512]{1,0:T(8,128)(2,1)S(1)} %slice.179), channel_id=1, source_target_pairs={{0,2},{1,3},{6,4},{7,5},{8,10},{9,11},{14,12},{15,13},{16,18},{17,... | collective-permute-start | bytes 393224 | tf_op jit(solution)/shard_map/ppermute | solution.py:288
  176.6 26.2 %collective-permute-start.8 = (bf16[256,2048]{1,0:T(8,128)(2,1)S(1)}, bf16[256,2048]{1,0:T(8,128)(2,1)S(1)}, u32[]{:S(2)}, u32[]{:S(2)}) collective-permute-start(bf16[256,2048]{1,0:T(8,128)(2,1)S(1)} %get-tuple-element.25), channel_id=1, source_target_pairs={{0,1},{1,0},{2,3},{3,2},{4,5},{5,4},{6,7},{7,6},{8,9},{9,8},{10,11... | collective-permute-start | bytes 3145736 | tf_op jit(solution)/shard_map/ppermute | solution.py:285
  176.6 48.6 %collective-permute-start.13 = (bf16[256,2048]{1,0:T(8,128)(2,1)S(1)}, bf16[256,2048]{1,0:T(8,128)(2,1)S(1)}, u32[]{:S(2)}, u32[]{:S(2)}) collective-permute-start(bf16[256,2048]{1,0:T(8,128)(2,1)S(1)} %get-tuple-element.27), channel_id=1, source_target_pairs={{0,1},{1,0},{2,3},{3,2},{4,5},{5,4},{6,7},{7,6},{8,9},{9,8},{10,11... | collective-permute-start | bytes 3145736 | tf_op jit(solution)/shard_map/ppermute | solution.py:285
  178.7 69.0 %collective-permute-start.18 = (bf16[256,2048]{1,0:T(8,128)(2,1)S(1)}, bf16[256,2048]{1,0:T(8,128)(2,1)S(1)}, u32[]{:S(2)}, u32[]{:S(2)}) collective-permute-start(bf16[256,2048]{1,0:T(8,128)(2,1)S(1)} %get-tuple-element.29), channel_id=1, source_target_pairs={{0,1},{1,0},{2,3},{3,2},{4,5},{5,4},{6,7},{7,6},{8,9},{9,8},{10,11... | collective-permute-start | bytes 3145736 | tf_op jit(solution)/shard_map/ppermute | solution.py:285
  178.9 0.9 collective-permute-start.36
  179.8 88.7 %collective-permute-start.23 = (bf16[256,2048]{1,0:T(8,128)(2,1)S(1)}, bf16[256,2048]{1,0:T(8,128)(2,1)S(1)}, u32[]{:S(2)}, u32[]{:S(2)}) collective-permute-start(bf16[256,2048]{1,0:T(8,128)(2,1)S(1)} %get-tuple-element.31), channel_id=1, source_target_pairs={{0,1},{1,0},{2,3},{3,2},{4,5},{5,4},{6,7},{7,6},{8,9},{9,8},{10,11... | collective-permute-start | bytes 3145736 | tf_op jit(solution)/shard_map/ppermute | solution.py:285
  181.8 12.6 %collective-permute-start.30 = (bf16[128,1024]{1,0:T(8,128)(2,1)S(1)}, bf16[128,1024]{1,0:T(8,128)(2,1)S(1)}, u32[]{:S(2)}, u32[]{:S(2)}) collective-permute-start(bf16[128,1024]{1,0:T(8,128)(2,1)S(1)} %slice.174), channel_id=1, source_target_pairs={{0,2},{1,3},{6,4},{7,5},{8,10},{9,11},{14,12},{15,13},{16,18},{17,... | collective-permute-start | bytes 786440 | tf_op jit(solution)/shard_map/ppermute | solution.py:288
  194.4 215.3 %collective-permute-start.34 = (bf16[64,512]{1,0:T(8,128)(2,1)S(1)}, bf16[64,512]{1,0:T(8,128)(2,1)S(1)}, u32[]{:S(2)}, u32[]{:S(2)}) collective-permute-start(bf16[64,512]{1,0:T(8,128)(2,1)S(1)} %slice.178), channel_id=1, source_target_pairs={{0,2},{1,3},{6,4},{7,5},{8,10},{9,11},{14,12},{15,13},{16,18},{17,... | collective-permute-start | bytes 196616 | tf_op jit(solution)/shard_map/ppermute | solution.py:287
  202.7 205.7 %collective-permute-start.29 = (bf16[64,1024]{1,0:T(8,128)(2,1)S(1)}, bf16[64,1024]{1,0:T(8,128)(2,1)S(1)}, u32[]{:S(2)}, u32[]{:S(2)}) collective-permute-start(bf16[64,1024]{1,0:T(8,128)(2,1)S(1)} %slice.173), channel_id=1, source_target_pairs={{0,2},{1,3},{6,4},{7,5},{8,10},{9,11},{14,12},{15,13},{16,18},{17,... | collective-permute-start | bytes 393224 | tf_op jit(solution)/shard_map/ppermute | solution.py:287
  225.2 55.2 %collective-permute-start.5 = (bf16[128,1536]{1,0:T(8,128)(2,1)S(1)}, bf16[128,1536]{1,0:T(8,128)(2,1)S(1)}, u32[]{:S(2)}, u32[]{:S(2)}) collective-permute-start(bf16[128,1536]{1,0:T(8,128)(2,1)S(1)} %slice.149), channel_id=1, source_target_pairs={{0,2},{1,3},{6,4},{7,5},{8,10},{9,11},{14,12},{15,13},{16,18},{17,... | collective-permute-start | bytes 1179656 | tf_op jit(solution)/shard_map/ppermute | solution.py:288
  247.7 77.1 %collective-permute-start.4 = (bf16[64,1536]{1,0:T(8,128)(2,1)S(1)}, bf16[64,1536]{1,0:T(8,128)(2,1)S(1)}, u32[]{:S(2)}, u32[]{:S(2)}) collective-permute-start(bf16[64,1536]{1,0:T(8,128)(2,1)S(1)} %slice.148), channel_id=1, source_target_pairs={{0,2},{1,3},{6,4},{7,5},{8,10},{9,11},{14,12},{15,13},{16,18},{17,... | collective-permute-start | bytes 589832 | tf_op jit(solution)/shard_map/ppermute | solution.py:287
  268.4 1.1 collective-permute-start.31
  269.6 22.8 %collective-permute-start.10 = (bf16[128,2048]{1,0:T(8,128)(2,1)S(1)}, bf16[128,2048]{1,0:T(8,128)(2,1)S(1)}, u32[]{:S(2)}, u32[]{:S(2)}) collective-permute-start(bf16[128,2048]{1,0:T(8,128)(2,1)S(1)} %slice.154), channel_id=1, source_target_pairs={{0,2},{1,3},{6,4},{7,5},{8,10},{9,11},{14,12},{15,13},{16,18},{17,... | collective-permute-start | bytes 1572872 | tf_op jit(solution)/shard_map/ppermute | solution.py:288
  280.4 23.3 %collective-permute-start.15 = (bf16[128,2048]{1,0:T(8,128)(2,1)S(1)}, bf16[128,2048]{1,0:T(8,128)(2,1)S(1)}, u32[]{:S(2)}, u32[]{:S(2)}) collective-permute-start(bf16[128,2048]{1,0:T(8,128)(2,1)S(1)} %slice.159), channel_id=1, source_target_pairs={{0,2},{1,3},{6,4},{7,5},{8,10},{9,11},{14,12},{15,13},{16,18},{17,... | collective-permute-start | bytes 1572872 | tf_op jit(solution)/shard_map/ppermute | solution.py:288
  292.4 22.5 %collective-permute-start.20 = (bf16[128,2048]{1,0:T(8,128)(2,1)S(1)}, bf16[128,2048]{1,0:T(8,128)(2,1)S(1)}, u32[]{:S(2)}, u32[]{:S(2)}) collective-permute-start(bf16[128,2048]{1,0:T(8,128)(2,1)S(1)} %slice.164), channel_id=1, source_target_pairs={{0,2},{1,3},{6,4},{7,5},{8,10},{9,11},{14,12},{15,13},{16,18},{17,... | collective-permute-start | bytes 1572872 | tf_op jit(solution)/shard_map/ppermute | solution.py:288
  303.7 19.6 %collective-permute-start.25 = (bf16[128,2048]{1,0:T(8,128)(2,1)S(1)}, bf16[128,2048]{1,0:T(8,128)(2,1)S(1)}, u32[]{:S(2)}, u32[]{:S(2)}) collective-permute-start(bf16[128,2048]{1,0:T(8,128)(2,1)S(1)} %slice.169), channel_id=1, source_target_pairs={{0,2},{1,3},{6,4},{7,5},{8,10},{9,11},{14,12},{15,13},{16,18},{17,... | collective-permute-start | bytes 1572872 | tf_op jit(solution)/shard_map/ppermute | solution.py:288
  314.9 0.8 collective-permute-start.6
  315.7 20.6 %collective-permute-start.11 = (bf16[128,2048]{1,0:T(8,128)(2,1)S(1)}, bf16[128,2048]{1,0:T(8,128)(2,1)S(1)}, u32[]{:S(2)}, u32[]{:S(2)}) collective-permute-start(bf16[128,2048]{1,0:T(8,128)(2,1)S(1)} %add_convert_fusion.9), channel_id=1, source_target_pairs={{2,4},{3,5},{4,2},{5,3},{10,12},{11,13},{12,10},{13,11},{18,20},{1... | collective-permute-start | bytes 1572872 | tf_op jit(solution)/shard_map/ppermute | solution.py:289
  323.3 12.2 %collective-permute-start.7 = (bf16[64,1536]{1,0:T(8,128)(2,1)S(1)}, bf16[64,1536]{1,0:T(8,128)(2,1)S(1)}, u32[]{:S(2)}, u32[]{:S(2)}) collective-permute-start(bf16[64,1536]{1,0:T(8,128)(2,1)S(1)} %fusion.12), channel_id=1, source_target_pairs={{2,0},{3,1},{4,6},{5,7},{10,8},{11,9},{12,14},{13,15},{18,16},{19,... | collective-permute-start | bytes 589832 | tf_op jit(solution)/shard_map/ppermute | solution.py:290
  324.7 85.0 %collective-permute-start.37 = (bf16[64,512]{1,0:T(8,128)(2,1)S(1)}, bf16[64,512]{1,0:T(8,128)(2,1)S(1)}, u32[]{:S(2)}, u32[]{:S(2)}) collective-permute-start(bf16[64,512]{1,0:T(8,128)(2,1)S(1)} %fusion.18), channel_id=1, source_target_pairs={{2,0},{3,1},{4,6},{5,7},{10,8},{11,9},{12,14},{13,15},{18,16},{19,... | collective-permute-start | bytes 196616 | tf_op jit(solution)/shard_map/ppermute | solution.py:290
  335.5 1.6 collective-permute-start.16
  336.4 1.6 collective-permute-start.21
  337.1 31.3 %collective-permute-start.26 = (bf16[128,2048]{1,0:T(8,128)(2,1)S(1)}, bf16[128,2048]{1,0:T(8,128)(2,1)S(1)}, u32[]{:S(2)}, u32[]{:S(2)}) collective-permute-start(bf16[128,2048]{1,0:T(8,128)(2,1)S(1)} %add_convert_fusion.6), channel_id=1, source_target_pairs={{2,4},{3,5},{4,2},{5,3},{10,12},{11,13},{12,10},{13,11},{18,20},{1... | collective-permute-start | bytes 1572872 | tf_op jit(solution)/shard_map/ppermute | solution.py:289
  337.9 36.2 %collective-permute-start.9 = (bf16[64,2048]{1,0:T(8,128)(2,1)S(1)}, bf16[64,2048]{1,0:T(8,128)(2,1)S(1)}, u32[]{:S(2)}, u32[]{:S(2)}) collective-permute-start(bf16[64,2048]{1,0:T(8,128)(2,1)S(1)} %slice.153), channel_id=1, source_target_pairs={{0,2},{1,3},{6,4},{7,5},{8,10},{9,11},{14,12},{15,13},{16,18},{17,... | collective-permute-start | bytes 786440 | tf_op jit(solution)/shard_map/ppermute | solution.py:287
  368.4 11.5 %collective-permute-start.12 = (bf16[64,2048]{1,0:T(8,128)(2,1)S(1)}, bf16[64,2048]{1,0:T(8,128)(2,1)S(1)}, u32[]{:S(2)}, u32[]{:S(2)}) collective-permute-start(bf16[64,2048]{1,0:T(8,128)(2,1)S(1)} %fusion), channel_id=1, source_target_pairs={{2,0},{3,1},{4,6},{5,7},{10,8},{11,9},{12,14},{13,15},{18,16},{19,... | collective-permute-start | bytes 786440 | tf_op jit(solution)/shard_map/ppermute | solution.py:290
  374.1 9.4 %collective-permute-start.14 = (bf16[64,2048]{1,0:T(8,128)(2,1)S(1)}, bf16[64,2048]{1,0:T(8,128)(2,1)S(1)}, u32[]{:S(2)}, u32[]{:S(2)}) collective-permute-start(bf16[64,2048]{1,0:T(8,128)(2,1)S(1)} %slice.158), channel_id=1, source_target_pairs={{0,2},{1,3},{6,4},{7,5},{8,10},{9,11},{14,12},{15,13},{16,18},{17,... | collective-permute-start | bytes 786440 | tf_op jit(solution)/shard_map/ppermute | solution.py:287
  379.9 9.8 %collective-permute-start.17 = (bf16[64,2048]{1,0:T(8,128)(2,1)S(1)}, bf16[64,2048]{1,0:T(8,128)(2,1)S(1)}, u32[]{:S(2)}, u32[]{:S(2)}) collective-permute-start(bf16[64,2048]{1,0:T(8,128)(2,1)S(1)} %fusion.3), channel_id=1, source_target_pairs={{2,0},{3,1},{4,6},{5,7},{10,8},{11,9},{12,14},{13,15},{18,16},{19,... | collective-permute-start | bytes 786440 | tf_op jit(solution)/shard_map/ppermute | solution.py:290
  383.5 8.4 %collective-permute-start.19 = (bf16[64,2048]{1,0:T(8,128)(2,1)S(1)}, bf16[64,2048]{1,0:T(8,128)(2,1)S(1)}, u32[]{:S(2)}, u32[]{:S(2)}) collective-permute-start(bf16[64,2048]{1,0:T(8,128)(2,1)S(1)} %slice.163), channel_id=1, source_target_pairs={{0,2},{1,3},{6,4},{7,5},{8,10},{9,11},{14,12},{15,13},{16,18},{17,... | collective-permute-start | bytes 786440 | tf_op jit(solution)/shard_map/ppermute | solution.py:287
  389.7 10.3 %collective-permute-start.22 = (bf16[64,2048]{1,0:T(8,128)(2,1)S(1)}, bf16[64,2048]{1,0:T(8,128)(2,1)S(1)}, u32[]{:S(2)}, u32[]{:S(2)}) collective-permute-start(bf16[64,2048]{1,0:T(8,128)(2,1)S(1)} %fusion.6), channel_id=1, source_target_pairs={{2,0},{3,1},{4,6},{5,7},{10,8},{11,9},{12,14},{13,15},{18,16},{19,... | collective-permute-start | bytes 786440 | tf_op jit(solution)/shard_map/ppermute | solution.py:290
  391.2 18.7 %copy-start.2 = (f32[11264]{0:T(1024)S(1)}, f32[11264]{0:T(1024)}, u32[]{:S(2)}) copy-start(f32[11264]{0:T(1024)} %param.11) | copy-start | bytes 135172
  391.9 9.6 %collective-permute-start.24 = (bf16[64,2048]{1,0:T(8,128)(2,1)S(1)}, bf16[64,2048]{1,0:T(8,128)(2,1)S(1)}, u32[]{:S(2)}, u32[]{:S(2)}) collective-permute-start(bf16[64,2048]{1,0:T(8,128)(2,1)S(1)} %slice.168), channel_id=1, source_target_pairs={{0,2},{1,3},{6,4},{7,5},{8,10},{9,11},{14,12},{15,13},{16,18},{17,... | collective-permute-start | bytes 786440 | tf_op jit(solution)/shard_map/ppermute | solution.py:287
  400.0 8.3 %collective-permute-start.27 = (bf16[64,2048]{1,0:T(8,128)(2,1)S(1)}, bf16[64,2048]{1,0:T(8,128)(2,1)S(1)}, u32[]{:S(2)}, u32[]{:S(2)}) collective-permute-start(bf16[64,2048]{1,0:T(8,128)(2,1)S(1)} %fusion.9), channel_id=1, source_target_pairs={{2,0},{3,1},{4,6},{5,7},{10,8},{11,9},{12,14},{13,15},{18,16},{19,... | collective-permute-start | bytes 786440 | tf_op jit(solution)/shard_map/ppermute | solution.py:290
  401.5 8.2 %collective-permute-start.32 = (bf16[64,1024]{1,0:T(8,128)(2,1)S(1)}, bf16[64,1024]{1,0:T(8,128)(2,1)S(1)}, u32[]{:S(2)}, u32[]{:S(2)}) collective-permute-start(bf16[64,1024]{1,0:T(8,128)(2,1)S(1)} %fusion.15), channel_id=1, source_target_pairs={{2,0},{3,1},{4,6},{5,7},{10,8},{11,9},{12,14},{13,15},{18,16},{19,... | collective-permute-start | bytes 393224 | tf_op jit(solution)/shard_map/ppermute | solution.py:290
  411.7 5.3 %collective-permute-start.38 = (f32[11264]{0:T(1024)S(1)}, f32[11264]{0:T(1024)S(1)}, u32[]{:S(2)}, u32[]{:S(2)}) collective-permute-start(f32[11264]{0:T(1024)S(1)} %get-tuple-element.36), channel_id=1, source_target_pairs={{0,1},{1,0},{2,3},{3,2},{4,5},{5,4},{6,7},{7,6},{8,9},{9,8},{10,11... | collective-permute-start | bytes 135176 | tf_op jit(solution)/shard_map/ppermute | solution.py:307
  417.0 4.1 collective-permute-start.39
  421.1 5.0 %collective-permute-start.40 = (f32[11264]{0:T(1024)S(1)}, f32[11264]{0:T(1024)S(1)}, u32[]{:S(2)}, u32[]{:S(2)}) collective-permute-start(f32[11264]{0:T(1024)S(1)} %max.10), channel_id=1, source_target_pairs={{0,4},{1,5},{2,6},{3,7},{4,0},{5,1},{6,2},{7,3},{8,12},{9,13},{10,... | collective-permute-start | bytes 135176 | tf_op jit(solution)/shard_map/ppermute | solution.py:307

commit v2 on v0

v2 whole, which is shorter than its diff:
```python
import functools

import jax
import jax.numpy as jnp
from jax import lax
from jax.experimental import pallas as pl
from jax.experimental.pallas import tpu as pltpu
from jax.sharding import PartitionSpec as P

NB = 71680
TILE = 128
WINDOW = 4
EARLY = 8
STEP = 2
F32 = jnp.float32
BF16 = jnp.bfloat16


def params(n, mib=16):
    return pltpu.CompilerParams(
        dimension_semantics=("arbitrary",) * n, vmem_limit_bytes=mib * 1024 * 1024
    )


def cost(flops, nbytes):
    return pl.CostEstimate(flops=int(flops), bytes_accessed=int(nbytes), transcendentals=0)


def hot(ids, first, rows):
    at = lax.broadcasted_iota(jnp.int32, (rows, ids.shape[1]), 0) + first
    return (at == ids).astype(F32).astype(BF16)


def down(row):
    return jnp.broadcast_to(row, (row.shape[1], row.shape[1])).T


def hot_rows(ids, first, columns):
    at = lax.broadcasted_iota(jnp.int32, ids.shape, 1) + first
    tables = [
        (ids == at + c).astype(F32).astype(BF16) for c in range(0, columns, ids.shape[1])
    ]
    return jnp.concatenate(tables, axis=1)


def running_count(mask, part):
    rows, lanes = mask.shape
    mask = mask.astype(F32).astype(BF16)
    up_to = lax.broadcasted_iota(jnp.int32, (lanes, lanes), 0) <= lax.broadcasted_iota(
        jnp.int32, (lanes, lanes), 1
    )
    inside = jnp.dot(mask, up_to.astype(F32).astype(BF16), preferred_element_type=F32)
    r = lax.broadcasted_iota(jnp.int32, (rows, rows), 0)
    c = lax.broadcasted_iota(jnp.int32, (rows, rows), 1)
    earlier = ((c < r) & ((c ^ r) < part)).astype(F32).astype(BF16)
    before = jnp.dot(earlier, mask, preferred_element_type=F32)
    return (inside + jnp.sum(before, axis=1, keepdims=True)).astype(jnp.int32)


def route_kernel(here_ref, bus_ref, values_ref, out_ref, rounded, places, *, groups, bus_dev):
    del here_ref
    group = pl.program_id(0)
    width = out_ref.shape[2]
    rows = bus_ref.shape[0]

    @pl.when(group == 0)
    def _():
        rounded[...] = values_ref[...].astype(BF16)
        ids = bus_ref[...]
        masks = [(ids >= g * bus_dev) & (ids < (g + 1) * bus_dev) for g in range(groups)]
        masks = jnp.concatenate([mask.astype(F32) for mask in masks], axis=0)
        count = running_count(masks, rows)
        place = jnp.zeros(ids.shape, jnp.int32)
        for g in range(groups):
            part = slice(g * rows, (g + 1) * rows)
            place += jnp.where(masks[part] > 0, count[part] + (g * width - 1), 0)
        for r in range(rows):
            places[r * TILE : (r + 1) * TILE] = down(place[r : r + 1])

    total = jnp.zeros(out_ref.shape[1:], F32)
    step = 4 * TILE
    for at in range(0, rows * TILE, step):
        table = hot_rows(places[at : at + step], group * width, width)
        total += jnp.dot(rounded[:, at : at + step], table, preferred_element_type=F32)
    out_ref[0] = total.astype(BF16)


def route(here, site_bus, values, groups, bus_dev):
    scen, depth = values.shape
    width = depth // groups
    rows = depth // TILE
    return pl.pallas_call(
        functools.partial(route_kernel, groups=groups, bus_dev=bus_dev),
        grid_spec=pltpu.PrefetchScalarGridSpec(
            num_scalar_prefetch=1,
            grid=(groups,),
            in_specs=[
                pl.BlockSpec((rows, TILE), lambda g, here: (here[0], 0)),
                pl.BlockSpec((scen, depth), lambda g, here: (0, 0)),
            ],
            out_specs=pl.BlockSpec((1, scen, width), lambda g, here: (g, 0, 0)),
            scratch_shapes=[pltpu.VMEM((scen, depth), BF16), pltpu.VMEM((depth, TILE), jnp.int32)],
        ),
        out_shape=jax.ShapeDtypeStruct((groups, scen, width), BF16),
        compiler_params=params(1),
        cost_estimate=cost(4 * scen * depth * depth, 4 * scen * depth),
        name="route",
    )(here.reshape(1), site_bus.reshape(-1, TILE), values)


def arrivals_kernel(here_ref, bus_ref, out_ref, places, local, *, bus_dev):
    block = pl.program_id(0)
    width = out_ref.shape[2]
    rows = bus_ref.shape[0] // pl.num_programs(0)

    @pl.when(block == 0)
    def _():
        ids = bus_ref[...] - here_ref[0] * bus_dev
        mask = (ids >= 0) & (ids < bus_dev)
        places[...] = jnp.where(mask, running_count(mask, rows) - 1, -1)
        local[...] = jnp.where(mask, ids, 0)

    sub = lax.broadcasted_iota(jnp.int32, (16, TILE), 0)
    total = jnp.zeros((16, width), F32)
    step = 4
    for at in range(0, rows, step):
        tables, parts = [], []
        for r in range(at, at + step):
            row = pl.ds(block * rows + r, 1)
            tables.append(hot_rows(down(places[row]), 0, width))
            ids = local[row]
            part = jnp.where(sub == 0, ids >> 7, jnp.where(sub == 1, ids & 127, 0))
            parts.append(part.astype(F32).astype(BF16))
        total += jnp.dot(
            jnp.concatenate(parts, axis=1),
            jnp.concatenate(tables, axis=0),
            preferred_element_type=F32,
        )
    out_ref[0] = (total[0:1] * 128.0 + total[1:2]).astype(jnp.int32)


def arrivals(here, site_bus, groups, site_dev, bus_dev):
    width = site_dev // groups
    rows = site_bus.shape[0] // TILE
    return pl.pallas_call(
        functools.partial(arrivals_kernel, bus_dev=bus_dev),
        grid_spec=pltpu.PrefetchScalarGridSpec(
            num_scalar_prefetch=1,
            grid=(groups,),
            in_specs=[pl.BlockSpec((rows, TILE), lambda g, here: (0, 0))],
            out_specs=pl.BlockSpec((1, 1, width), lambda g, here: (g, 0, 0)),
            scratch_shapes=[pltpu.VMEM((rows, TILE), jnp.int32)] * 2,
        ),
        out_shape=jax.ShapeDtypeStruct((groups, 1, width), jnp.int32),
        compiler_params=params(1),
        cost_estimate=cost(4 * 16 * site_dev * site_dev, 4 * rows * TILE),
        name="arrivals",
    )(here.reshape(1), site_bus.reshape(-1, TILE))


def merge_kernel(order_ref, runs_ref, out_ref):
    runs, rows, width = runs_ref.shape
    ids = order_ref[0]
    total = jnp.zeros((rows, ids.shape[1]), F32)
    for run in range(runs):
        total += jnp.dot(runs_ref[run], hot(ids, run * width, width), preferred_element_type=F32)
    total = total.astype(BF16)
    for part in range(out_ref.shape[0]):
        out_ref[part] = total[:, part * TILE : (part + 1) * TILE]


def merge(order, runs):
    count, rows, width = runs.shape
    sites = count * width
    step = 4 * TILE
    return pl.pallas_call(
        merge_kernel,
        grid=(sites // step,),
        in_specs=[
            pl.BlockSpec((1, 1, step), lambda t: (t, 0, 0)),
            pl.BlockSpec((count, rows, width), lambda t: (0, 0, 0)),
        ],
        out_specs=pl.BlockSpec((step // TILE, rows, TILE), lambda t: (t, 0, 0)),
        out_shape=jax.ShapeDtypeStruct((sites // TILE, rows, TILE), BF16),
        compiler_params=params(1),
        cost_estimate=cost(4 * rows * sites * sites, 4 * rows * sites),
        name="merge",
    )(order.reshape(sites // step, 1, step), runs)


def inject_kernel(first_ref, windows_ref, rows_ref, ids_ref, *refs):
    pieces, out_ref, total, places = refs[:-3], refs[-3], refs[-2], refs[-1]
    zone = pl.program_id(0)
    scen, width = total.shape
    tiles = ids_ref.shape[0]

    @pl.when(zone == 0)
    def _():
        for t in range(tiles):
            places[t] = down(ids_ref[t])

    def window(w):
        parts, tables = [], []
        for j in range(WINDOW):
            t = first_ref[zone] + w * WINDOW + j
            at = jnp.minimum(t, tiles - 1)
            ids = jnp.where(t < tiles, places[at], -1)
            tables.append(hot_rows(ids, zone * width, width))
            parts.append(jnp.concatenate([piece[at] for piece in pieces], axis=0))
        return jnp.dot(
            jnp.concatenate(parts, axis=1),
            jnp.concatenate(tables, axis=0),
            preferred_element_type=F32,
        )

    total[...] = window(0)

    @pl.loop(1, windows_ref[zone])
    def _(w):
        total[...] += window(w)

    blocks = rows_ref.shape[0]
    high = scen // blocks
    for j in range(blocks):
        rows = pl.ds(pl.multiple_of(rows_ref[j] * high, high), high)
        out_ref[0, j * high : (j + 1) * high] = total[rows, :].astype(BF16)


def inject(first, windows, row_blocks, ids, pieces, zones, width):
    tiles, rows, _ = pieces[0].shape
    scen = rows * len(pieces)
    whole = pl.BlockSpec((tiles, rows, TILE), lambda z, *_: (0, 0, 0))
    return pl.pallas_call(
        inject_kernel,
        grid_spec=pltpu.PrefetchScalarGridSpec(
            num_scalar_prefetch=3,
            grid=(zones,),
            in_specs=[pl.BlockSpec((tiles, 1, TILE), lambda z, *_: (0, 0, 0))]
            + [whole] * len(pieces),
            out_specs=pl.BlockSpec((1, scen, width), lambda z, *_: (z, 0, 0)),
            scratch_shapes=[
                pltpu.VMEM((scen, width), F32),
                pltpu.VMEM((tiles, TILE, TILE), jnp.int32),
            ],
        ),
        out_shape=jax.ShapeDtypeStruct((zones, scen, width), BF16),
        compiler_params=params(1),
        cost_estimate=cost(1 << 16, 1 << 10),
        name="inject",
    )(first, windows, row_blocks, ids, *pieces)


def sum_x(give, own, received):
    rows = give.shape[0]
    return (
        add(give[...], received[:rows]).astype(BF16),
        add(own[...], received[rows:]).astype(BF16),
    )


def sum_z(own, received, near, high):
    mine = add(own[...], received[...]).astype(BF16)
    if mine.shape[0] == high:
        return mine, mine
    low, top = mine[:high], mine[high:]
    return jnp.where(near, top, low), jnp.where(near, low, top)


def run_stages(taken, outs, near, high):
    if taken[0]:
        for result in sum_x(*taken[0]):
            next(outs)[...] = result
    if taken[1]:
        for result in sum_z(*taken[1], near, high):
            next(outs)[...] = result
    if taken[2]:
        next(outs)[...] = add(taken[2][0][...], taken[2][1][...])


def stage_shapes(stages, high):
    shapes = [jax.ShapeDtypeStruct(array.shape, BF16) for array in stages[0][:2]]
    shapes += [jax.ShapeDtypeStruct((high, array.shape[1]), BF16) for array in stages[1]]
    return shapes + [jax.ShapeDtypeStruct(array.shape, F32) for array in stages[2][:1]]


def sums_kernel(near_ref, *refs, stages, high):
    extra = iter(refs)
    taken = [[next(extra) for _ in range(count)] for count in stages]
    run_stages(taken, extra, near_ref[0] == 1, high)


def sums(near, stages, high):
    vmem = pl.BlockSpec(memory_space=pltpu.VMEM)
    shapes = stage_shapes(stages, high)
    return pl.pallas_call(
        functools.partial(sums_kernel, stages=[len(stage) for stage in stages], high=high),
        in_specs=[pl.BlockSpec(memory_space=pltpu.SMEM)] + [vmem] * sum(map(len, stages)),
        out_specs=[vmem] * len(shapes),
        out_shape=shapes,
        compiler_params=pltpu.CompilerParams(vmem_limit_bytes=32 * 1024 * 1024),
        cost_estimate=cost(1 << 16, 1 << 10),
        name="sums",
    )(near, *[array for stage in stages for array in stage])


def flow_kernel(
    count_ref, zone_ref, last_ref, near_ref, token_ref, *refs, base, slots, halves, splits, stages
):
    inj, blocks = refs[: halves * slots], refs[halves * slots : (halves + 1) * slots]
    extra = iter(refs[(halves + 1) * slots :])
    taken = [[next(extra) for _ in range(count)] for count in stages]
    outs = [next(extra) for _ in splits]

    if any(stages):

        @pl.when(pl.program_id(0) == 0)
        def _():
            run_stages(taken, extra, near_ref[0] == 1, splits[-1][0])

    live = count_ref[pl.program_id(0) + base]
    for count in range(slots + 1):

        @pl.when(live == count)
        def _(count=count):
            if count == 0:
                for out in outs:
                    out[...] = jnp.zeros_like(out)
                return
            for half in range(halves):
                total = sum(
                    lax.dot_general(
                        inj[half * slots + k][0],
                        blocks[k][0, 0],
                        (((1,), (1,)), ((), ())),
                        preferred_element_type=F32,
                    )
                    for k in range(count)
                )
                row = 0
                for out, parts in zip(outs, splits):
                    at = half * parts[0]
                    for rows in parts:
                        out[at : at + rows] = total[row : row + rows].astype(BF16)
                        row += rows
                        at += halves * rows


def last_live(count, slots):
    zones = count.shape[0]
    at = jnp.arange(zones, dtype=jnp.int32)[:, None]
    live = jnp.arange(slots, dtype=jnp.int32)[None, :] < count[:, None]
    return lax.cummax(jnp.where(live, at, 0), axis=0).reshape(-1)


def partial_flow(
    count, zone, last, near, token, injs, blocks, base, zones, splits, stages=((), (), ())
):
    _, slots, lines, width = blocks.shape
    scen = injs[0].shape[1]
    halves = len(injs)

    def inj_at(k):
        def at(z, count, zone, last, near):
            return zone[last[(z + base) * slots + k] * slots + k], 0, 0

        return pl.BlockSpec((1, scen, width), at)

    def block_at(k):
        def at(z, count, zone, last, near):
            return last[(z + base) * slots + k], k, 0, 0

        return pl.BlockSpec((1, 1, lines, width), at)

    def whole(array):
        return pl.BlockSpec(array.shape, lambda z, *_: (0, 0))

    high = splits[-1][0]
    shapes = [
        jax.ShapeDtypeStruct((halves * sum(parts), zones * lines), BF16) for parts in splits
    ]
    later = stage_shapes(stages, high)
    extra = [array for stage in stages for array in stage]
    live = zones * slots / 2
    return pl.pallas_call(
        functools.partial(
            flow_kernel,
            base=base,
            slots=slots,
            halves=halves,
            splits=splits,
            stages=[len(stage) for stage in stages],
        ),
        grid_spec=pltpu.PrefetchScalarGridSpec(
            num_scalar_prefetch=4,
            grid=(zones,),
            in_specs=[pl.BlockSpec(memory_space=pl.ANY)]
            + [inj_at(k) for k in range(slots)] * halves
            + [block_at(k) for k in range(slots)]
            + [whole(array) for array in extra],
            out_specs=[
                pl.BlockSpec((halves * sum(parts), lines), lambda z, *_: (0, z))
                for parts in splits
            ]
            + [whole(array) for array in later],
        ),
        out_shape=shapes + later,
        compiler_params=params(1, 32),
        cost_estimate=cost(
            2 * live * halves * scen * lines * width, 2 * live * (halves * scen + lines) * width
        ),
        name="partial_flow",
    )(
        count,
        zone,
        last,
        near,
        token,
        *[inj for inj in injs for _ in range(slots)],
        *[blocks] * slots,
        *extra,
    )


def copy_after(values, token):
    def kernel(values_ref, token_ref, out_ref):
        out_ref[...] = values_ref[...]

    tiles, rows, lanes = values.shape
    block = pl.BlockSpec((tiles // 4, rows, lanes), lambda i: (i, 0, 0))
    return pl.pallas_call(
        kernel,
        grid=(4,),
        in_specs=[block, pl.BlockSpec(memory_space=pl.ANY)],
        out_specs=block,
        out_shape=jax.ShapeDtypeStruct(values.shape, values.dtype),
        compiler_params=params(1),
        cost_estimate=cost(1 << 16, 1 << 10),
        name="copy_after",
    )(values, token)


def cut(first, last, size):
    return [(base, min(size, last - base)) for base in range(first, last, size)]


def add(*terms):
    return sum(term.astype(F32) for term in terms)


def max_over_bus(values, groups):
    if groups & (groups - 1):
        return lax.pmax(values, "bus")
    step = 1
    while step < groups:
        pairs = [(i, i ^ step) for i in range(groups)]
        values = jnp.maximum(values, lax.ppermute(values, "bus", pairs))
        step *= 2
    return values


def body(site_values, site_bus, block_count, block_zone, ptdf_blocks, rating):
    here = lax.axis_index("bus")
    groups = lax.axis_size("bus")
    lines_size = lax.axis_size("line")
    scen_part, site_dev = site_values.shape
    bus_dev = NB // groups
    group_sites = groups * (site_dev // groups)
    zones_dev, slots_dev, line_zone, zone_width = ptdf_blocks.shape
    bus_zones = bus_dev // zone_width
    scen = scen_part * lines_size
    high = scen // groups

    got = lax.all_to_all(
        route(here, site_bus, site_values, groups, bus_dev), "bus", 0, 0, tiled=True
    )

    local = arrivals(here, site_bus, groups, site_dev, bus_dev).reshape(group_sites)
    keys = lax.sort(local * group_sites + jnp.arange(group_sites, dtype=jnp.int32))
    local = keys // group_sites
    edges = jnp.arange(bus_zones + 1, dtype=jnp.int32) * zone_width
    starts = jnp.sum((local[None, :] < edges[:, None]).astype(jnp.int32), axis=1)
    first = starts[:-1] // TILE
    span = WINDOW * TILE
    windows = (starts[1:] - first * TILE + span - 1) // span
    ids = local.reshape(group_sites // TILE, 1, TILE)
    count = block_count[:, 0]
    zone = block_zone.reshape(-1)
    last = last_live(count, slots_dev)
    sites = merge(keys % group_sites, got)

    def injections(row_blocks, pieces):
        return inject(
            first, windows, row_blocks.astype(jnp.int32), ids, pieces, bus_zones, zone_width
        )

    def partial(*call, **options):
        return partial_flow(count, zone, last, *call, **options)

    if groups == 8 and lines_size == 4 and scen_part == 2 * high:
        flows = staged(sites, injections, high, ptdf_blocks, partial)
    else:
        gathered = lax.all_gather(sites, "line", axis=0)
        inj = injections(jnp.arange(groups), [gathered[i] for i in range(lines_size)])
        (whole,) = partial(here.reshape(1), count, [inj], ptdf_blocks, 0, zones_dev, ((scen,),))
        flows = [lax.psum_scatter(whole, "bus", scatter_dimension=0, tiled=True).astype(F32)]

    loadings, worst, at = [], [], 0
    for flow in flows:
        loadings.append(flow / rating[None, at : at + flow.shape[1]])
        worst.append(jnp.max(jnp.abs(loadings[-1]), axis=0))
        at += flow.shape[1]
    worst = max_over_bus(jnp.concatenate(worst), groups)
    return jnp.concatenate(loadings, axis=1), worst


def staged(sites, injections, high, blocks, partial):
    me, here = lax.axis_index("line"), lax.axis_index("bus")
    side = me // 2
    near = here // 4 == side
    by_core = [(i, i ^ 1) for i in range(4)]
    by_y = [(i, i ^ 2) for i in range(4)]
    swap_x = [(i, i ^ 1) for i in range(8)]
    swap_z = [(i, i ^ 2) for i in range(8)]
    swap_far = [(i, i ^ 4) for i in range(8)]

    def to_side(half):
        pairs = []
        for line in range(4):
            goal = (line // 2) ^ half
            pairs += [(line * 8 + b, line * 8 + (b ^ 4)) for b in range(8) if b // 4 != goal]
        return pairs

    def half_injections(half, pieces):
        rows = []
        for q in (3, 1, 2, 0):
            owner = (side ^ half) * 4 + ((here & 3) ^ q)
            rows.append((((owner >> 1) ^ me) & 1) * 2 + (owner & 1))
        return injections(jnp.stack(rows), pieces)

    across = lax.ppermute(sites, "line", by_y)
    other = lax.ppermute(sites, "line", by_core)
    injs = [half_injections(0, [sites, other])]

    zones_dev = blocks.shape[0]
    early = min(EARLY, zones_dev)
    chunks = [((0,), 0, early)] + [((1,), *c) for c in cut(0, early, 2 * STEP)]
    slow = max(early, zones_dev - 2)
    chunks += [((0, 1), *c) for c in cut(early, slow, STEP) + cut(slow, zones_dev, 1)]
    total = len(chunks)
    token = injs[0]
    near_flag = near.astype(jnp.int32).reshape(1)
    splits = ((high, high), (high,), (high,))
    sent, kept, own, moved, late, flows = {}, {}, {}, {}, {}, {}
    for t in range(total + 6):
        stages = [
            (*kept.pop(t - 2), sent.pop(t - 2)) if t - 2 in sent else (),
            (own.pop(t - 4), moved.pop(t - 4)) if t - 4 in moved else (),
            (own.pop(t - 6), late.pop(t - 6)) if t - 6 in late else (),
        ]
        if t < total:
            halves, base, zones = chunks[t]
            if 1 in halves and len(injs) == 1:
                across = copy_after(across, token)
                injs.append(half_injections(1, [across, lax.ppermute(across, "line", by_core)]))
            send, give, keep, *done = partial(
                near_flag,
                token,
                [injs[h] for h in halves],
                blocks,
                base,
                zones,
                splits,
                stages=stages,
            )
            sent[t] = lax.ppermute(send, "bus", swap_x)
            kept[t] = (give, keep)
            token = keep
        else:
            done = sums(near_flag, stages, high)
        done = iter(done)
        if stages[0]:
            moved[t - 2] = lax.ppermute(next(done), "bus", swap_z)
            own[t - 2] = next(done)
        if stages[1]:
            halves = chunks[t - 4][0]
            if len(halves) == 1:
                late[t - 4] = lax.ppermute(next(done), ("line", "bus"), to_side(halves[0]))
            else:
                late[t - 4] = lax.ppermute(next(done), "bus", swap_far)
            own[t - 4] = next(done)
        if stages[2]:
            flows[t - 6] = next(done)
    first_flows = [
        jnp.concatenate([flows[t] for t in range(total) if chunks[t][0] == (half,)], axis=1)
        for half in range(2)
    ]
    flows = [flows[t] for t in range(total) if len(chunks[t][0]) == 2]
    return [jnp.where(near, *first_flows)] + flows


def solution(mesh):
    return jax.shard_map(
        body,
        mesh=mesh,
        in_specs=(
            P("line", "bus"),
            P(),
            P("line", "bus"),
            P("line", "bus"),
            P("line", "bus", None, None),
            P("line"),
        ),
        out_specs=(P("bus", "line"), P("line")),
        check_vma=False,
    )
```

time: 1140 us -> 267 us (0.23)
  waiting for transfers between devices: 585 us -> 93.6 us
  matrix products: 200 us -> 0 us
  local copies, waits for them, and re-layouts: 170 us -> 3.48 us
  loops' own time: 113 us -> 0 us
  Pallas kernels: 0 us -> 87.2 us
  starting transfers between devices: 0.3 us -> 69.3 us
  blocking collectives: 36.1 us -> 0 us
  between operations: 13.9 us -> 1.17 us
    reduce_scatter x1 -> x0, waiting for transfers between devices: 309 us -> none  [body(): lax.psum_scatter(every_bus.astype(jnp.bfloat16), 'bus', scatter_dimension...]
    unnamed x4 -> x0, waiting for transfers between devices: 212 us -> none
    dot_general x46 -> x0, matrix products: 200 us -> none  [the longest x8 135 us: one_group(): jnp.dot(vals, table, precision=lax.Precision.HIGHEST, preferred_element_t...]
    another operation x68 -> x0, loops' own time: 113 us -> none  [the longest x66 69 us: one_zone(): lax.cond(slot < live_count, lambda acc: acc + lax.dot_general(piece, bloc...]
    pallas_call x0 -> x23, Pallas kernels: none -> 87.2 us  [the longest x11 49.2 us: partial_flow(): pl.pallas_call(functools.partial(flow_kernel, base=base, slots=slots, hal...]
    ppermute x0 -> x39, waiting for transfers between devices: none -> 80 us  [the longest x11 21.3 us: staged(): moved[t - 2] = lax.ppermute(next(done), 'bus', swap_z)]
    all_gather x1 -> x0, waiting for transfers between devices: 64.4 us -> none  [body(): injection = lax.all_gather(partial_value, 'line', axis=0, tiled=True)]
    ppermute x0 -> x39, starting transfers between devices: none -> 62.1 us  [the longest x8 19.8 us: staged(): late[t - 4] = lax.ppermute(next(done), 'bus', swap_far)]
  transfers between devices with their start and end apart: 3 -> 40, of which waited for: 3 -> 20; matrix products, arithmetic and copies ran while one was open for 0% -> 3% of each run, Pallas kernels for 0% -> 26%
where the time goes in v2:
time: 267 us; the launch traced here: 262 us
  waiting for transfers between devices  93.6 us (35%)
  Pallas kernels  87.2 us (33%)
  starting transfers between devices  69.3 us (26%)
  other arithmetic  7.48 us (3%)
  local copies, waits for them, and re-layouts  3.48 us (1%)
    pallas_call x11, Pallas kernels, partial_flow(): pl.pallas_call(functools.partial(flow_kernel, base=base, slots=slots, hal...  49.2 us
    ppermute x11, waiting for transfers between devices, staged(): moved[t - 2] = lax.ppermute(next(done), 'bus', swap_z)  21.3 us
    ppermute x11, waiting for transfers between devices, staged(): sent[t] = lax.ppermute(send, 'bus', swap_x)  20.6 us
    ppermute x8, starting transfers between devices, staged(): late[t - 4] = lax.ppermute(next(done), 'bus', swap_far)  19.8 us
    ppermute x8, waiting for transfers between devices, staged(): late[t - 4] = lax.ppermute(next(done), 'bus', swap_far)  18.7 us
    pallas_call x2, Pallas kernels, inject(): pl.pallas_call(inject_kernel, grid_spec=pltpu.PrefetchScalarGridSpec(num_...  17 us
    ppermute x11, starting transfers between devices, staged(): moved[t - 2] = lax.ppermute(next(done), 'bus', swap_z)  15.3 us
    ppermute x11, starting transfers between devices, staged(): sent[t] = lax.ppermute(send, 'bus', swap_x)  14.6 us
  transfers between devices with their start and end apart: 40, of which 20 were waited for; matrix products, arithmetic and copies ran while one was open for 3% of the time, Pallas kernels for 26%

profile of v2, /device:TPU:0, one launch (start us, length us, event | category | flops | bytes accessed | tf_op | source)
XLA Modules:
  0.0 262.3 jit_solution(9128917481368722263)
XLA Ops:
  0.6 1.6 copy-done.2
  2.2 0.9 copy-done.3
  3.1 7.5 %route.1 = bf16[8,128,512]{2,1,0:T(8,128)(2,1)} custom-call(s32[1]{0:T(128)} %bitcast.2.here_ref, s32[256,128]{1,0:T(8,128)S(1)} %bitcast.32, f32[128,4096]{1,0:T(8,128)S(1)} %copy-done.2), custom_call_target="tpu_custom_call" | custom-call | flops 8589934592 | bytes 2097152 | tf_op jit(solution)/shard_map/route/pallas_call | solution.py:92
  10.7 7.3 %all-to-all-start = ((bf16[8,128,512]{2,1,0:T(8,128)(2,1)}), bf16[8,128,512]{2,1,0:T(8,128)(2,1)S(1)}, u32[]{:S(2)}, u32[]{:S(2)}) async-start(bf16[8,128,512]{2,1,0:T(8,128)(2,1)} %route.1), calls=%async_computation | async-start | bytes 2097152 | tf_op jit(solution)/shard_map/all_to_all | solution.py:473
  17.9 6.3 %arrivals.1 = s32[8,1,512]{2,1,0:T(1,128)S(1)} custom-call(s32[1]{0:T(128)} %bitcast.2.here_ref, s32[256,128]{1,0:T(8,128)S(1)} %bitcast.33), custom_call_target="tpu_custom_call" | custom-call | flops 1073741824 | bytes 131072 | tf_op jit(solution)/shard_map/arrivals/pallas_call | solution.py:145
  24.3 5.8 %sort.14 = (s32[4096]{0:T(1024)S(1)}, s32[4096]{0:T(1024)}) sort(s32[4096]{0:T(1024)S(1)} %iota_add_fusion, s32[4096]{0:T(1024)S(1)} %iota.20), dimensions={0}, to_apply=%region_1.2 | sort | flops 49152 | bytes 65536 | tf_op jit(solution)/shard_map/sort | solution.py:478
  30.1 13.6 %all-to-all-done.runs_ref = bf16[8,128,512]{2,1,0:T(8,128)(2,1)S(1)} async-done(((bf16[8,128,512]{2,1,0:T(8,128)(2,1)}), bf16[8,128,512]{2,1,0:T(8,128)(2,1)S(1)}, u32[]{:S(2)}, u32[]{:S(2)}) %all-to-all-start) | async-done | bytes 1048608 | tf_op jit(solution)/shard_map/all_to_all | solution.py:473
  43.7 6.5 %merge.1.refs_0_ = bf16[32,128,128]{2,1,0:T(8,128)(2,1)} custom-call(s32[8,1,512]{2,1,0:T(1,128)S(1)} %bitcast.31, bf16[8,128,512]{2,1,0:T(8,128)(2,1)S(1)} %all-to-all-done.runs_ref), custom_call_target="tpu_custom_call" | custom-call | flops 8589934592 | bytes 2097152 | tf_op jit(solution)/shard_map/merge/pallas_call | solution.py:176
  50.2 1.5 collective-permute-start.1
  53.0 8.5 %inject.2.token_ref.refs_0_.refs_1_.refs_2_ = bf16[14,256,640]{2,1,0:T(8,128)(2,1)S(1)} custom-call(s32[14]{0:T(128)S(1)} %get-tuple-element.178.first_ref, s32[14]{0:T(128)S(1)} %get-tuple-element.177.windows_ref, s32[4]{0:T(128)S(1)} %pad_add_fusion.rows_ref, s32[32,1,128]{2,1,0:T(1,128)S(1)} %bitcast.17, bf16[32,128,128]{2,1,0:T(8,128)(2,1)} %merge.1.refs_0_, ...), custom_call_target="tpu_custom_call" | custom-call | flops 65536 | bytes 1024 | tf_op jit(solution)/shard_map/inject/pallas_call | solution.py:233
  61.6 9.6 %partial_flow.11 = (bf16[128,4096]{1,0:T(8,128)(2,1)}, bf16[64,4096]{1,0:T(8,128)(2,1)S(1)}, bf16[64,4096]{1,0:T(8,128)(2,1)S(1)}) custom-call(s32[22]{0:T(128)S(1)} %bitcast.20, s32[66]{0:T(128)S(1)} %reshape.46.zone_ref, s32[66]{0:T(128)S(1)} %reshape.47.last_ref, s32[1]{0:T(128)} %bitcast.1.near_ref, ...), custom_call_target="tpu_custom_call" | custom-call | flops 2013265920 | bytes 11796480 | tf_op jit(solution)/shard_map/partial_flow/pallas_call | solution.py:384
  71.2 4.8 %collective-permute-done.1.values_ref = bf16[32,128,128]{2,1,0:T(8,128)(2,1)S(1)} collective-permute-done((bf16[32,128,128]{2,1,0:T(8,128)(2,1)}, bf16[32,128,128]{2,1,0:T(8,128)(2,1)S(1)}, u32[]{:S(2)}, u32[]{:S(2)}) %collective-permute-start.1) | collective-permute-done | bytes 1048608 | tf_op jit(solution)/shard_map/ppermute | solution.py:540
  76.2 1.5 collective-permute-start.3
  77.7 1.2 collective-permute-done.2.refs_1_
  78.9 8.5 %inject.3.refs_0_.refs_1_.refs_2_.refs_3_.refs_4_.refs_5_ = bf16[14,256,640]{2,1,0:T(8,128)(2,1)S(1)} custom-call(s32[14]{0:T(128)S(1)} %get-tuple-element.178.first_ref, s32[14]{0:T(128)S(1)} %get-tuple-element.177.windows_ref, s32[4]{0:T(128)S(1)} %pad_add_fusion.1.rows_ref, s32[32,1,128]{2,1,0:T(1,128)S(1)} %bitcast.18, ...), custom_call_target="tpu_custom_call" | custom-call | flops 65536 | bytes 1024 | tf_op jit(solution)/shard_map/inject/pallas_call | solution.py:233
  87.4 5.2 %partial_flow.12 = (bf16[128,2048]{1,0:T(8,128)(2,1)S(1)}, bf16[64,2048]{1,0:T(8,128)(2,1)S(1)}, bf16[64,2048]{1,0:T(8,128)(2,1)S(1)}) custom-call(s32[22]{0:T(128)S(1)} %bitcast.21, s32[66]{0:T(128)S(1)} %reshape.46.zone_ref, s32[66]{0:T(128)S(1)} %reshape.47.last_ref, s32[1]{0:T(128)} %bitcast.1.near_ref, ...), custom_call_target="tpu_custom_call" | custom-call | flops 1006632960 | bytes 5898240 | tf_op jit(solution)/shard_map/partial_flow/pallas_call | solution.py:384
  92.7 9.7 %collective-permute-done.3.refs_8_ = bf16[128,4096]{1,0:T(8,128)(2,1)S(1)} collective-permute-done((bf16[128,4096]{1,0:T(8,128)(2,1)}, bf16[128,4096]{1,0:T(8,128)(2,1)S(1)}, u32[]{:S(2)}, u32[]{:S(2)}) %collective-permute-start.3) | collective-permute-done | bytes 1048608 | tf_op jit(solution)/shard_map/ppermute | solution.py:575
  102.4 5.1 %partial_flow.13 = (bf16[128,2048]{1,0:T(8,128)(2,1)S(1)}, bf16[64,2048]{1,0:T(8,128)(2,1)S(1)}, bf16[64,2048]{1,0:T(8,128)(2,1)S(1)}, bf16[64,4096]{1,0:T(8,128)(2,1)S(1)}, bf16[64,4096]{1,0:T(8,128)(2,1)S(1)}) custom-call(s32[22]{0:T(128)S(1)} %bitcast.22, s32[66]{0:T(128)S(1)} %reshape.46.zone_ref, s32[66]{0:T(128)S(1)} %reshape.47.last_ref, ...), custom_call_target="tpu_custom_call" | custom-call | flops 1006632960 | bytes 5898240 | tf_op jit(solution)/shard_map/partial_flow/pallas_call | solution.py:384
  108.8 4.9 %collective-permute-done.4.refs_11_ = bf16[128,2048]{1,0:T(8,128)(2,1)S(1)} collective-permute-done((bf16[128,2048]{1,0:T(8,128)(2,1)S(1)}, bf16[128,2048]{1,0:T(8,128)(2,1)S(1)}, u32[]{:S(2)}, u32[]{:S(2)}) %collective-permute-start.4) | collective-permute-done | bytes 524320 | tf_op jit(solution)/shard_map/ppermute | solution.py:575
  113.6 4.6 %partial_flow.14 = (bf16[256,1024]{1,0:T(8,128)(2,1)S(1)}, bf16[128,1024]{1,0:T(8,128)(2,1)S(1)}, bf16[128,1024]{1,0:T(8,128)(2,1)S(1)}, bf16[64,2048]{1,0:T(8,128)(2,1)S(1)}, bf16[64,2048]{1,0:T(8,128)(2,1)S(1)}) custom-call(s32[22]{0:T(128)S(1)} %bitcast.23, s32[66]{0:T(128)S(1)} %reshape.46.zone_ref, s32[66]{0:T(128)S(1)} %reshape.47.last_ref, ...), custom_call_target="tpu_custom_call" | custom-call | flops 1006632960 | bytes 3932160 | tf_op jit(solution)/shard_map/partial_flow/pallas_call | solution.py:384
  118.8 6.1 %collective-permute-done.5.refs_11_ = bf16[128,2048]{1,0:T(8,128)(2,1)S(1)} collective-permute-done((bf16[128,2048]{1,0:T(8,128)(2,1)S(1)}, bf16[128,2048]{1,0:T(8,128)(2,1)S(1)}, u32[]{:S(2)}, u32[]{:S(2)}) %collective-permute-start.5) | collective-permute-done | bytes 524320 | tf_op jit(solution)/shard_map/ppermute | solution.py:575
  124.9 3.7 %partial_flow.15 = (bf16[256,1024]{1,0:T(8,128)(2,1)S(1)}, bf16[128,1024]{1,0:T(8,128)(2,1)S(1)}, bf16[128,1024]{1,0:T(8,128)(2,1)S(1)}, bf16[64,2048]{1,0:T(8,1...) custom-call(s32[22]{0:T(128)S(1)} %bitcast.24, ...), custom_call_target="tpu_custom_call" | custom-call | flops 1006632960 | bytes 3932160 | tf_op jit(solution)/shard_map/partial_flow/pallas_call | solution.py:384
  128.6 1.7 collective-permute-start.9
  130.4 1.3 collective-permute-start.11
  131.7 2.0 collective-permute-start.10
  133.8 7.2 %collective-permute-done.8.refs_13_ = bf16[64,2048]{1,0:T(8,128)(2,1)S(1)} collective-permute-done((bf16[64,2048]{1,0:T(8,128)(2,1)S(1)}, bf16[64,2048]{1,0:T(8,128)(2,1)S(1)}, u32[]{:S(2)}, u32[]{:S(2)}) %collective-permute-start.8) | collective-permute-done | bytes 262176 | tf_op jit(solution)/shard_map/ppermute | solution.py:582
  141.0 3.7 %partial_flow.16 = (bf16[256,1024]{1,0:T(8,128)(2,1)S(1)}, bf16[128,1024]{1,0:T(8,128)(2,1)S(1)}, bf16[128,1024]{1,0:T(8,128)(2,1)S(1)}, bf16[128,1024]{1,0:T(8,...) custom-call(s32[22]{0:T(128)S(1)} %bitcast.25, ...), custom_call_target="tpu_custom_call" | custom-call | flops 1006632960 | bytes 3932160 | tf_op jit(solution)/shard_map/partial_flow/pallas_call | solution.py:384
  144.7 1.6 collective-permute-start.12
  146.3 11.4 %collective-permute-done.10.refs_13_ = bf16[64,2048]{1,0:T(8,128)(2,1)S(1)} collective-permute-done((bf16[64,2048]{1,0:T(8,128)(2,1)S(1)}, bf16[64,2048]{1,0:T(8,128)(2,1)S(1)}, u32[]{:S(2)}, u32[]{:S(2)}) %collective-permute-start.10) | collective-permute-done | bytes 262176 | tf_op jit(solution)/shard_map/ppermute | solution.py:582
  157.7 3.7 %partial_flow.17 = (bf16[256,1024]{1,0:T(8,128)(2,1)S(1)}, bf16[128,1024]{1,0:T(8,128)(2,1)S(1)}, bf16[128,1024]{1,0:T(8,128)(2,1)S(1)}, bf16[128,1024]{1,0:T(8,...) custom-call(s32[22]{0:T(128)S(1)} %bitcast.26, ...), custom_call_target="tpu_custom_call" | custom-call | flops 1006632960 | bytes 3932160 | tf_op jit(solution)/shard_map/partial_flow/pallas_call | solution.py:384
  161.4 1.2 collective-permute-start.15
  162.6 3.2 %collective-permute-start.14 = (bf16[64,2048]{1,0:T(8,128)(2,1)S(1)}, bf16[64,2048]{1,0:T(8,128)(2,1)S(1)}, u32[]{:S(2)}, u32[]{:S(2)}) collective-permute-start(bf16[64,2048]{1,0:T(8,128)(2,1)S(1)} %get-tuple-element.122), channel_id=1, source_target_pairs={{0,4},{1,5},{2,6},{3,7},{8,12},{9,13},{10,14},{11,15},{20,16},{21,... | collective-permute-start | bytes 786440 | tf_op jit(solution)/shard_map/ppermute | solution.py:587
  165.7 2.5 collective-permute-start.16
  168.3 1.3 collective-permute-start.17
  170.2 2.3 collective-permute-done.14.refs_15_
  172.5 3.4 %partial_flow.18 = (bf16[256,1024]{1,0:T(8,128)(2,1)S(1)}, bf16[128,1024]{1,0:T(8,128)(2,1)S(1)}, bf16[128,1024]{1,0:T(8,128)(2,1)S(1)}, bf16[128,1024]{1,0:T(8,...) custom-call(s32[22]{0:T(128)S(1)} %bitcast.27, ...), custom_call_target="tpu_custom_call" | custom-call | flops 1006632960 | bytes 3932160 | tf_op jit(solution)/shard_map/partial_flow/pallas_call | solution.py:384
  175.9 3.1 %collective-permute-start.18 = (bf16[256,1024]{1,0:T(8,128)(2,1)S(1)}, bf16[256,1024]{1,0:T(8,128)(2,1)S(1)}, u32[]{:S(2)}, u32[]{:S(2)}) collective-permute-start(bf16[256,1024]{1,0:T(8,128)(2,1)S(1)} %get-tuple-element.134), channel_id=1, source_target_pairs={{0,1},{1,0},{2,3},{3,2},{4,5},{5,4},{6,7},{7,6},{8,9},{9,8},{10,11... | collective-permute-start | bytes 1572872 | tf_op jit(solution)/shard_map/ppermute | solution.py:575
  179.0 2.2 collective-permute-done.17.refs_15_
  181.2 3.6 %partial_flow.19 = (bf16[256,1024]{1,0:T(8,128)(2,1)S(1)}, bf16[128,1024]{1,0:T(8,128)(2,1)S(1)}, bf16[128,1024]{1,0:T(8,128)(2,1)S(1)}, bf16[128,1024]{1,0:T(8,...) custom-call(s32[22]{0:T(128)S(1)} %bitcast.28, ...), custom_call_target="tpu_custom_call" | custom-call | flops 1006632960 | bytes 3932160 | tf_op jit(solution)/shard_map/partial_flow/pallas_call | solution.py:384
  184.8 2.2 collective-permute-start.21
  187.0 6.9 %collective-permute-start.19 = (bf16[128,1024]{1,0:T(8,128)(2,1)S(1)}, bf16[128,1024]{1,0:T(8,128)(2,1)S(1)}, u32[]{:S(2)}, u32[]{:S(2)}) collective-permute-start(bf16[128,1024]{1,0:T(8,128)(2,1)S(1)} %get-tuple-element.136), channel_id=1, source_target_pairs={{0,2},{1,3},{2,0},{3,1},{4,6},{5,7},{6,4},{7,5},{8,10},{9,11},{10,... | collective-permute-start | bytes 786440 | tf_op jit(solution)/shard_map/ppermute | solution.py:582
  193.9 4.0 %collective-permute-start.20 = (bf16[64,1024]{1,0:T(8,128)(2,1)S(1)}, bf16[64,1024]{1,0:T(8,128)(2,1)S(1)}, u32[]{:S(2)}, u32[]{:S(2)}) collective-permute-start(bf16[64,1024]{1,0:T(8,128)(2,1)S(1)} %get-tuple-element.138), channel_id=1, source_target_pairs={{0,4},{1,5},{2,6},{3,7},{4,0},{5,1},{6,2},{7,3},{8,12},{9,13},{10,... | collective-permute-start | bytes 393224 | tf_op jit(solution)/shard_map/ppermute | solution.py:589
  198.0 4.6 %collective-permute-done.20.refs_15_ = bf16[64,1024]{1,0:T(8,128)(2,1)S(1)} collective-permute-done((bf16[64,1024]{1,0:T(8,128)(2,1)S(1)}, bf16[64,1024]{1,0:T(8,128)(2,1)S(1)}, u32[]{:S(2)}, u32[]{:S(2)}) %collective-permute-start.20) | collective-permute-done | bytes 131104 | tf_op jit(solution)/shard_map/ppermute | solution.py:589
  202.6 3.4 %collective-permute-start.23 = (bf16[64,1024]{1,0:T(8,128)(2,1)S(1)}, bf16[64,1024]{1,0:T(8,128)(2,1)S(1)}, u32[]{:S(2)}, u32[]{:S(2)}) collective-permute-start(bf16[64,1024]{1,0:T(8,128)(2,1)S(1)} %get-tuple-element.146), channel_id=1, source_target_pairs={{0,4},{1,5},{2,6},{3,7},{4,0},{5,1},{6,2},{7,3},{8,12},{9,13},{10,... | collective-permute-start | bytes 393224 | tf_op jit(solution)/shard_map/ppermute | solution.py:589
  206.0 2.9 %partial_flow.20 = (bf16[256,512]{1,0:T(8,128)(2,1)S(1)}, bf16[128,512]{1,0:T(8,128)(2,1)S(1)}, bf16[128,512]{1,0:T(8,128)(2,1)S(1)}, bf16[128,1024]{1,0:T(8,128...) custom-call(s32[22]{0:T(128)S(1)} %bitcast.29, ...), custom_call_target="tpu_custom_call" | custom-call | flops 503316480 | bytes 1966080 | tf_op jit(solution)/shard_map/partial_flow/pallas_call | solution.py:384
  209.0 3.7 %partial_flow.21 = (bf16[256,512]{1,0:T(8,128)(2,1)S(1)}, bf16[128,512]{1,0:T(8,128)(2,1)S(1)}, bf16[128,512]{1,0:T(8,128)(2,1)S(1)}, bf16[128,1024]{1,0:T(8,128...) custom-call(s32[22]{0:T(128)S(1)} %bitcast.30, ...), custom_call_target="tpu_custom_call" | custom-call | flops 503316480 | bytes 1966080 | tf_op jit(solution)/shard_map/partial_flow/pallas_call | solution.py:384
  212.8 3.2 %collective-permute-start.28 = (bf16[128,1024]{1,0:T(8,128)(2,1)S(1)}, bf16[128,1024]{1,0:T(8,128)(2,1)S(1)}, u32[]{:S(2)}, u32[]{:S(2)}) collective-permute-start(bf16[128,1024]{1,0:T(8,128)(2,1)S(1)} %get-tuple-element.159), channel_id=1, source_target_pairs={{0,2},{1,3},{2,0},{3,1},{4,6},{5,7},{6,4},{7,5},{8,10},{9,11},{10,... | collective-permute-start | bytes 786440 | tf_op jit(solution)/shard_map/ppermute | solution.py:582
  216.0 2.4 collective-permute-start.29
  218.4 1.9 collective-permute-start.24
  220.5 5.0 %collective-permute-done.29.refs_6_ = bf16[64,1024]{1,0:T(8,128)(2,1)S(1)} collective-permute-done((bf16[64,1024]{1,0:T(8,128)(2,1)S(1)}, bf16[64,1024]{1,0:T(8,128)(2,1)S(1)}, u32[]{:S(2)}, u32[]{:S(2)}) %collective-permute-start.29) | collective-permute-done | bytes 131104 | tf_op jit(solution)/shard_map/ppermute | solution.py:589
  225.5 3.4 %collective-permute-start.26 = (bf16[64,1024]{1,0:T(8,128)(2,1)S(1)}, bf16[64,1024]{1,0:T(8,128)(2,1)S(1)}, u32[]{:S(2)}, u32[]{:S(2)}) collective-permute-start(bf16[64,1024]{1,0:T(8,128)(2,1)S(1)} %get-tuple-element.153), channel_id=1, source_target_pairs={{0,4},{1,5},{2,6},{3,7},{4,0},{5,1},{6,2},{7,3},{8,12},{9,13},{10,... | collective-permute-start | bytes 393224 | tf_op jit(solution)/shard_map/ppermute | solution.py:589
  229.1 3.0 %collective-permute-start.33 = (bf16[64,1024]{1,0:T(8,128)(2,1)S(1)}, bf16[64,1024]{1,0:T(8,128)(2,1)S(1)}, u32[]{:S(2)}, u32[]{:S(2)}) collective-permute-start(bf16[64,1024]{1,0:T(8,128)(2,1)S(1)} %get-tuple-element.171), channel_id=1, source_target_pairs={{0,4},{1,5},{2,6},{3,7},{4,0},{5,1},{6,2},{7,3},{8,12},{9,13},{10,... | collective-permute-start | bytes 393224 | tf_op jit(solution)/shard_map/ppermute | solution.py:589
  232.1 3.8 %collective-permute-done.26.refs_6_ = bf16[64,1024]{1,0:T(8,128)(2,1)S(1)} collective-permute-done((bf16[64,1024]{1,0:T(8,128)(2,1)S(1)}, bf16[64,1024]{1,0:T(8,128)(2,1)S(1)}, u32[]{:S(2)}, u32[]{:S(2)}) %collective-permute-start.26) | collective-permute-done | bytes 131104 | tf_op jit(solution)/shard_map/ppermute | solution.py:589
  236.2 2.0 collective-permute-start.31
  238.3 1.6 collective-permute-done.33.refs_3_
  240.1 2.6 %collective-permute-done.30.refs_1_ = bf16[128,512]{1,0:T(8,128)(2,1)S(1)} collective-permute-done((bf16[128,512]{1,0:T(8,128)(2,1)S(1)}, bf16[128,512]{1,0:T(8,128)(2,1)S(1)}, u32[]{:S(2)}, u32[]{:S(2)}) %collective-permute-start.30) | collective-permute-done | bytes 131104 | tf_op jit(solution)/shard_map/ppermute | solution.py:582
  242.8 1.4 collective-permute-start.34
  244.4 3.7 %collective-permute-done.34.refs_1_ = bf16[64,512]{1,0:T(8,128)(2,1)S(1)} collective-permute-done((bf16[64,512]{1,0:T(8,128)(2,1)S(1)}, bf16[64,512]{1,0:T(8,128)(2,1)S(1)}, u32[]{:S(2)}, u32[]{:S(2)}) %collective-permute-start.34) | collective-permute-done | bytes 65568 | tf_op jit(solution)/shard_map/ppermute | solution.py:589
  248.2 2.3 collective-permute-start.36
  250.5 2.0 collective-permute-done.36
  252.5 1.5 collective-permute-start.37
  254.0 2.6 %collective-permute-done.37 = f32[11264]{0:T(1024)S(1)} collective-permute-done((f32[11264]{0:T(1024)S(1)}, f32[11264]{0:T(1024)S(1)}, u32[]{:S(2)}, u32[]{:S(2)}) %collective-permute-start.37) | collective-permute-done | bytes 45088 | tf_op jit(solution)/shard_map/ppermute | solution.py:456
  256.6 1.2 collective-permute-start.38
  257.9 3.8 %collective-permute-done.38 = f32[11264]{0:T(1024)S(1)} collective-permute-done((f32[11264]{0:T(1024)S(1)}, f32[11264]{0:T(1024)S(1)}, u32[]{:S(2)}, u32[]{:S(2)}) %collective-permute-start.38) | collective-permute-done | bytes 45088 | tf_op jit(solution)/shard_map/ppermute | solution.py:456
  (112 shorter events, 6.2 us)
Async XLA Ops:
  0.6 1.6 copy-start.2
  2.2 0.9 copy-start.3
  3.1 14.8 %copy-start.4 = (s32[32768]{0:T(1024)S(1)}, s32[32768]{0:T(1024)}, u32[]{:S(2)}) copy-start(s32[32768]{0:T(1024)} %param.7) | copy-start | bytes 393220
  10.7 33.0 %all-to-all-start = ((bf16[8,128,512]{2,1,0:T(8,128)(2,1)}), bf16[8,128,512]{2,1,0:T(8,128)(2,1)S(1)}, u32[]{:S(2)}, u32[]{:S(2)}) async-start(bf16[8,128,512]{2,1,0:T(8,128)(2,1)} %route.1), calls=%async_computation | async-start | bytes 2097152 | tf_op jit(solution)/shard_map/all_to_all | solution.py:473
  43.7 8.0 %copy-start.13 = (s32[22,3]{0,1:T(4,128)S(1)}, s32[22,3]{0,1:T(4,128)}, u32[]{:S(2)}) copy-start(s32[22,3]{0,1:T(4,128)} %param.9) | copy-start | bytes 796
  43.7 8.2 %copy-start.1 = (s32[22,1]{0,1:T(1,128)S(1)}, s32[22,1]{0,1:T(1,128)}, u32[]{:S(2)}) copy-start(s32[22,1]{0,1:T(1,128)} %param.8) | copy-start | bytes 268
  50.2 2.9 %collective-permute-start = (bf16[32,128,128]{2,1,0:T(8,128)(2,1)}, bf16[32,128,128]{2,1,0:T(8,128)(2,1)S(1)}, u32[]{:S(2)}, u32[]{:S(2)}) collective-permute-start(bf16[32,128,128]{2,1,0:T(8,128)(2,1)} %merge.1.refs_0_), channel_id=1, source_target_pairs={{0,8},{8,0},{16,24},{24,16},{1,9},{9,1},{17,25},{25,17},{2,10},{10... | collective-permute-start | bytes 3145736 | tf_op jit(solution)/shard_map/ppermute | solution.py:541
  50.2 25.8 %collective-permute-start.1 = (bf16[32,128,128]{2,1,0:T(8,128)(2,1)}, bf16[32,128,128]{2,1,0:T(8,128)(2,1)S(1)}, u32[]{:S(2)}, u32[]{:S(2)}) collective-permute-start(bf16[32,128,128]{2,1,0:T(8,128)(2,1)} %merge.1.refs_0_), channel_id=1, source_target_pairs={{0,16},{8,24},{16,0},{24,8},{1,17},{9,25},{17,1},{25,9},{2,18},{10... | collective-permute-start | bytes 3145736 | tf_op jit(solution)/shard_map/ppermute | solution.py:540
  61.5 9.6 %copy-start = (bf16[14,256,640]{2,1,0:T(8,128)(2,1)}, bf16[14,256,640]{2,1,0:T(8,128)(2,1)S(1)}, u32[]{:S(2)}) copy-start(bf16[14,256,640]{2,1,0:T(8,128)(2,1)S(1)} %inject.2.token_ref.refs_0_.refs_1_.refs_2_) | copy-start | bytes 13762564
  76.1 2.9 %collective-permute-start.2 = (bf16[32,128,128]{2,1,0:T(8,128)(2,1)S(1)}, bf16[32,128,128]{2,1,0:T(8,128)(2,1)}, u32[]{:S(2)}, u32[]{:S(2)}) collective-permute-start(bf16[32,128,128]{2,1,0:T(8,128)(2,1)S(1)} %copy_after.1.refs_0_), channel_id=1, source_target_pairs={{0,8},{8,0},{16,24},{24,16},{1,9},{9,1},{17,25},{25,17},{2,10},{10... | collective-permute-start | bytes 3145736 | tf_op jit(solution)/shard_map/ppermute | solution.py:564
  76.2 26.2 %collective-permute-start.3 = (bf16[128,4096]{1,0:T(8,128)(2,1)}, bf16[128,4096]{1,0:T(8,128)(2,1)S(1)}, u32[]{:S(2)}, u32[]{:S(2)}) collective-permute-start(bf16[128,4096]{1,0:T(8,128)(2,1)} %get-tuple-element.94), channel_id=1, source_target_pairs={{0,1},{1,0},{2,3},{3,2},{4,5},{5,4},{6,7},{7,6},{8,9},{9,8},{10,11... | collective-permute-start | bytes 3145736 | tf_op jit(solution)/shard_map/ppermute | solution.py:575
  92.7 21.0 %collective-permute-start.4 = (bf16[128,2048]{1,0:T(8,128)(2,1)S(1)}, bf16[128,2048]{1,0:T(8,128)(2,1)S(1)}, u32[]{:S(2)}, u32[]{:S(2)}) collective-permute-start(bf16[128,2048]{1,0:T(8,128)(2,1)S(1)} %get-tuple-element.97), channel_id=1, source_target_pairs={{0,1},{1,0},{2,3},{3,2},{4,5},{5,4},{6,7},{7,6},{8,9},{9,8},{10,11... | collective-permute-start | bytes 1572872 | tf_op jit(solution)/shard_map/ppermute | solution.py:575
  102.4 11.2 %slice-start = ((s8[4587520]{0:T(1024)(128)(4,1)}), s8[4194304]{0:T(1024)(128)(4,1)S(1)}, s32[]{:S(2)}) async-start(s8[4587520]{0:T(1024)(128)(4,1)} %bitcast.15), calls=%async_computation.1 | async-start | bytes 8388608
  102.4 11.2 %slice-start.1 = ((s8[4587520]{0:T(1024)(128)(4,1)}), s8[393216]{0:T(1024)(128)(4,1)S(1)}, s32[]{:S(2)}) async-start(s8[4587520]{0:T(1024)(128)(4,1)} %bitcast.15), calls=%async_computation.2 | async-start | bytes 786432
  107.5 17.3 %collective-permute-start.5 = (bf16[128,2048]{1,0:T(8,128)(2,1)S(1)}, bf16[128,2048]{1,0:T(8,128)(2,1)S(1)}, u32[]{:S(2)}, u32[]{:S(2)}) collective-permute-start(bf16[128,2048]{1,0:T(8,128)(2,1)S(1)} %get-tuple-element.100), channel_id=1, source_target_pairs={{0,1},{1,0},{2,3},{3,2},{4,5},{5,4},{6,7},{7,6},{8,9},{9,8},{10,11... | collective-permute-start | bytes 1572872 | tf_op jit(solution)/shard_map/ppermute | solution.py:575
  108.3 16.6 %collective-permute-start.6 = (bf16[64,4096]{1,0:T(8,128)(2,1)S(1)}, bf16[64,4096]{1,0:T(8,128)(2,1)S(1)}, u32[]{:S(2)}, u32[]{:S(2)}) collective-permute-start(bf16[64,4096]{1,0:T(8,128)(2,1)S(1)} %get-tuple-element.102), channel_id=1, source_target_pairs={{0,2},{1,3},{2,0},{3,1},{4,6},{5,7},{6,4},{7,5},{8,10},{9,11},{10,... | collective-permute-start | bytes 1572872 | tf_op jit(solution)/shard_map/ppermute | solution.py:582
  118.3 22.7 %collective-permute-start.7 = (bf16[256,1024]{1,0:T(8,128)(2,1)S(1)}, bf16[256,1024]{1,0:T(8,128)(2,1)S(1)}, u32[]{:S(2)}, u32[]{:S(2)}) collective-permute-start(bf16[256,1024]{1,0:T(8,128)(2,1)S(1)} %get-tuple-element.105), channel_id=1, source_target_pairs={{0,1},{1,0},{2,3},{3,2},{4,5},{5,4},{6,7},{7,6},{8,9},{9,8},{10,11... | collective-permute-start | bytes 1572872 | tf_op jit(solution)/shard_map/ppermute | solution.py:575
  128.6 29.1 %collective-permute-start.9 = (bf16[256,1024]{1,0:T(8,128)(2,1)S(1)}, bf16[256,1024]{1,0:T(8,128)(2,1)S(1)}, u32[]{:S(2)}, u32[]{:S(2)}) collective-permute-start(bf16[256,1024]{1,0:T(8,128)(2,1)S(1)} %get-tuple-element.110), channel_id=1, source_target_pairs={{0,1},{1,0},{2,3},{3,2},{4,5},{5,4},{6,7},{7,6},{8,9},{9,8},{10,11... | collective-permute-start | bytes 1572872 | tf_op jit(solution)/shard_map/ppermute | solution.py:575
  130.4 27.4 %collective-permute-start.11 = (bf16[64,4096]{1,0:T(8,128)(2,1)S(1)}, bf16[64,4096]{1,0:T(8,128)(2,1)S(1)}, u32[]{:S(2)}, u32[]{:S(2)}) collective-permute-start(bf16[64,4096]{1,0:T(8,128)(2,1)S(1)} %get-tuple-element.114), channel_id=1, source_target_pairs={{4,0},{5,1},{6,2},{7,3},{12,8},{13,9},{14,10},{15,11},{16,20},{17,... | collective-permute-start | bytes 1572872 | tf_op jit(solution)/shard_map/ppermute | solution.py:587
  131.6 9.3 %collective-permute-start.8 = (bf16[64,2048]{1,0:T(8,128)(2,1)S(1)}, bf16[64,2048]{1,0:T(8,128)(2,1)S(1)}, u32[]{:S(2)}, u32[]{:S(2)}) collective-permute-start(bf16[64,2048]{1,0:T(8,128)(2,1)S(1)} %get-tuple-element.107), channel_id=1, source_target_pairs={{0,2},{1,3},{2,0},{3,1},{4,6},{5,7},{6,4},{7,5},{8,10},{9,11},{10,... | collective-permute-start | bytes 786440 | tf_op jit(solution)/shard_map/ppermute | solution.py:582
  131.7 26.0 %collective-permute-start.10 = (bf16[64,2048]{1,0:T(8,128)(2,1)S(1)}, bf16[64,2048]{1,0:T(8,128)(2,1)S(1)}, u32[]{:S(2)}, u32[]{:S(2)}) collective-permute-start(bf16[64,2048]{1,0:T(8,128)(2,1)S(1)} %get-tuple-element.112), channel_id=1, source_target_pairs={{0,2},{1,3},{2,0},{3,1},{4,6},{5,7},{6,4},{7,5},{8,10},{9,11},{10,... | collective-permute-start | bytes 786440 | tf_op jit(solution)/shard_map/ppermute | solution.py:582
  144.7 27.8 %collective-permute-start.12 = (bf16[256,1024]{1,0:T(8,128)(2,1)S(1)}, bf16[256,1024]{1,0:T(8,128)(2,1)S(1)}, u32[]{:S(2)}, u32[]{:S(2)}) collective-permute-start(bf16[256,1024]{1,0:T(8,128)(2,1)S(1)} %get-tuple-element.118), channel_id=1, source_target_pairs={{0,1},{1,0},{2,3},{3,2},{4,5},{5,4},{6,7},{7,6},{8,9},{9,8},{10,11... | collective-permute-start | bytes 1572872 | tf_op jit(solution)/shard_map/ppermute | solution.py:575
  146.3 22.0 %collective-permute-start.13 = (bf16[128,1024]{1,0:T(8,128)(2,1)S(1)}, bf16[128,1024]{1,0:T(8,128)(2,1)S(1)}, u32[]{:S(2)}, u32[]{:S(2)}) collective-permute-start(bf16[128,1024]{1,0:T(8,128)(2,1)S(1)} %get-tuple-element.120), channel_id=1, source_target_pairs={{0,2},{1,3},{2,0},{3,1},{4,6},{5,7},{6,4},{7,5},{8,10},{9,11},{10,... | collective-permute-start | bytes 786440 | tf_op jit(solution)/shard_map/ppermute | solution.py:582
  157.7 11.9 %copy-start.6 = (f32[11264]{0:T(1024)S(1)}, f32[11264]{0:T(1024)}, u32[]{:S(2)}) copy-start(f32[11264]{0:T(1024)} %param.11) | copy-start | bytes 135172
  161.4 19.8 %collective-permute-start.15 = (bf16[256,1024]{1,0:T(8,128)(2,1)S(1)}, bf16[256,1024]{1,0:T(8,128)(2,1)S(1)}, u32[]{:S(2)}, u32[]{:S(2)}) collective-permute-start(bf16[256,1024]{1,0:T(8,128)(2,1)S(1)} %get-tuple-element.126), channel_id=1, source_target_pairs={{0,1},{1,0},{2,3},{3,2},{4,5},{5,4},{6,7},{7,6},{8,9},{9,8},{10,11... | collective-permute-start | bytes 1572872 | tf_op jit(solution)/shard_map/ppermute | solution.py:575
  162.6 9.9 %collective-permute-start.14 = (bf16[64,2048]{1,0:T(8,128)(2,1)S(1)}, bf16[64,2048]{1,0:T(8,128)(2,1)S(1)}, u32[]{:S(2)}, u32[]{:S(2)}) collective-permute-start(bf16[64,2048]{1,0:T(8,128)(2,1)S(1)} %get-tuple-element.122), channel_id=1, source_target_pairs={{0,4},{1,5},{2,6},{3,7},{8,12},{9,13},{10,14},{11,15},{20,16},{21,... | collective-permute-start | bytes 786440 | tf_op jit(solution)/shard_map/ppermute | solution.py:587
  165.7 13.2 %collective-permute-start.16 = (bf16[128,1024]{1,0:T(8,128)(2,1)S(1)}, bf16[128,1024]{1,0:T(8,128)(2,1)S(1)}, u32[]{:S(2)}, u32[]{:S(2)}) collective-permute-start(bf16[128,1024]{1,0:T(8,128)(2,1)S(1)} %get-tuple-element.128), channel_id=1, source_target_pairs={{0,2},{1,3},{2,0},{3,1},{4,6},{5,7},{6,4},{7,5},{8,10},{9,11},{10,... | collective-permute-start | bytes 786440 | tf_op jit(solution)/shard_map/ppermute | solution.py:582
  168.3 12.9 %collective-permute-start.17 = (bf16[64,2048]{1,0:T(8,128)(2,1)S(1)}, bf16[64,2048]{1,0:T(8,128)(2,1)S(1)}, u32[]{:S(2)}, u32[]{:S(2)}) collective-permute-start(bf16[64,2048]{1,0:T(8,128)(2,1)S(1)} %get-tuple-element.130), channel_id=1, source_target_pairs={{0,4},{1,5},{2,6},{3,7},{8,12},{9,13},{10,14},{11,15},{20,16},{21,... | collective-permute-start | bytes 786440 | tf_op jit(solution)/shard_map/ppermute | solution.py:587
  175.9 30.1 %collective-permute-start.18 = (bf16[256,1024]{1,0:T(8,128)(2,1)S(1)}, bf16[256,1024]{1,0:T(8,128)(2,1)S(1)}, u32[]{:S(2)}, u32[]{:S(2)}) collective-permute-start(bf16[256,1024]{1,0:T(8,128)(2,1)S(1)} %get-tuple-element.134), channel_id=1, source_target_pairs={{0,1},{1,0},{2,3},{3,2},{4,5},{5,4},{6,7},{7,6},{8,9},{9,8},{10,11... | collective-permute-start | bytes 1572872 | tf_op jit(solution)/shard_map/ppermute | solution.py:575
  181.2 16.7 %slice-start.2 = ((f32[11264]{0:T(1024)}), f32[4096]{0:T(1024)S(1)}, s32[]{:S(2)}) async-start(f32[11264]{0:T(1024)} %param.11), calls=%async_computation.3 | async-start | bytes 32768 | tf_op jit(solution)/shard_map/slice | solution.py:509
  184.8 24.2 %collective-permute-start.21 = (bf16[256,1024]{1,0:T(8,128)(2,1)S(1)}, bf16[256,1024]{1,0:T(8,128)(2,1)S(1)}, u32[]{:S(2)}, u32[]{:S(2)}) collective-permute-start(bf16[256,1024]{1,0:T(8,128)(2,1)S(1)} %get-tuple-element.142), channel_id=1, source_target_pairs={{0,1},{1,0},{2,3},{3,2},{4,5},{5,4},{6,7},{7,6},{8,9},{9,8},{10,11... | collective-permute-start | bytes 1572872 | tf_op jit(solution)/shard_map/ppermute | solution.py:575
  187.0 19.0 %collective-permute-start.19 = (bf16[128,1024]{1,0:T(8,128)(2,1)S(1)}, bf16[128,1024]{1,0:T(8,128)(2,1)S(1)}, u32[]{:S(2)}, u32[]{:S(2)}) collective-permute-start(bf16[128,1024]{1,0:T(8,128)(2,1)S(1)} %get-tuple-element.136), channel_id=1, source_target_pairs={{0,2},{1,3},{2,0},{3,1},{4,6},{5,7},{6,4},{7,5},{8,10},{9,11},{10,... | collective-permute-start | bytes 786440 | tf_op jit(solution)/shard_map/ppermute | solution.py:582
  193.9 8.7 %collective-permute-start.20 = (bf16[64,1024]{1,0:T(8,128)(2,1)S(1)}, bf16[64,1024]{1,0:T(8,128)(2,1)S(1)}, u32[]{:S(2)}, u32[]{:S(2)}) collective-permute-start(bf16[64,1024]{1,0:T(8,128)(2,1)S(1)} %get-tuple-element.138), channel_id=1, source_target_pairs={{0,4},{1,5},{2,6},{3,7},{4,0},{5,1},{6,2},{7,3},{8,12},{9,13},{10,... | collective-permute-start | bytes 393224 | tf_op jit(solution)/shard_map/ppermute | solution.py:589
  197.9 11.1 %collective-permute-start.22 = (bf16[128,1024]{1,0:T(8,128)(2,1)S(1)}, bf16[128,1024]{1,0:T(8,128)(2,1)S(1)}, u32[]{:S(2)}, u32[]{:S(2)}) collective-permute-start(bf16[128,1024]{1,0:T(8,128)(2,1)S(1)} %get-tuple-element.144), channel_id=1, source_target_pairs={{0,2},{1,3},{2,0},{3,1},{4,6},{5,7},{6,4},{7,5},{8,10},{9,11},{10,... | collective-permute-start | bytes 786440 | tf_op jit(solution)/shard_map/ppermute | solution.py:582
  202.6 6.4 %collective-permute-start.23 = (bf16[64,1024]{1,0:T(8,128)(2,1)S(1)}, bf16[64,1024]{1,0:T(8,128)(2,1)S(1)}, u32[]{:S(2)}, u32[]{:S(2)}) collective-permute-start(bf16[64,1024]{1,0:T(8,128)(2,1)S(1)} %get-tuple-element.146), channel_id=1, source_target_pairs={{0,4},{1,5},{2,6},{3,7},{4,0},{5,1},{6,2},{7,3},{8,12},{9,13},{10,... | collective-permute-start | bytes 393224 | tf_op jit(solution)/shard_map/ppermute | solution.py:589
  209.0 11.4 %copy-start.12 = (f32[1024]{0:T(1024)S(1)}, f32[1024]{0:T(1024)}, u32[]{:S(2)}) copy-start(f32[1024]{0:T(1024)} %get-tuple-element.204) | copy-start | bytes 12292
  209.0 11.4 %copy-start.11 = (f32[1024]{0:T(1024)S(1)}, f32[1024]{0:T(1024)}, u32[]{:S(2)}) copy-start(f32[1024]{0:T(1024)} %get-tuple-element.203) | copy-start | bytes 12292
  212.7 25.5 %copy-start.10 = (f32[1024]{0:T(1024)S(1)}, f32[1024]{0:T(1024)}, u32[]{:S(2)}) copy-start(f32[1024]{0:T(1024)} %get-tuple-element.202) | copy-start | bytes 12292
  212.7 25.5 %copy-start.9 = (f32[1024]{0:T(1024)S(1)}, f32[1024]{0:T(1024)}, u32[]{:S(2)}) copy-start(f32[1024]{0:T(1024)} %get-tuple-element.201) | copy-start | bytes 12292
  212.7 16.1 %collective-permute-start.27 = (bf16[256,512]{1,0:T(8,128)(2,1)S(1)}, bf16[256,512]{1,0:T(8,128)(2,1)S(1)}, u32[]{:S(2)}, u32[]{:S(2)}) collective-permute-start(bf16[256,512]{1,0:T(8,128)(2,1)S(1)} %get-tuple-element.157), channel_id=1, source_target_pairs={{0,1},{1,0},{2,3},{3,2},{4,5},{5,4},{6,7},{7,6},{8,9},{9,8},{10,11... | collective-permute-start | bytes 786440 | tf_op jit(solution)/shard_map/ppermute | solution.py:575
  212.8 16.1 %collective-permute-start.28 = (bf16[128,1024]{1,0:T(8,128)(2,1)S(1)}, bf16[128,1024]{1,0:T(8,128)(2,1)S(1)}, u32[]{:S(2)}, u32[]{:S(2)}) collective-permute-start(bf16[128,1024]{1,0:T(8,128)(2,1)S(1)} %get-tuple-element.159), channel_id=1, source_target_pairs={{0,2},{1,3},{2,0},{3,1},{4,6},{5,7},{6,4},{7,5},{8,10},{9,11},{10,... | collective-permute-start | bytes 786440 | tf_op jit(solution)/shard_map/ppermute | solution.py:582
  216.0 9.5 %collective-permute-start.29 = (bf16[64,1024]{1,0:T(8,128)(2,1)S(1)}, bf16[64,1024]{1,0:T(8,128)(2,1)S(1)}, u32[]{:S(2)}, u32[]{:S(2)}) collective-permute-start(bf16[64,1024]{1,0:T(8,128)(2,1)S(1)} %get-tuple-element.161), channel_id=1, source_target_pairs={{0,4},{1,5},{2,6},{3,7},{4,0},{5,1},{6,2},{7,3},{8,12},{9,13},{10,... | collective-permute-start | bytes 393224 | tf_op jit(solution)/shard_map/ppermute | solution.py:589
  218.4 17.6 %collective-permute-start.24 = (bf16[256,512]{1,0:T(8,128)(2,1)S(1)}, bf16[256,512]{1,0:T(8,128)(2,1)S(1)}, u32[]{:S(2)}, u32[]{:S(2)}) collective-permute-start(bf16[256,512]{1,0:T(8,128)(2,1)S(1)} %get-tuple-element.149), channel_id=1, source_target_pairs={{0,1},{1,0},{2,3},{3,2},{4,5},{5,4},{6,7},{7,6},{8,9},{9,8},{10,11... | collective-permute-start | bytes 786440 | tf_op jit(solution)/shard_map/ppermute | solution.py:575
  220.3 15.6 %collective-permute-start.25 = (bf16[128,1024]{1,0:T(8,128)(2,1)S(1)}, bf16[128,1024]{1,0:T(8,128)(2,1)S(1)}, u32[]{:S(2)}, u32[]{:S(2)}) collective-permute-start(bf16[128,1024]{1,0:T(8,128)(2,1)S(1)} %get-tuple-element.151), channel_id=1, source_target_pairs={{0,2},{1,3},{2,0},{3,1},{4,6},{5,7},{6,4},{7,5},{8,10},{9,11},{10,... | collective-permute-start | bytes 786440 | tf_op jit(solution)/shard_map/ppermute | solution.py:582
  220.3 23.9 %copy-start.8 = (f32[1024]{0:T(1024)S(1)}, f32[1024]{0:T(1024)}, u32[]{:S(2)}) copy-start(f32[1024]{0:T(1024)} %get-tuple-element.200) | copy-start | bytes 12292
  220.4 23.9 %copy-start.7 = (f32[1024]{0:T(1024)S(1)}, f32[1024]{0:T(1024)}, u32[]{:S(2)}) copy-start(f32[1024]{0:T(1024)} %get-tuple-element.199) | copy-start | bytes 12292
  225.5 10.5 %collective-permute-start.26 = (bf16[64,1024]{1,0:T(8,128)(2,1)S(1)}, bf16[64,1024]{1,0:T(8,128)(2,1)S(1)}, u32[]{:S(2)}, u32[]{:S(2)}) collective-permute-start(bf16[64,1024]{1,0:T(8,128)(2,1)S(1)} %get-tuple-element.153), channel_id=1, source_target_pairs={{0,4},{1,5},{2,6},{3,7},{4,0},{5,1},{6,2},{7,3},{8,12},{9,13},{10,... | collective-permute-start | bytes 393224 | tf_op jit(solution)/shard_map/ppermute | solution.py:589
  229.0 9.3 %collective-permute-start.32 = (bf16[128,512]{1,0:T(8,128)(2,1)S(1)}, bf16[128,512]{1,0:T(8,128)(2,1)S(1)}, u32[]{:S(2)}, u32[]{:S(2)}) collective-permute-start(bf16[128,512]{1,0:T(8,128)(2,1)S(1)} %get-tuple-element.169), channel_id=1, source_target_pairs={{0,2},{1,3},{2,0},{3,1},{4,6},{5,7},{6,4},{7,5},{8,10},{9,11},{10,... | collective-permute-start | bytes 393224 | tf_op jit(solution)/shard_map/ppermute | solution.py:582
  229.1 10.8 %collective-permute-start.33 = (bf16[64,1024]{1,0:T(8,128)(2,1)S(1)}, bf16[64,1024]{1,0:T(8,128)(2,1)S(1)}, u32[]{:S(2)}, u32[]{:S(2)}) collective-permute-start(bf16[64,1024]{1,0:T(8,128)(2,1)S(1)} %get-tuple-element.171), channel_id=1, source_target_pairs={{0,4},{1,5},{2,6},{3,7},{4,0},{5,1},{6,2},{7,3},{8,12},{9,13},{10,... | collective-permute-start | bytes 393224 | tf_op jit(solution)/shard_map/ppermute | solution.py:589
  236.1 6.6 %collective-permute-start.30 = (bf16[128,512]{1,0:T(8,128)(2,1)S(1)}, bf16[128,512]{1,0:T(8,128)(2,1)S(1)}, u32[]{:S(2)}, u32[]{:S(2)}) collective-permute-start(bf16[128,512]{1,0:T(8,128)(2,1)S(1)} %get-tuple-element.164), channel_id=1, source_target_pairs={{0,2},{1,3},{2,0},{3,1},{4,6},{5,7},{6,4},{7,5},{8,10},{9,11},{10,... | collective-permute-start | bytes 393224 | tf_op jit(solution)/shard_map/ppermute | solution.py:582
  236.2 6.5 %collective-permute-start.31 = (bf16[64,1024]{1,0:T(8,128)(2,1)S(1)}, bf16[64,1024]{1,0:T(8,128)(2,1)S(1)}, u32[]{:S(2)}, u32[]{:S(2)}) collective-permute-start(bf16[64,1024]{1,0:T(8,128)(2,1)S(1)} %get-tuple-element.166), channel_id=1, source_target_pairs={{0,4},{1,5},{2,6},{3,7},{4,0},{5,1},{6,2},{7,3},{8,12},{9,13},{10,... | collective-permute-start | bytes 393224 | tf_op jit(solution)/shard_map/ppermute | solution.py:589
  240.0 8.1 %collective-permute-start.35 = (bf16[64,512]{1,0:T(8,128)(2,1)S(1)}, bf16[64,512]{1,0:T(8,128)(2,1)S(1)}, u32[]{:S(2)}, u32[]{:S(2)}) collective-permute-start(bf16[64,512]{1,0:T(8,128)(2,1)S(1)} %get-tuple-element.176), channel_id=1, source_target_pairs={{0,4},{1,5},{2,6},{3,7},{4,0},{5,1},{6,2},{7,3},{8,12},{9,13},{10,... | collective-permute-start | bytes 196616 | tf_op jit(solution)/shard_map/ppermute | solution.py:589
  242.8 5.2 %collective-permute-start.34 = (bf16[64,512]{1,0:T(8,128)(2,1)S(1)}, bf16[64,512]{1,0:T(8,128)(2,1)S(1)}, u32[]{:S(2)}, u32[]{:S(2)}) collective-permute-start(bf16[64,512]{1,0:T(8,128)(2,1)S(1)} %get-tuple-element.174), channel_id=1, source_target_pairs={{0,4},{1,5},{2,6},{3,7},{4,0},{5,1},{6,2},{7,3},{8,12},{9,13},{10,... | collective-permute-start | bytes 196616 | tf_op jit(solution)/shard_map/ppermute | solution.py:589
  248.2 14.1 %copy-start.5 = (f32[64,11264]{1,0:T(8,128)}, f32[64,11264]{1,0:T(8,128)S(1)}, u32[]{:S(2)}) copy-start(f32[64,11264]{1,0:T(8,128)S(1)} %get-tuple-element.194) | copy-start | bytes 8650756
  248.2 4.3 %collective-permute-start.36 = (f32[11264]{0:T(1024)S(1)}, f32[11264]{0:T(1024)S(1)}, u32[]{:S(2)}, u32[]{:S(2)}) collective-permute-start(f32[11264]{0:T(1024)S(1)} %constant_dynamic-update-slice_fusion.2), channel_id=1, source_target_pairs={{0,1},{1,0},{2,3},{3,2},{4,5},{5,4},{6,7},{7,6},{8,9},{9,8},{10,11... | collective-permute-start | bytes 135176 | tf_op jit(solution)/shard_map/ppermute | solution.py:456
  252.5 4.1 %collective-permute-start.37 = (f32[11264]{0:T(1024)S(1)}, f32[11264]{0:T(1024)S(1)}, u32[]{:S(2)}, u32[]{:S(2)}) collective-permute-start(f32[11264]{0:T(1024)S(1)} %max.9), channel_id=1, source_target_pairs={{0,2},{1,3},{2,0},{3,1},{4,6},{5,7},{6,4},{7,5},{8,10},{9,11},{10,... | collective-permute-start | bytes 135176 | tf_op jit(solution)/shard_map/ppermute | solution.py:456
  256.6 5.0 %collective-permute-start.38 = (f32[11264]{0:T(1024)S(1)}, f32[11264]{0:T(1024)S(1)}, u32[]{:S(2)}, u32[]{:S(2)}) collective-permute-start(f32[11264]{0:T(1024)S(1)} %max.10), channel_id=1, source_target_pairs={{0,4},{1,5},{2,6},{3,7},{4,0},{5,1},{6,2},{7,3},{8,12},{9,13},{10,... | collective-permute-start | bytes 135176 | tf_op jit(solution)/shard_map/ppermute | solution.py:456

commit v3 on v2

--- a/solution.py
+++ b/solution.py
@@ -12,6 +12,8 @@
 WINDOW = 4
 EARLY = 8
 STEP = 2
+Z_FIRST = ()
+DEPTH = (3, 2, 2)
 F32 = jnp.float32
 BF16 = jnp.bfloat16
 
@@ -315,7 +317,7 @@
 
         @pl.when(pl.program_id(0) == 0)
         def _():
-            run_stages(taken, extra, near_ref[0] == 1, splits[-1][0])
+            run_stages(taken, extra, near_ref[0] == 1, splits[-1][-1][1])
 
     live = count_ref[pl.program_id(0) + base]
     for count in range(slots + 1):
@@ -336,13 +338,10 @@
                     )
                     for k in range(count)
                 )
-                row = 0
                 for out, parts in zip(outs, splits):
-                    at = half * parts[0]
-                    for rows in parts:
+                    for i, (row, rows) in enumerate(parts):
+                        at = (i * halves + half) * rows
                         out[at : at + rows] = total[row : row + rows].astype(BF16)
-                        row += rows
-                        at += halves * rows
 
 
 def last_live(count, slots):
@@ -374,9 +373,10 @@
     def whole(array):
         return pl.BlockSpec(array.shape, lambda z, *_: (0, 0))
 
-    high = splits[-1][0]
+    high = splits[-1][-1][1]
     shapes = [
-        jax.ShapeDtypeStruct((halves * sum(parts), zones * lines), BF16) for parts in splits
+        jax.ShapeDtypeStruct((halves * len(parts) * parts[0][1], zones * lines), BF16)
+        for parts in splits
     ]
     later = stage_shapes(stages, high)
     extra = [array for stage in stages for array in stage]
@@ -398,7 +398,7 @@
             + [block_at(k) for k in range(slots)]
             + [whole(array) for array in extra],
             out_specs=[
-                pl.BlockSpec((halves * sum(parts), lines), lambda z, *_: (0, z))
+                pl.BlockSpec((halves * len(parts) * parts[0][1], lines), lambda z, *_: (0, z))
                 for parts in splits
             ]
             + [whole(array) for array in later],
@@ -450,11 +450,11 @@
 def max_over_bus(values, groups):
     if groups & (groups - 1):
         return lax.pmax(values, "bus")
-    step = 1
-    while step < groups:
-        pairs = [(i, i ^ step) for i in range(groups)]
-        values = jnp.maximum(values, lax.ppermute(values, "bus", pairs))
-        step *= 2
+    for steps in ((1,), range(2, groups, 2)):
+        others = [
+            lax.ppermute(values, "bus", [(i, i ^ step) for i in range(groups)]) for step in steps
+        ]
+        values = functools.reduce(jnp.maximum, others, values)
     return values
 
 
@@ -501,7 +501,7 @@
     else:
         gathered = lax.all_gather(sites, "line", axis=0)
         inj = injections(jnp.arange(groups), [gathered[i] for i in range(lines_size)])
-        (whole,) = partial(here.reshape(1), count, [inj], ptdf_blocks, 0, zones_dev, ((scen,),))
+        (whole,) = partial(here.reshape(1), count, [inj], ptdf_blocks, 0, zones_dev, (((0, scen),),))
         flows = [lax.psum_scatter(whole, "bus", scatter_dimension=0, tiled=True).astype(F32)]
 
     loadings, worst, at = [], [], 0
@@ -543,25 +543,31 @@
 
     zones_dev = blocks.shape[0]
     early = min(EARLY, zones_dev)
-    chunks = [((0,), 0, early)] + [((1,), *c) for c in cut(0, early, 2 * STEP)]
+    chunks = [((0,), *c) for c in cut(0, early, 4)] + [((1,), *c) for c in cut(0, early, 2 * STEP)]
     slow = max(early, zones_dev - 2)
     chunks += [((0, 1), *c) for c in cut(early, slow, STEP) + cut(slow, zones_dev, 1)]
     total = len(chunks)
     token = injs[0]
     near_flag = near.astype(jnp.int32).reshape(1)
-    splits = ((high, high), (high,), (high,))
-    sent, kept, own, moved, late, flows = {}, {}, {}, {}, {}, {}
-    for t in range(total + 6):
+    row = {q: (i * high, high) for i, q in enumerate((3, 1, 2, 0))}
+    full = [t for t in range(total) if len(chunks[t][0]) == 2]
+    z_first = [full[i] for i in Z_FIRST if i < len(full)]
+    swaps = [(swap_z, swap_x) if t in z_first else (swap_x, swap_z) for t in range(total)]
+    sent, kept, own, moved, late, flows, ending = {}, {}, {}, {}, {}, {}, {}
+    summed, shared, ended = DEPTH[0], sum(DEPTH[:2]), sum(DEPTH)
+    for t in range(total + ended):
         stages = [
-            (*kept.pop(t - 2), sent.pop(t - 2)) if t - 2 in sent else (),
-            (own.pop(t - 4), moved.pop(t - 4)) if t - 4 in moved else (),
-            (own.pop(t - 6), late.pop(t - 6)) if t - 6 in late else (),
+            (*kept.pop(t - summed), sent.pop(t - summed)) if t - summed in sent else (),
+            (own.pop(t - shared), moved.pop(t - shared)) if t - shared in moved else (),
+            (own.pop(t - ended), late.pop(t - ended)) if t - ended in late else (),
         ]
         if t < total:
             halves, base, zones = chunks[t]
             if 1 in halves and len(injs) == 1:
                 across = copy_after(across, token)
                 injs.append(half_injections(1, [across, lax.ppermute(across, "line", by_core)]))
+            lead, then = (2, 1) if t in z_first else (1, 2)
+            splits = ((row[3], row[lead]), (row[then],), (row[0],))
             send, give, keep, *done = partial(
                 near_flag,
                 token,
@@ -572,24 +578,26 @@
                 splits,
                 stages=stages,
             )
-            sent[t] = lax.ppermute(send, "bus", swap_x)
+            sent[t] = lax.ppermute(send, "bus", swaps[t][0])
             kept[t] = (give, keep)
             token = keep
         else:
-            done = sums(near_flag, stages, high)
+            ending[t - ended], stages[2] = stages[2], ()
+            done = sums(near_flag, stages, high) if any(stages) else []
         done = iter(done)
         if stages[0]:
-            moved[t - 2] = lax.ppermute(next(done), "bus", swap_z)
-            own[t - 2] = next(done)
+            moved[t - summed] = lax.ppermute(next(done), "bus", swaps[t - summed][1])
+            own[t - summed] = next(done)
         if stages[1]:
-            halves = chunks[t - 4][0]
+            halves = chunks[t - shared][0]
             if len(halves) == 1:
-                late[t - 4] = lax.ppermute(next(done), ("line", "bus"), to_side(halves[0]))
+                late[t - shared] = lax.ppermute(next(done), ("line", "bus"), to_side(halves[0]))
             else:
-                late[t - 4] = lax.ppermute(next(done), "bus", swap_far)
-            own[t - 4] = next(done)
+                late[t - shared] = lax.ppermute(next(done), "bus", swap_far)
+            own[t - shared] = next(done)
         if stages[2]:
-            flows[t - 6] = next(done)
+            flows[t - ended] = next(done)
+    flows.update((t, add(*stage)) for t, stage in ending.items() if stage)
     first_flows = [
         jnp.concatenate([flows[t] for t in range(total) if chunks[t][0] == (half,)], axis=1)
         for half in range(2)

time: 267 us -> 239 us (0.90); the launches traced: 262 us -> 239 us
  waiting for transfers between devices: 93.6 us -> 70.9 us
  starting transfers between devices: 69.3 us -> 60.2 us
  Pallas kernels: 87.2 us -> 94.5 us
    ppermute x36 -> x40, waiting for transfers between devices: 73.5 us -> 55.7 us  [the longest x12 22.2 us: staged(): sent[t] = lax.ppermute(send, 'bus', swaps[t][0])]
    ppermute x36 -> x40, starting transfers between devices: 60.5 us -> 51.3 us  [the longest x8 15.1 us: staged(): late[t - shared] = lax.ppermute(next(done), 'bus', swap_far)]
    pallas_call x11 -> x12, Pallas kernels: 49.2 us -> 57.7 us  [partial_flow(): pl.pallas_call(functools.partial(flow_kernel, base=base, slots=slots, hal...]
    ppermute x1, waiting for transfers between devices: 4.79 us -> 0.62 us  [staged(): across = lax.ppermute(sites, 'line', by_y)]
  transfers between devices with their start and end apart: 40 -> 44, of which waited for: 20 -> 25; matrix products, arithmetic and copies ran while one was open for 3% -> 3% of each run, Pallas kernels for 26% -> 34%
where the time goes in v3:
time: 239 us
  Pallas kernels  94.5 us (40%)
  waiting for transfers between devices  70.9 us (30%)
  starting transfers between devices  60.2 us (25%)
  other arithmetic  7.59 us (3%)
  local copies, waits for them, and re-layouts  4.28 us (2%)
    pallas_call x12, Pallas kernels, partial_flow(): pl.pallas_call(functools.partial(flow_kernel, base=base, slots=slots, hal...  57.7 us
    ppermute x12, waiting for transfers between devices, staged(): sent[t] = lax.ppermute(send, 'bus', swaps[t][0])  22.2 us
    pallas_call x2, Pallas kernels, inject(): pl.pallas_call(inject_kernel, grid_spec=pltpu.PrefetchScalarGridSpec(num_...  15.7 us
    ppermute x8, starting transfers between devices, staged(): late[t - shared] = lax.ppermute(next(done), 'bus', swap_far)  15.1 us
    ppermute x12, waiting for transfers between devices, staged(): moved[t - summed] = lax.ppermute(next(done), 'bus', swaps[t - summed][1])  14.1 us
    all_to_all x1, waiting for transfers between devices, body(): lax.all_to_all(route(here, site_bus, site_values, groups, bus_dev), 'bus'...  13.6 us
    ppermute x12, starting transfers between devices, staged(): sent[t] = lax.ppermute(send, 'bus', swaps[t][0])  13.3 us
    ppermute x12, starting transfers between devices, staged(): moved[t - summed] = lax.ppermute(next(done), 'bus', swaps[t - summed][1])  11.9 us
  transfers between devices with their start and end apart: 44, of which 25 were waited for; matrix products, arithmetic and copies ran while one was open for 3% of the time, Pallas kernels for 34%

profile of v3, /device:TPU:0, one launch (start us, length us, event | category | flops | bytes accessed | tf_op | source)
XLA Modules:
  0.0 238.6 jit_solution(12211150684413286268)
XLA Ops:
  0.6 1.6 copy-done.4
  2.2 0.9 copy-done.5
  3.1 7.5 %route.1 = bf16[8,128,512]{2,1,0:T(8,128)(2,1)} custom-call(s32[1]{0:T(128)} %bitcast.2.here_ref, s32[256,128]{1,0:T(8,128)S(1)} %bitcast.33, f32[128,4096]{1,0:T(8,128)S(1)} %copy-done.4), custom_call_target="tpu_custom_call" | custom-call | flops 8589934592 | bytes 2097152 | tf_op jit(solution)/shard_map/route/pallas_call | solution.py:94
  10.7 7.3 %all-to-all-start = ((bf16[8,128,512]{2,1,0:T(8,128)(2,1)}), bf16[8,128,512]{2,1,0:T(8,128)(2,1)S(1)}, u32[]{:S(2)}, u32[]{:S(2)}) async-start(bf16[8,128,512]{2,1,0:T(8,128)(2,1)} %route.1), calls=%async_computation | async-start | bytes 2097152 | tf_op jit(solution)/shard_map/all_to_all | solution.py:473
  17.9 6.3 %arrivals.1 = s32[8,1,512]{2,1,0:T(1,128)S(1)} custom-call(s32[1]{0:T(128)} %bitcast.2.here_ref, s32[256,128]{1,0:T(8,128)S(1)} %bitcast.34), custom_call_target="tpu_custom_call" | custom-call | flops 1073741824 | bytes 131072 | tf_op jit(solution)/shard_map/arrivals/pallas_call | solution.py:147
  24.3 5.8 %sort.14 = (s32[4096]{0:T(1024)S(1)}, s32[4096]{0:T(1024)}) sort(s32[4096]{0:T(1024)S(1)} %iota_add_fusion, s32[4096]{0:T(1024)S(1)} %iota.20), dimensions={0}, to_apply=%region_1.2 | sort | flops 49152 | bytes 65536 | tf_op jit(solution)/shard_map/sort | solution.py:478
  30.1 13.6 %all-to-all-done.runs_ref = bf16[8,128,512]{2,1,0:T(8,128)(2,1)S(1)} async-done(((bf16[8,128,512]{2,1,0:T(8,128)(2,1)}), bf16[8,128,512]{2,1,0:T(8,128)(2,1)S(1)}, u32[]{:S(2)}, u32[]{:S(2)}) %all-to-all-start) | async-done | bytes 1048608 | tf_op jit(solution)/shard_map/all_to_all | solution.py:473
  43.7 6.5 %merge.1.refs_0_ = bf16[32,128,128]{2,1,0:T(8,128)(2,1)} custom-call(s32[8,1,512]{2,1,0:T(1,128)S(1)} %bitcast.32, bf16[8,128,512]{2,1,0:T(8,128)(2,1)S(1)} %all-to-all-done.runs_ref), custom_call_target="tpu_custom_call" | custom-call | flops 8589934592 | bytes 2097152 | tf_op jit(solution)/shard_map/merge/pallas_call | solution.py:178
  50.2 1.5 collective-permute-start.1
  53.0 8.5 %inject.2.token_ref.refs_0_.refs_1_.refs_2_ = bf16[14,256,640]{2,1,0:T(8,128)(2,1)S(1)} custom-call(s32[14]{0:T(128)S(1)} %get-tuple-element.186.first_ref, s32[14]{0:T(128)S(1)} %get-tuple-element.185.windows_ref, s32[4]{0:T(128)S(1)} %pad_add_fusion.rows_ref, s32[32,1,128]{2,1,0:T(1,128)S(1)} %bitcast.17, bf16[32,128,128]{2,1,0:T(8,128)(2,1)} %merge.1.refs_0_, ...), custom_call_target="tpu_custom_call" | custom-call | flops 65536 | bytes 1024 | tf_op jit(solution)/shard_map/inject/pallas_call | solution.py:235
  61.6 7.1 %partial_flow.12 = (bf16[128,2048]{1,0:T(8,128)(2,1)}, bf16[64,2048]{1,0:T(8,128)(2,1)S(1)}, bf16[64,2048]{1,0:T(8,128)(2,1)S(1)}) custom-call(s32[22]{0:T(128)S(1)} %bitcast.20, s32[66]{0:T(128)S(1)} %reshape.46.zone_ref, s32[66]{0:T(128)S(1)} %reshape.47.last_ref, s32[1]{0:T(128)} %bitcast.1.near_ref, ...), custom_call_target="tpu_custom_call" | custom-call | flops 1006632960 | bytes 5898240 | tf_op jit(solution)/shard_map/partial_flow/pallas_call | solution.py:384
  69.3 6.0 %partial_flow.13 = (bf16[128,2048]{1,0:T(8,128)(2,1)}, bf16[64,2048]{1,0:T(8,128)(2,1)S(1)}, bf16[64,2048]{1,0:T(8,128)(2,1)S(1)}) custom-call(s32[22]{0:T(128)S(1)} %bitcast.21, s32[66]{0:T(128)S(1)} %reshape.46.zone_ref, s32[66]{0:T(128)S(1)} %reshape.47.last_ref, s32[1]{0:T(128)} %bitcast.1.near_ref, ...), custom_call_target="tpu_custom_call" | custom-call | flops 1006632960 | bytes 5898240 | tf_op jit(solution)/shard_map/partial_flow/pallas_call | solution.py:384
  76.2 1.5 collective-permute-start.3
  78.8 7.3 %inject.3.refs_0_.refs_1_.refs_2_.refs_3_.refs_4_.refs_5_ = bf16[14,256,640]{2,1,0:T(8,128)(2,1)S(1)} custom-call(s32[14]{0:T(128)S(1)} %get-tuple-element.186.first_ref, s32[14]{0:T(128)S(1)} %get-tuple-element.185.windows_ref, s32[4]{0:T(128)S(1)} %pad_add_fusion.1.rows_ref, s32[32,1,128]{2,1,0:T(1,128)S(1)} %bitcast.18, ...), custom_call_target="tpu_custom_call" | custom-call | flops 65536 | bytes 1024 | tf_op jit(solution)/shard_map/inject/pallas_call | solution.py:235
  86.1 5.4 %partial_flow.14 = (bf16[128,2048]{1,0:T(8,128)(2,1)S(1)}, bf16[64,2048]{1,0:T(8,128)(2,1)S(1)}, bf16[64,2048]{1,0:T(8,128)(2,1)S(1)}) custom-call(s32[22]{0:T(128)S(1)} %bitcast.22, s32[66]{0:T(128)S(1)} %reshape.46.zone_ref, s32[66]{0:T(128)S(1)} %reshape.47.last_ref, s32[1]{0:T(128)} %bitcast.1.near_ref, ...), custom_call_target="tpu_custom_call" | custom-call | flops 1006632960 | bytes 5898240 | tf_op jit(solution)/shard_map/partial_flow/pallas_call | solution.py:384
  91.5 1.5 collective-permute-start.5
  93.0 6.2 %partial_flow.15 = (bf16[128,2048]{1,0:T(8,128)(2,1)S(1)}, bf16[64,2048]{1,0:T(8,128)(2,1)S(1)}, bf16[64,2048]{1,0:T(8,128)(2,1)S(1)}, bf16[64,2048]{1,0:T(8,128)(2,1)S(1)}, bf16[64,2048]{1,0:T(8,128)(2,1)S(1)}) custom-call(s32[22]{0:T(128)S(1)} %bitcast.23, s32[66]{0:T(128)S(1)} %reshape.46.zone_ref, s32[66]{0:T(128)S(1)} %reshape.47.last_ref, ...), custom_call_target="tpu_custom_call" | custom-call | flops 1006632960 | bytes 5898240 | tf_op jit(solution)/shard_map/partial_flow/pallas_call | solution.py:384
  99.4 3.0 %collective-permute-done.4.refs_11_ = bf16[128,2048]{1,0:T(8,128)(2,1)S(1)} collective-permute-done((bf16[128,2048]{1,0:T(8,128)(2,1)}, bf16[128,2048]{1,0:T(8,128)(2,1)S(1)}, u32[]{:S(2)}, u32[]{:S(2)}) %collective-permute-start.4) | collective-permute-done | bytes 524320 | tf_op jit(solution)/shard_map/ppermute | solution.py:581
  102.4 4.2 %partial_flow.16 = (bf16[256,1024]{1,0:T(8,128)(2,1)S(1)}, bf16[128,1024]{1,0:T(8,128)(2,1)S(1)}, bf16[128,1024]{1,0:T(8,128)(2,1)S(1)}, bf16[64,2048]{1,0:T(8,128)(2,1)S(1)}, bf16[64,2048]{1,0:T(8,128)(2,1)S(1)}) custom-call(s32[22]{0:T(128)S(1)} %bitcast.24, s32[66]{0:T(128)S(1)} %reshape.46.zone_ref, s32[66]{0:T(128)S(1)} %reshape.47.last_ref, ...), custom_call_target="tpu_custom_call" | custom-call | flops 1006632960 | bytes 3932160 | tf_op jit(solution)/shard_map/partial_flow/pallas_call | solution.py:384
  106.6 0.9 collective-permute-start.9
  107.7 5.9 %collective-permute-done.5.refs_11_ = bf16[128,2048]{1,0:T(8,128)(2,1)S(1)} collective-permute-done((bf16[128,2048]{1,0:T(8,128)(2,1)S(1)}, bf16[128,2048]{1,0:T(8,128)(2,1)S(1)}, u32[]{:S(2)}, u32[]{:S(2)}) %collective-permute-start.5) | collective-permute-done | bytes 524320 | tf_op jit(solution)/shard_map/ppermute | solution.py:581
  113.6 4.1 %partial_flow.17 = (bf16[256,1024]{1,0:T(8,128)(2,1)S(1)}, bf16[128,1024]{1,0:T(8,128)(2,1)S(1)}, bf16[128,1024]{1,0:T(8,128)(2,1)S(1)}, bf16[64,2048]{1,0:T(8,1...) custom-call(s32[22]{0:T(128)S(1)} %bitcast.25, ...), custom_call_target="tpu_custom_call" | custom-call | flops 1006632960 | bytes 3932160 | tf_op jit(solution)/shard_map/partial_flow/pallas_call | solution.py:384
  117.9 1.3 collective-permute-start.11
  119.2 1.3 collective-permute-start.12
  120.4 4.4 %collective-permute-done.7.refs_11_ = bf16[128,2048]{1,0:T(8,128)(2,1)S(1)} collective-permute-done((bf16[128,2048]{1,0:T(8,128)(2,1)S(1)}, bf16[128,2048]{1,0:T(8,128)(2,1)S(1)}, u32[]{:S(2)}, u32[]{:S(2)}) %collective-permute-start.7) | collective-permute-done | bytes 524320 | tf_op jit(solution)/shard_map/ppermute | solution.py:581
  124.9 4.9 %partial_flow.18 = (bf16[256,1024]{1,0:T(8,128)(2,1)S(1)}, bf16[128,1024]{1,0:T(8,128)(2,1)S(1)}, bf16[128,1024]{1,0:T(8,128)(2,1)S(1)}, bf16[64,2048]{1,0:T(8,1...) custom-call(s32[22]{0:T(128)S(1)} %bitcast.26, ...), custom_call_target="tpu_custom_call" | custom-call | flops 1006632960 | bytes 3932160 | tf_op jit(solution)/shard_map/partial_flow/pallas_call | solution.py:384
  129.8 1.9 collective-permute-start.15
  131.7 4.4 %collective-permute-done.9.refs_11_ = bf16[256,1024]{1,0:T(8,128)(2,1)S(1)} collective-permute-done((bf16[256,1024]{1,0:T(8,128)(2,1)S(1)}, bf16[256,1024]{1,0:T(8,128)(2,1)S(1)}, u32[]{:S(2)}, u32[]{:S(2)}) %collective-permute-start.9) | collective-permute-done | bytes 524320 | tf_op jit(solution)/shard_map/ppermute | solution.py:581
  136.1 1.3 collective-permute-start.14
  137.4 3.6 %partial_flow.19 = (bf16[256,1024]{1,0:T(8,128)(2,1)S(1)}, bf16[128,1024]{1,0:T(8,128)(2,1)S(1)}, bf16[128,1024]{1,0:T(8,128)(2,1)S(1)}, bf16[128,1024]{1,0:T(8,...) custom-call(s32[22]{0:T(128)S(1)} %bitcast.27, ...), custom_call_target="tpu_custom_call" | custom-call | flops 1006632960 | bytes 3932160 | tf_op jit(solution)/shard_map/partial_flow/pallas_call | solution.py:384
  141.0 2.5 %collective-permute-start.18 = (bf16[256,1024]{1,0:T(8,128)(2,1)S(1)}, bf16[256,1024]{1,0:T(8,128)(2,1)S(1)}, u32[]{:S(2)}, u32[]{:S(2)}) collective-permute-start(bf16[256,1024]{1,0:T(8,128)(2,1)S(1)} %get-tuple-element.138), channel_id=1, source_target_pairs={{0,1},{1,0},{2,3},{3,2},{4,5},{5,4},{6,7},{7,6},{8,9},{9,8},{10,11... | collective-permute-start | bytes 1572872 | tf_op jit(solution)/shard_map/ppermute | solution.py:581
  144.1 1.7 collective-permute-done.13.refs_13_
  146.2 5.9 %collective-permute-done.14.refs_15_ = bf16[64,2048]{1,0:T(8,128)(2,1)S(1)} collective-permute-done((bf16[64,2048]{1,0:T(8,128)(2,1)S(1)}, bf16[64,2048]{1,0:T(8,128)(2,1)S(1)}, u32[]{:S(2)}, u32[]{:S(2)}) %collective-permute-start.14) | collective-permute-done | bytes 262176 | tf_op jit(solution)/shard_map/ppermute | solution.py:594
  152.1 1.4 collective-permute-start.17
  153.5 5.6 %partial_flow.20 = (bf16[256,1024]{1,0:T(8,128)(2,1)S(1)}, bf16[128,1024]{1,0:T(8,128)(2,1)S(1)}, bf16[128,1024]{1,0:T(8,128)(2,1)S(1)}, bf16[128,1024]{1,0:T(8,...) custom-call(s32[22]{0:T(128)S(1)} %bitcast.28, ...), custom_call_target="tpu_custom_call" | custom-call | flops 1006632960 | bytes 3932160 | tf_op jit(solution)/shard_map/partial_flow/pallas_call | solution.py:384
  159.2 1.3 collective-permute-start.20
  160.5 1.1 collective-permute-start.21
  161.6 3.8 %partial_flow.21 = (bf16[256,1024]{1,0:T(8,128)(2,1)S(1)}, bf16[128,1024]{1,0:T(8,128)(2,1)S(1)}, bf16[128,1024]{1,0:T(8,128)(2,1)S(1)}, bf16[128,1024]{1,0:T(8,...) custom-call(s32[22]{0:T(128)S(1)} %bitcast.29, ...), custom_call_target="tpu_custom_call" | custom-call | flops 1006632960 | bytes 3932160 | tf_op jit(solution)/shard_map/partial_flow/pallas_call | solution.py:384
  165.4 2.9 %collective-permute-start.22 = (bf16[128,1024]{1,0:T(8,128)(2,1)S(1)}, bf16[128,1024]{1,0:T(8,128)(2,1)S(1)}, u32[]{:S(2)}, u32[]{:S(2)}) collective-permute-start(bf16[128,1024]{1,0:T(8,128)(2,1)S(1)} %get-tuple-element.148), channel_id=1, source_target_pairs={{0,2},{1,3},{2,0},{3,1},{4,6},{5,7},{6,4},{7,5},{8,10},{9,11},{10,... | collective-permute-start | bytes 786440 | tf_op jit(solution)/shard_map/ppermute | solution.py:589
  168.3 1.5 collective-permute-done.18.refs_11_
  169.8 1.3 collective-permute-start.23
  171.2 2.9 %partial_flow.22 = (bf16[256,512]{1,0:T(8,128)(2,1)S(1)}, bf16[128,512]{1,0:T(8,128)(2,1)S(1)}, bf16[128,512]{1,0:T(8,128)(2,1)S(1)}, bf16[128,1024]{1,0:T(8,128...) custom-call(s32[22]{0:T(128)S(1)} %bitcast.30, ...), custom_call_target="tpu_custom_call" | custom-call | flops 503316480 | bytes 1966080 | tf_op jit(solution)/shard_map/partial_flow/pallas_call | solution.py:384
  174.1 4.1 %collective-permute-start.27 = (bf16[128,1024]{1,0:T(8,128)(2,1)S(1)}, bf16[128,1024]{1,0:T(8,128)(2,1)S(1)}, u32[]{:S(2)}, u32[]{:S(2)}) collective-permute-start(bf16[128,1024]{1,0:T(8,128)(2,1)S(1)} %get-tuple-element.159), channel_id=1, source_target_pairs={{0,2},{1,3},{2,0},{3,1},{4,6},{5,7},{6,4},{7,5},{8,10},{9,11},{10,... | collective-permute-start | bytes 786440 | tf_op jit(solution)/shard_map/ppermute | solution.py:589
  179.0 1.7 collective-permute-start.29
  180.7 3.4 %collective-permute-start.24 = (bf16[64,1024]{1,0:T(8,128)(2,1)S(1)}, bf16[64,1024]{1,0:T(8,128)(2,1)S(1)}, u32[]{:S(2)}, u32[]{:S(2)}) collective-permute-start(bf16[64,1024]{1,0:T(8,128)(2,1)S(1)} %get-tuple-element.153), channel_id=1, source_target_pairs={{0,4},{1,5},{2,6},{3,7},{4,0},{5,1},{6,2},{7,3},{8,12},{9,13},{10,... | collective-permute-start | bytes 393224 | tf_op jit(solution)/shard_map/ppermute | solution.py:596
  184.1 4.0 %partial_flow.23 = (bf16[256,512]{1,0:T(8,128)(2,1)S(1)}, bf16[128,512]{1,0:T(8,128)(2,1)S(1)}, bf16[128,512]{1,0:T(8,128)(2,1)S(1)}, bf16[128,1024]{1,0:T(8,128...) custom-call(s32[22]{0:T(128)S(1)} %bitcast.31, ...), custom_call_target="tpu_custom_call" | custom-call | flops 503316480 | bytes 1966080 | tf_op jit(solution)/shard_map/partial_flow/pallas_call | solution.py:384
  188.2 2.0 collective-permute-done.24
  190.3 2.0 collective-permute-done.26.refs_2_
  192.3 3.0 %collective-permute-start.30 = (bf16[128,1024]{1,0:T(8,128)(2,1)S(1)}, bf16[128,1024]{1,0:T(8,128)(2,1)S(1)}, u32[]{:S(2)}, u32[]{:S(2)}) collective-permute-start(bf16[128,1024]{1,0:T(8,128)(2,1)S(1)} %get-tuple-element.165), channel_id=1, source_target_pairs={{0,2},{1,3},{2,0},{3,1},{4,6},{5,7},{6,4},{7,5},{8,10},{9,11},{10,... | collective-permute-start | bytes 786440 | tf_op jit(solution)/shard_map/ppermute | solution.py:589
  197.9 7.4 %collective-permute-done.30.refs_4_ = bf16[128,1024]{1,0:T(8,128)(2,1)S(1)} collective-permute-done((bf16[128,1024]{1,0:T(8,128)(2,1)S(1)}, bf16[128,1024]{1,0:T(8,128)(2,1)S(1)}, u32[]{:S(2)}, u32[]{:S(2)}) %collective-permute-start.30) | collective-permute-done | bytes 262176 | tf_op jit(solution)/shard_map/ppermute | solution.py:589
  205.5 4.8 %collective-permute-start.31 = (bf16[64,1024]{1,0:T(8,128)(2,1)S(1)}, bf16[64,1024]{1,0:T(8,128)(2,1)S(1)}, u32[]{:S(2)}, u32[]{:S(2)}) collective-permute-start(bf16[64,1024]{1,0:T(8,128)(2,1)S(1)} %get-tuple-element.167), channel_id=1, source_target_pairs={{0,4},{1,5},{2,6},{3,7},{4,0},{5,1},{6,2},{7,3},{8,12},{9,13},{10,... | collective-permute-start | bytes 393224 | tf_op jit(solution)/shard_map/ppermute | solution.py:596
  210.4 2.3 collective-permute-done.33.refs_4_
  212.8 1.0 collective-permute-start.37
  213.9 3.7 %collective-permute-start.34 = (bf16[64,1024]{1,0:T(8,128)(2,1)S(1)}, bf16[64,1024]{1,0:T(8,128)(2,1)S(1)}, u32[]{:S(2)}, u32[]{:S(2)}) collective-permute-start(bf16[64,1024]{1,0:T(8,128)(2,1)S(1)} %get-tuple-element.174), channel_id=1, source_target_pairs={{0,4},{1,5},{2,6},{3,7},{4,0},{5,1},{6,2},{7,3},{8,12},{9,13},{10,... | collective-permute-start | bytes 393224 | tf_op jit(solution)/shard_map/ppermute | solution.py:596
  217.9 2.8 %collective-permute-done.37.refs_1_ = bf16[128,512]{1,0:T(8,128)(2,1)S(1)} collective-permute-done((bf16[128,512]{1,0:T(8,128)(2,1)S(1)}, bf16[128,512]{1,0:T(8,128)(2,1)S(1)}, u32[]{:S(2)}, u32[]{:S(2)}) %collective-permute-start.37) | collective-permute-done | bytes 131104 | tf_op jit(solution)/shard_map/ppermute | solution.py:589
  220.7 1.0 collective-permute-start.38
  221.7 2.8 %collective-permute-done.34 = bf16[64,1024]{1,0:T(8,128)(2,1)S(1)} collective-permute-done((bf16[64,1024]{1,0:T(8,128)(2,1)S(1)}, bf16[64,1024]{1,0:T(8,128)(2,1)S(1)}, u32[]{:S(2)}, u32[]{:S(2)}) %collective-permute-start.34) | collective-permute-done | bytes 131104 | tf_op jit(solution)/shard_map/ppermute | solution.py:596
  225.2 1.3 collective-permute-done.38
  226.6 1.2 collective-permute-start.39
  227.9 2.9 %collective-permute-done.39 = f32[11264]{0:T(1024)S(1)} collective-permute-done((f32[11264]{0:T(1024)S(1)}, f32[11264]{0:T(1024)S(1)}, u32[]{:S(2)}, u32[]{:S(2)}) %collective-permute-start.39) | collective-permute-done | bytes 45088 | tf_op jit(solution)/shard_map/ppermute | solution.py:455
  230.8 2.3 collective-permute-start.42
  233.0 2.2 collective-permute-start.40
  235.2 1.5 collective-permute-done.42
  236.7 1.3 collective-permute-done.41
  (124 shorter events, 11.4 us)
Async XLA Ops:
  0.6 1.6 copy-start.4
  2.2 0.9 copy-start.5
  3.1 14.8 %copy-start.6 = (s32[32768]{0:T(1024)S(1)}, s32[32768]{0:T(1024)}, u32[]{:S(2)}) copy-start(s32[32768]{0:T(1024)} %param.7) | copy-start | bytes 393220
  10.7 33.0 %all-to-all-start = ((bf16[8,128,512]{2,1,0:T(8,128)(2,1)}), bf16[8,128,512]{2,1,0:T(8,128)(2,1)S(1)}, u32[]{:S(2)}, u32[]{:S(2)}) async-start(bf16[8,128,512]{2,1,0:T(8,128)(2,1)} %route.1), calls=%async_computation | async-start | bytes 2097152 | tf_op jit(solution)/shard_map/all_to_all | solution.py:473
  43.7 8.0 %copy-start.15 = (s32[22,3]{0,1:T(4,128)S(1)}, s32[22,3]{0,1:T(4,128)}, u32[]{:S(2)}) copy-start(s32[22,3]{0,1:T(4,128)} %param.9) | copy-start | bytes 796
  43.7 8.2 %copy-start.3 = (s32[22,1]{0,1:T(1,128)S(1)}, s32[22,1]{0,1:T(1,128)}, u32[]{:S(2)}) copy-start(s32[22,1]{0,1:T(1,128)} %param.8) | copy-start | bytes 268
  50.2 2.9 %collective-permute-start = (bf16[32,128,128]{2,1,0:T(8,128)(2,1)}, bf16[32,128,128]{2,1,0:T(8,128)(2,1)S(1)}, u32[]{:S(2)}, u32[]{:S(2)}) collective-permute-start(bf16[32,128,128]{2,1,0:T(8,128)(2,1)} %merge.1.refs_0_), channel_id=1, source_target_pairs={{0,8},{8,0},{16,24},{24,16},{1,9},{9,1},{17,25},{25,17},{2,10},{10... | collective-permute-start | bytes 3145736 | tf_op jit(solution)/shard_map/ppermute | solution.py:541
  50.2 25.8 %collective-permute-start.1 = (bf16[32,128,128]{2,1,0:T(8,128)(2,1)}, bf16[32,128,128]{2,1,0:T(8,128)(2,1)S(1)}, u32[]{:S(2)}, u32[]{:S(2)}) collective-permute-start(bf16[32,128,128]{2,1,0:T(8,128)(2,1)} %merge.1.refs_0_), channel_id=1, source_target_pairs={{0,16},{8,24},{16,0},{24,8},{1,17},{9,25},{17,1},{25,9},{2,18},{10... | collective-permute-start | bytes 3145736 | tf_op jit(solution)/shard_map/ppermute | solution.py:540
  61.5 7.8 %copy-start = (bf16[14,256,640]{2,1,0:T(8,128)(2,1)}, bf16[14,256,640]{2,1,0:T(8,128)(2,1)S(1)}, u32[]{:S(2)}) copy-start(bf16[14,256,640]{2,1,0:T(8,128)(2,1)S(1)} %inject.2.token_ref.refs_0_.refs_1_.refs_2_) | copy-start | bytes 13762564
  68.6 0.7 copy-start.1
  76.1 2.7 %collective-permute-start.2 = (bf16[32,128,128]{2,1,0:T(8,128)(2,1)S(1)}, bf16[32,128,128]{2,1,0:T(8,128)(2,1)S(1)}, u32[]{:S(2)}, u32[]{:S(2)}) collective-permute-start(bf16[32,128,128]{2,1,0:T(8,128)(2,1)S(1)} %copy_after.1.refs_0_), channel_id=1, source_target_pairs={{0,8},{8,0},{16,24},{24,16},{1,9},{9,1},{17,25},{25,17},{2,10},{10... | collective-permute-start | bytes 3145736 | tf_op jit(solution)/shard_map/ppermute | solution.py:568
  76.2 16.9 %collective-permute-start.3 = (bf16[128,2048]{1,0:T(8,128)(2,1)}, bf16[128,2048]{1,0:T(8,128)(2,1)}, u32[]{:S(2)}, u32[]{:S(2)}) collective-permute-start(bf16[128,2048]{1,0:T(8,128)(2,1)} %get-tuple-element.98), channel_id=1, source_target_pairs={{0,1},{1,0},{2,3},{3,2},{4,5},{5,4},{6,7},{7,6},{8,9},{9,8},{10,11... | collective-permute-start | bytes 1572872 | tf_op jit(solution)/shard_map/ppermute | solution.py:581
  77.7 24.7 %collective-permute-start.4 = (bf16[128,2048]{1,0:T(8,128)(2,1)}, bf16[128,2048]{1,0:T(8,128)(2,1)S(1)}, u32[]{:S(2)}, u32[]{:S(2)}) collective-permute-start(bf16[128,2048]{1,0:T(8,128)(2,1)} %get-tuple-element.101), channel_id=1, source_target_pairs={{0,1},{1,0},{2,3},{3,2},{4,5},{5,4},{6,7},{7,6},{8,9},{9,8},{10,11... | collective-permute-start | bytes 1572872 | tf_op jit(solution)/shard_map/ppermute | solution.py:581
  86.1 7.0 %copy-start.2 = (bf16[64,2048]{1,0:T(8,128)(2,1)S(1)}, bf16[64,2048]{1,0:T(8,128)(2,1)}, u32[]{:S(2)}) copy-start(bf16[64,2048]{1,0:T(8,128)(2,1)} %copy-done.1) | copy-start | bytes 786436
  91.5 22.1 %collective-permute-start.5 = (bf16[128,2048]{1,0:T(8,128)(2,1)S(1)}, bf16[128,2048]{1,0:T(8,128)(2,1)S(1)}, u32[]{:S(2)}, u32[]{:S(2)}) collective-permute-start(bf16[128,2048]{1,0:T(8,128)(2,1)S(1)} %get-tuple-element.104), channel_id=1, source_target_pairs={{0,1},{1,0},{2,3},{3,2},{4,5},{5,4},{6,7},{7,6},{8,9},{9,8},{10,11... | collective-permute-start | bytes 1572872 | tf_op jit(solution)/shard_map/ppermute | solution.py:581
  93.0 9.4 %slice-start = ((s8[4587520]{0:T(1024)(128)(4,1)}), s8[4194304]{0:T(1024)(128)(4,1)S(1)}, s32[]{:S(2)}) async-start(s8[4587520]{0:T(1024)(128)(4,1)} %bitcast.15), calls=%async_computation.1 | async-start | bytes 8388608
  93.0 9.4 %slice-start.1 = ((s8[4587520]{0:T(1024)(128)(4,1)}), s8[393216]{0:T(1024)(128)(4,1)S(1)}, s32[]{:S(2)}) async-start(s8[4587520]{0:T(1024)(128)(4,1)} %bitcast.15), calls=%async_computation.2 | async-start | bytes 786432
  99.2 25.6 %collective-permute-start.7 = (bf16[128,2048]{1,0:T(8,128)(2,1)S(1)}, bf16[128,2048]{1,0:T(8,128)(2,1)S(1)}, u32[]{:S(2)}, u32[]{:S(2)}) collective-permute-start(bf16[128,2048]{1,0:T(8,128)(2,1)S(1)} %get-tuple-element.109), channel_id=1, source_target_pairs={{0,1},{1,0},{2,3},{3,2},{4,5},{5,4},{6,7},{7,6},{8,9},{9,8},{10,11... | collective-permute-start | bytes 1572872 | tf_op jit(solution)/shard_map/ppermute | solution.py:581
  99.3 8.4 %collective-permute-start.6 = (bf16[64,2048]{1,0:T(8,128)(2,1)S(1)}, bf16[64,2048]{1,0:T(8,128)(2,1)S(1)}, u32[]{:S(2)}, u32[]{:S(2)}) collective-permute-start(bf16[64,2048]{1,0:T(8,128)(2,1)S(1)} %get-tuple-element.106), channel_id=1, source_target_pairs={{0,2},{1,3},{2,0},{3,1},{4,6},{5,7},{6,4},{7,5},{8,10},{9,11},{10,... | collective-permute-start | bytes 786440 | tf_op jit(solution)/shard_map/ppermute | solution.py:589
  106.6 29.5 %collective-permute-start.9 = (bf16[256,1024]{1,0:T(8,128)(2,1)S(1)}, bf16[256,1024]{1,0:T(8,128)(2,1)S(1)}, u32[]{:S(2)}, u32[]{:S(2)}) collective-permute-start(bf16[256,1024]{1,0:T(8,128)(2,1)S(1)} %get-tuple-element.114), channel_id=1, source_target_pairs={{0,1},{1,0},{2,3},{3,2},{4,5},{5,4},{6,7},{7,6},{8,9},{9,8},{10,11... | collective-permute-start | bytes 1572872 | tf_op jit(solution)/shard_map/ppermute | solution.py:581
  107.5 11.6 %collective-permute-start.8 = (bf16[64,2048]{1,0:T(8,128)(2,1)S(1)}, bf16[64,2048]{1,0:T(8,128)(2,1)S(1)}, u32[]{:S(2)}, u32[]{:S(2)}) collective-permute-start(bf16[64,2048]{1,0:T(8,128)(2,1)S(1)} %get-tuple-element.111), channel_id=1, source_target_pairs={{0,2},{1,3},{2,0},{3,1},{4,6},{5,7},{6,4},{7,5},{8,10},{9,11},{10,... | collective-permute-start | bytes 786440 | tf_op jit(solution)/shard_map/ppermute | solution.py:589
  117.7 18.4 %collective-permute-start.10 = (bf16[64,2048]{1,0:T(8,128)(2,1)S(1)}, bf16[64,2048]{1,0:T(8,128)(2,1)S(1)}, u32[]{:S(2)}, u32[]{:S(2)}) collective-permute-start(bf16[64,2048]{1,0:T(8,128)(2,1)S(1)} %get-tuple-element.116), channel_id=1, source_target_pairs={{0,2},{1,3},{2,0},{3,1},{4,6},{5,7},{6,4},{7,5},{8,10},{9,11},{10,... | collective-permute-start | bytes 786440 | tf_op jit(solution)/shard_map/ppermute | solution.py:589
  117.9 19.5 %collective-permute-start.11 = (bf16[64,2048]{1,0:T(8,128)(2,1)S(1)}, bf16[64,2048]{1,0:T(8,128)(2,1)S(1)}, u32[]{:S(2)}, u32[]{:S(2)}) collective-permute-start(bf16[64,2048]{1,0:T(8,128)(2,1)S(1)} %get-tuple-element.118), channel_id=1, source_target_pairs={{4,0},{5,1},{6,2},{7,3},{12,8},{13,9},{14,10},{15,11},{16,20},{17,... | collective-permute-start | bytes 786440 | tf_op jit(solution)/shard_map/ppermute | solution.py:594
  119.2 34.3 %collective-permute-start.12 = (bf16[256,1024]{1,0:T(8,128)(2,1)S(1)}, bf16[256,1024]{1,0:T(8,128)(2,1)S(1)}, u32[]{:S(2)}, u32[]{:S(2)}) collective-permute-start(bf16[256,1024]{1,0:T(8,128)(2,1)S(1)} %get-tuple-element.122), channel_id=1, source_target_pairs={{0,1},{1,0},{2,3},{3,2},{4,5},{5,4},{6,7},{7,6},{8,9},{9,8},{10,11... | collective-permute-start | bytes 1572872 | tf_op jit(solution)/shard_map/ppermute | solution.py:581
  129.8 29.4 %collective-permute-start.15 = (bf16[256,1024]{1,0:T(8,128)(2,1)S(1)}, bf16[256,1024]{1,0:T(8,128)(2,1)S(1)}, u32[]{:S(2)}, u32[]{:S(2)}) collective-permute-start(bf16[256,1024]{1,0:T(8,128)(2,1)S(1)} %get-tuple-element.130), channel_id=1, source_target_pairs={{0,1},{1,0},{2,3},{3,2},{4,5},{5,4},{6,7},{7,6},{8,9},{9,8},{10,11... | collective-permute-start | bytes 1572872 | tf_op jit(solution)/shard_map/ppermute | solution.py:581
  136.1 9.7 %collective-permute-start.13 = (bf16[64,2048]{1,0:T(8,128)(2,1)S(1)}, bf16[64,2048]{1,0:T(8,128)(2,1)S(1)}, u32[]{:S(2)}, u32[]{:S(2)}) collective-permute-start(bf16[64,2048]{1,0:T(8,128)(2,1)S(1)} %get-tuple-element.124), channel_id=1, source_target_pairs={{0,2},{1,3},{2,0},{3,1},{4,6},{5,7},{6,4},{7,5},{8,10},{9,11},{10,... | collective-permute-start | bytes 786440 | tf_op jit(solution)/shard_map/ppermute | solution.py:589
  136.1 16.0 %collective-permute-start.14 = (bf16[64,2048]{1,0:T(8,128)(2,1)S(1)}, bf16[64,2048]{1,0:T(8,128)(2,1)S(1)}, u32[]{:S(2)}, u32[]{:S(2)}) collective-permute-start(bf16[64,2048]{1,0:T(8,128)(2,1)S(1)} %get-tuple-element.126), channel_id=1, source_target_pairs={{4,0},{5,1},{6,2},{7,3},{12,8},{13,9},{14,10},{15,11},{16,20},{17,... | collective-permute-start | bytes 786440 | tf_op jit(solution)/shard_map/ppermute | solution.py:594
  137.4 6.1 %copy-start.8 = (f32[11264]{0:T(1024)S(1)}, f32[11264]{0:T(1024)}, u32[]{:S(2)}) copy-start(f32[11264]{0:T(1024)} %param.11) | copy-start | bytes 135172
  141.0 28.8 %collective-permute-start.18 = (bf16[256,1024]{1,0:T(8,128)(2,1)S(1)}, bf16[256,1024]{1,0:T(8,128)(2,1)S(1)}, u32[]{:S(2)}, u32[]{:S(2)}) collective-permute-start(bf16[256,1024]{1,0:T(8,128)(2,1)S(1)} %get-tuple-element.138), channel_id=1, source_target_pairs={{0,1},{1,0},{2,3},{3,2},{4,5},{5,4},{6,7},{7,6},{8,9},{9,8},{10,11... | collective-permute-start | bytes 1572872 | tf_op jit(solution)/shard_map/ppermute | solution.py:581
  145.8 14.7 %collective-permute-start.16 = (bf16[128,1024]{1,0:T(8,128)(2,1)S(1)}, bf16[128,1024]{1,0:T(8,128)(2,1)S(1)}, u32[]{:S(2)}, u32[]{:S(2)}) collective-permute-start(bf16[128,1024]{1,0:T(8,128)(2,1)S(1)} %get-tuple-element.132), channel_id=1, source_target_pairs={{0,2},{1,3},{2,0},{3,1},{4,6},{5,7},{6,4},{7,5},{8,10},{9,11},{10,... | collective-permute-start | bytes 786440 | tf_op jit(solution)/shard_map/ppermute | solution.py:589
  152.1 9.6 %collective-permute-start.17 = (bf16[64,2048]{1,0:T(8,128)(2,1)S(1)}, bf16[64,2048]{1,0:T(8,128)(2,1)S(1)}, u32[]{:S(2)}, u32[]{:S(2)}) collective-permute-start(bf16[64,2048]{1,0:T(8,128)(2,1)S(1)} %get-tuple-element.134), channel_id=1, source_target_pairs={{0,4},{1,5},{2,6},{3,7},{8,12},{9,13},{10,14},{11,15},{20,16},{21,... | collective-permute-start | bytes 786440 | tf_op jit(solution)/shard_map/ppermute | solution.py:594
  159.1 12.0 %collective-permute-start.19 = (bf16[128,1024]{1,0:T(8,128)(2,1)S(1)}, bf16[128,1024]{1,0:T(8,128)(2,1)S(1)}, u32[]{:S(2)}, u32[]{:S(2)}) collective-permute-start(bf16[128,1024]{1,0:T(8,128)(2,1)S(1)} %get-tuple-element.140), channel_id=1, source_target_pairs={{0,2},{1,3},{2,0},{3,1},{4,6},{5,7},{6,4},{7,5},{8,10},{9,11},{10,... | collective-permute-start | bytes 786440 | tf_op jit(solution)/shard_map/ppermute | solution.py:589
  159.2 12.0 %collective-permute-start.20 = (bf16[64,2048]{1,0:T(8,128)(2,1)S(1)}, bf16[64,2048]{1,0:T(8,128)(2,1)S(1)}, u32[]{:S(2)}, u32[]{:S(2)}) collective-permute-start(bf16[64,2048]{1,0:T(8,128)(2,1)S(1)} %get-tuple-element.142), channel_id=1, source_target_pairs={{0,4},{1,5},{2,6},{3,7},{8,12},{9,13},{10,14},{11,15},{20,16},{21,... | collective-permute-start | bytes 786440 | tf_op jit(solution)/shard_map/ppermute | solution.py:594
  160.5 23.6 %collective-permute-start.21 = (bf16[256,1024]{1,0:T(8,128)(2,1)S(1)}, bf16[256,1024]{1,0:T(8,128)(2,1)S(1)}, u32[]{:S(2)}, u32[]{:S(2)}) collective-permute-start(bf16[256,1024]{1,0:T(8,128)(2,1)S(1)} %get-tuple-element.146), channel_id=1, source_target_pairs={{0,1},{1,0},{2,3},{3,2},{4,5},{5,4},{6,7},{7,6},{8,9},{9,8},{10,11... | collective-permute-start | bytes 1572872 | tf_op jit(solution)/shard_map/ppermute | solution.py:581
  165.4 15.3 %collective-permute-start.22 = (bf16[128,1024]{1,0:T(8,128)(2,1)S(1)}, bf16[128,1024]{1,0:T(8,128)(2,1)S(1)}, u32[]{:S(2)}, u32[]{:S(2)}) collective-permute-start(bf16[128,1024]{1,0:T(8,128)(2,1)S(1)} %get-tuple-element.148), channel_id=1, source_target_pairs={{0,2},{1,3},{2,0},{3,1},{4,6},{5,7},{6,4},{7,5},{8,10},{9,11},{10,... | collective-permute-start | bytes 786440 | tf_op jit(solution)/shard_map/ppermute | solution.py:589
  169.8 9.2 %collective-permute-start.23 = (bf16[64,1024]{1,0:T(8,128)(2,1)S(1)}, bf16[64,1024]{1,0:T(8,128)(2,1)S(1)}, u32[]{:S(2)}, u32[]{:S(2)}) collective-permute-start(bf16[64,1024]{1,0:T(8,128)(2,1)S(1)} %get-tuple-element.150), channel_id=1, source_target_pairs={{0,4},{1,5},{2,6},{3,7},{4,0},{5,1},{6,2},{7,3},{8,12},{9,13},{10,... | collective-permute-start | bytes 393224 | tf_op jit(solution)/shard_map/ppermute | solution.py:596
  171.1 21.2 %collective-permute-start.26 = (bf16[256,1024]{1,0:T(8,128)(2,1)S(1)}, bf16[256,1024]{1,0:T(8,128)(2,1)S(1)}, u32[]{:S(2)}, u32[]{:S(2)}) collective-permute-start(bf16[256,1024]{1,0:T(8,128)(2,1)S(1)} %get-tuple-element.157), channel_id=1, source_target_pairs={{0,1},{1,0},{2,3},{3,2},{4,5},{5,4},{6,7},{7,6},{8,9},{9,8},{10,11... | collective-permute-start | bytes 1572872 | tf_op jit(solution)/shard_map/ppermute | solution.py:581
  171.2 7.0 %slice-start.2 = ((f32[11264]{0:T(1024)}), f32[4096]{0:T(1024)S(1)}, s32[]{:S(2)}) async-start(f32[11264]{0:T(1024)} %param.11), calls=%async_computation.3 | async-start | bytes 32768 | tf_op jit(solution)/shard_map/slice | solution.py:509
  174.1 21.1 %collective-permute-start.27 = (bf16[128,1024]{1,0:T(8,128)(2,1)S(1)}, bf16[128,1024]{1,0:T(8,128)(2,1)S(1)}, u32[]{:S(2)}, u32[]{:S(2)}) collective-permute-start(bf16[128,1024]{1,0:T(8,128)(2,1)S(1)} %get-tuple-element.159), channel_id=1, source_target_pairs={{0,2},{1,3},{2,0},{3,1},{4,6},{5,7},{6,4},{7,5},{8,10},{9,11},{10,... | collective-permute-start | bytes 786440 | tf_op jit(solution)/shard_map/ppermute | solution.py:589
  179.0 18.9 %collective-permute-start.29 = (bf16[256,512]{1,0:T(8,128)(2,1)S(1)}, bf16[256,512]{1,0:T(8,128)(2,1)S(1)}, u32[]{:S(2)}, u32[]{:S(2)}) collective-permute-start(bf16[256,512]{1,0:T(8,128)(2,1)S(1)} %get-tuple-element.163), channel_id=1, source_target_pairs={{0,1},{1,0},{2,3},{3,2},{4,5},{5,4},{6,7},{7,6},{8,9},{9,8},{10,11... | collective-permute-start | bytes 786440 | tf_op jit(solution)/shard_map/ppermute | solution.py:581
  180.7 9.5 %collective-permute-start.24 = (bf16[64,1024]{1,0:T(8,128)(2,1)S(1)}, bf16[64,1024]{1,0:T(8,128)(2,1)S(1)}, u32[]{:S(2)}, u32[]{:S(2)}) collective-permute-start(bf16[64,1024]{1,0:T(8,128)(2,1)S(1)} %get-tuple-element.153), channel_id=1, source_target_pairs={{0,4},{1,5},{2,6},{3,7},{4,0},{5,1},{6,2},{7,3},{8,12},{9,13},{10,... | collective-permute-start | bytes 393224 | tf_op jit(solution)/shard_map/ppermute | solution.py:596
  184.1 4.1 %copy-start.14 = (f32[1024]{0:T(1024)S(1)}, f32[1024]{0:T(1024)}, u32[]{:S(2)}) copy-start(f32[1024]{0:T(1024)} %get-tuple-element.210) | copy-start | bytes 12292
  184.1 6.1 %copy-start.13 = (f32[1024]{0:T(1024)S(1)}, f32[1024]{0:T(1024)}, u32[]{:S(2)}) copy-start(f32[1024]{0:T(1024)} %get-tuple-element.209) | copy-start | bytes 12292
  184.1 12.8 %copy-start.12 = (f32[1024]{0:T(1024)S(1)}, f32[1024]{0:T(1024)}, u32[]{:S(2)}) copy-start(f32[1024]{0:T(1024)} %get-tuple-element.208) | copy-start | bytes 12292
  188.1 22.3 %copy-start.11 = (f32[1024]{0:T(1024)S(1)}, f32[1024]{0:T(1024)}, u32[]{:S(2)}) copy-start(f32[1024]{0:T(1024)} %get-tuple-element.207) | copy-start | bytes 12292
  188.1 22.3 %collective-permute-start.32 = (bf16[256,512]{1,0:T(8,128)(2,1)S(1)}, bf16[256,512]{1,0:T(8,128)(2,1)S(1)}, u32[]{:S(2)}, u32[]{:S(2)}) collective-permute-start(bf16[256,512]{1,0:T(8,128)(2,1)S(1)} %get-tuple-element.170), channel_id=1, source_target_pairs={{0,1},{1,0},{2,3},{3,2},{4,5},{5,4},{6,7},{7,6},{8,9},{9,8},{10,11... | collective-permute-start | bytes 786440 | tf_op jit(solution)/shard_map/ppermute | solution.py:581
  188.2 29.5 %copy-start.10 = (f32[1024]{0:T(1024)S(1)}, f32[1024]{0:T(1024)}, u32[]{:S(2)}) copy-start(f32[1024]{0:T(1024)} %get-tuple-element.206) | copy-start | bytes 12292
  190.2 6.0 %collective-permute-start.25 = (bf16[64,1024]{1,0:T(8,128)(2,1)S(1)}, bf16[64,1024]{1,0:T(8,128)(2,1)S(1)}, u32[]{:S(2)}, u32[]{:S(2)}) collective-permute-start(bf16[64,1024]{1,0:T(8,128)(2,1)S(1)} %get-tuple-element.155), channel_id=1, source_target_pairs={{0,4},{1,5},{2,6},{3,7},{4,0},{5,1},{6,2},{7,3},{8,12},{9,13},{10,... | collective-permute-start | bytes 393224 | tf_op jit(solution)/shard_map/ppermute | solution.py:596
  192.3 13.0 %collective-permute-start.30 = (bf16[128,1024]{1,0:T(8,128)(2,1)S(1)}, bf16[128,1024]{1,0:T(8,128)(2,1)S(1)}, u32[]{:S(2)}, u32[]{:S(2)}) collective-permute-start(bf16[128,1024]{1,0:T(8,128)(2,1)S(1)} %get-tuple-element.165), channel_id=1, source_target_pairs={{0,2},{1,3},{2,0},{3,1},{4,6},{5,7},{6,4},{7,5},{8,10},{9,11},{10,... | collective-permute-start | bytes 786440 | tf_op jit(solution)/shard_map/ppermute | solution.py:589
  195.3 29.2 %copy-start.9 = (f32[1024]{0:T(1024)S(1)}, f32[1024]{0:T(1024)}, u32[]{:S(2)}) copy-start(f32[1024]{0:T(1024)} %get-tuple-element.205) | copy-start | bytes 12292
  195.5 17.2 %collective-permute-start.33 = (bf16[128,1024]{1,0:T(8,128)(2,1)S(1)}, bf16[128,1024]{1,0:T(8,128)(2,1)S(1)}, u32[]{:S(2)}, u32[]{:S(2)}) collective-permute-start(bf16[128,1024]{1,0:T(8,128)(2,1)S(1)} %get-tuple-element.172), channel_id=1, source_target_pairs={{0,2},{1,3},{2,0},{3,1},{4,6},{5,7},{6,4},{7,5},{8,10},{9,11},{10,... | collective-permute-start | bytes 786440 | tf_op jit(solution)/shard_map/ppermute | solution.py:589
  196.2 14.2 %collective-permute-start.28 = (bf16[64,1024]{1,0:T(8,128)(2,1)S(1)}, bf16[64,1024]{1,0:T(8,128)(2,1)S(1)}, u32[]{:S(2)}, u32[]{:S(2)}) collective-permute-start(bf16[64,1024]{1,0:T(8,128)(2,1)S(1)} %get-tuple-element.161), channel_id=1, source_target_pairs={{0,4},{1,5},{2,6},{3,7},{4,0},{5,1},{6,2},{7,3},{8,12},{9,13},{10,... | collective-permute-start | bytes 393224 | tf_op jit(solution)/shard_map/ppermute | solution.py:596
  205.4 12.2 %collective-permute-start.35 = (bf16[128,512]{1,0:T(8,128)(2,1)S(1)}, bf16[128,512]{1,0:T(8,128)(2,1)S(1)}, u32[]{:S(2)}, u32[]{:S(2)}) collective-permute-start(bf16[128,512]{1,0:T(8,128)(2,1)S(1)} %get-tuple-element.176), channel_id=1, source_target_pairs={{0,2},{1,3},{2,0},{3,1},{4,6},{5,7},{6,4},{7,5},{8,10},{9,11},{10,... | collective-permute-start | bytes 393224 | tf_op jit(solution)/shard_map/ppermute | solution.py:589
  205.5 12.3 %collective-permute-start.31 = (bf16[64,1024]{1,0:T(8,128)(2,1)S(1)}, bf16[64,1024]{1,0:T(8,128)(2,1)S(1)}, u32[]{:S(2)}, u32[]{:S(2)}) collective-permute-start(bf16[64,1024]{1,0:T(8,128)(2,1)S(1)} %get-tuple-element.167), channel_id=1, source_target_pairs={{0,4},{1,5},{2,6},{3,7},{4,0},{5,1},{6,2},{7,3},{8,12},{9,13},{10,... | collective-permute-start | bytes 393224 | tf_op jit(solution)/shard_map/ppermute | solution.py:596
  212.8 7.8 %collective-permute-start.37 = (bf16[128,512]{1,0:T(8,128)(2,1)S(1)}, bf16[128,512]{1,0:T(8,128)(2,1)S(1)}, u32[]{:S(2)}, u32[]{:S(2)}) collective-permute-start(bf16[128,512]{1,0:T(8,128)(2,1)S(1)} %get-tuple-element.180), channel_id=1, source_target_pairs={{0,2},{1,3},{2,0},{3,1},{4,6},{5,7},{6,4},{7,5},{8,10},{9,11},{10,... | collective-permute-start | bytes 393224 | tf_op jit(solution)/shard_map/ppermute | solution.py:589
  213.9 10.6 %collective-permute-start.34 = (bf16[64,1024]{1,0:T(8,128)(2,1)S(1)}, bf16[64,1024]{1,0:T(8,128)(2,1)S(1)}, u32[]{:S(2)}, u32[]{:S(2)}) collective-permute-start(bf16[64,1024]{1,0:T(8,128)(2,1)S(1)} %get-tuple-element.174), channel_id=1, source_target_pairs={{0,4},{1,5},{2,6},{3,7},{4,0},{5,1},{6,2},{7,3},{8,12},{9,13},{10,... | collective-permute-start | bytes 393224 | tf_op jit(solution)/shard_map/ppermute | solution.py:596
  217.7 7.5 %collective-permute-start.36 = (bf16[64,512]{1,0:T(8,128)(2,1)S(1)}, bf16[64,512]{1,0:T(8,128)(2,1)S(1)}, u32[]{:S(2)}, u32[]{:S(2)}) collective-permute-start(bf16[64,512]{1,0:T(8,128)(2,1)S(1)} %get-tuple-element.178), channel_id=1, source_target_pairs={{0,4},{1,5},{2,6},{3,7},{4,0},{5,1},{6,2},{7,3},{8,12},{9,13},{10,... | collective-permute-start | bytes 196616 | tf_op jit(solution)/shard_map/ppermute | solution.py:596
  220.7 5.9 %collective-permute-start.38 = (bf16[64,512]{1,0:T(8,128)(2,1)S(1)}, bf16[64,512]{1,0:T(8,128)(2,1)S(1)}, u32[]{:S(2)}, u32[]{:S(2)}) collective-permute-start(bf16[64,512]{1,0:T(8,128)(2,1)S(1)} %get-tuple-element.182), channel_id=1, source_target_pairs={{0,4},{1,5},{2,6},{3,7},{4,0},{5,1},{6,2},{7,3},{8,12},{9,13},{10,... | collective-permute-start | bytes 196616 | tf_op jit(solution)/shard_map/ppermute | solution.py:596
  226.6 12.0 %copy-start.7 = (f32[64,11264]{1,0:T(8,128)}, f32[64,11264]{1,0:T(8,128)S(1)}, u32[]{:S(2)}) copy-start(f32[64,11264]{1,0:T(8,128)S(1)} %get-tuple-element.200) | copy-start | bytes 8650756
  226.6 4.1 %collective-permute-start.39 = (f32[11264]{0:T(1024)S(1)}, f32[11264]{0:T(1024)S(1)}, u32[]{:S(2)}, u32[]{:S(2)}) collective-permute-start(f32[11264]{0:T(1024)S(1)} %constant_dynamic-update-slice_fusion.2), channel_id=1, source_target_pairs={{0,1},{1,0},{2,3},{3,2},{4,5},{5,4},{6,7},{7,6},{8,9},{9,8},{10,11... | collective-permute-start | bytes 135176 | tf_op jit(solution)/shard_map/ppermute | solution.py:455
  230.8 5.9 %collective-permute-start.42 = (f32[11264]{0:T(1024)S(1)}, f32[11264]{0:T(1024)S(1)}, u32[]{:S(2)}, u32[]{:S(2)}) collective-permute-start(f32[11264]{0:T(1024)S(1)} %max.12), channel_id=1, source_target_pairs={{0,6},{1,7},{2,4},{3,5},{4,2},{5,3},{6,0},{7,1},{8,14},{9,15},{10,... | collective-permute-start | bytes 135176 | tf_op jit(solution)/shard_map/ppermute | solution.py:455
  233.0 4.9 %collective-permute-start.41 = (f32[11264]{0:T(1024)S(1)}, f32[11264]{0:T(1024)S(1)}, u32[]{:S(2)}, u32[]{:S(2)}) collective-permute-start(f32[11264]{0:T(1024)S(1)} %max.12), channel_id=1, source_target_pairs={{0,4},{1,5},{2,6},{3,7},{4,0},{5,1},{6,2},{7,3},{8,12},{9,13},{10,... | collective-permute-start | bytes 135176 | tf_op jit(solution)/shard_map/ppermute | solution.py:455
  233.0 4.9 %collective-permute-start.40 = (f32[11264]{0:T(1024)S(1)}, f32[11264]{0:T(1024)S(1)}, u32[]{:S(2)}, u32[]{:S(2)}) collective-permute-start(f32[11264]{0:T(1024)S(1)} %max.12), channel_id=1, source_target_pairs={{0,2},{1,3},{2,0},{3,1},{4,6},{5,7},{6,4},{7,5},{8,10},{9,11},{10,... | collective-permute-start | bytes 135176 | tf_op jit(solution)/shard_map/ppermute | solution.py:455

commit v4 on v3

--- a/solution.py
+++ b/solution.py
@@ -285,24 +285,25 @@
     return shapes + [jax.ShapeDtypeStruct(array.shape, F32) for array in stages[2][:1]]
 
 
-def sums_kernel(near_ref, *refs, stages, high):
+def sums_kernel(near_ref, token_ref, *refs, stages, high):
     extra = iter(refs)
     taken = [[next(extra) for _ in range(count)] for count in stages]
     run_stages(taken, extra, near_ref[0] == 1, high)
 
 
-def sums(near, stages, high):
+def sums(near, token, stages, high):
     vmem = pl.BlockSpec(memory_space=pltpu.VMEM)
     shapes = stage_shapes(stages, high)
     return pl.pallas_call(
         functools.partial(sums_kernel, stages=[len(stage) for stage in stages], high=high),
-        in_specs=[pl.BlockSpec(memory_space=pltpu.SMEM)] + [vmem] * sum(map(len, stages)),
+        in_specs=[pl.BlockSpec(memory_space=pltpu.SMEM), pl.BlockSpec(memory_space=pl.ANY)]
+        + [vmem] * sum(map(len, stages)),
         out_specs=[vmem] * len(shapes),
         out_shape=shapes,
         compiler_params=pltpu.CompilerParams(vmem_limit_bytes=32 * 1024 * 1024),
         cost_estimate=cost(1 << 16, 1 << 10),
         name="sums",
-    )(near, *[array for stage in stages for array in stage])
+    )(near, token, *[array for stage in stages for array in stage])
 
 
 def flow_kernel(
@@ -583,7 +584,11 @@
             token = keep
         else:
             ending[t - ended], stages[2] = stages[2], ()
-            done = sums(near_flag, stages, high) if any(stages) else []
+            done = []
+            for stage in ([stages[0], (), ()], [(), stages[1], ()]):
+                if any(stage):
+                    done += sums(near_flag, token, stage, high)
+                    token = done[-1]
         done = iter(done)
         if stages[0]:
             moved[t - summed] = lax.ppermute(next(done), "bus", swaps[t - summed][1])

time: 239 us -> 237 us (level)
  waiting for transfers between devices: 70.9 us -> 76.5 us
  Pallas kernels: 94.5 us -> 90.3 us
  starting transfers between devices: 60.2 us -> 56.6 us
    ppermute x12, waiting for transfers between devices: 14.1 us -> 4.76 us  [staged(): moved[t - summed] = lax.ppermute(next(done), 'bus', swaps[t - summed][1])]
    ppermute x8, waiting for transfers between devices: 7.82 us -> 15.6 us  [staged(): late[t - shared] = lax.ppermute(next(done), 'bus', swap_far)]
    ppermute x12, waiting for transfers between devices: 22.2 us -> 28 us  [staged(): sent[t] = lax.ppermute(send, 'bus', swaps[t][0])]
    pallas_call x12, Pallas kernels: 57.7 us -> 53.5 us  [partial_flow(): pl.pallas_call(functools.partial(flow_kernel, base=base, slots=slots, hal...]
    ppermute x12, starting transfers between devices: 11.9 us -> 9.26 us  [staged(): moved[t - summed] = lax.ppermute(next(done), 'bus', swaps[t - summed][1])]
  transfers between devices with their start and end apart: 44 -> 44, of which waited for: 25 -> 25; matrix products, arithmetic and copies ran while one was open for 3% -> 3% of each run, Pallas kernels for 34% -> 32%
where the time goes in v4:
time: 237 us; the launch traced here: 236 us
  Pallas kernels  90.3 us (38%)
  waiting for transfers between devices  76.5 us (32%)
  starting transfers between devices  56.6 us (24%)
  other arithmetic  7.58 us (3%)
  local copies, waits for them, and re-layouts  4.29 us (2%)
    pallas_call x12, Pallas kernels, partial_flow(): pl.pallas_call(functools.partial(flow_kernel, base=base, slots=slots, hal...  53.5 us
    ppermute x12, waiting for transfers between devices, staged(): sent[t] = lax.ppermute(send, 'bus', swaps[t][0])  28 us
    pallas_call x2, Pallas kernels, inject(): pl.pallas_call(inject_kernel, grid_spec=pltpu.PrefetchScalarGridSpec(num_...  15.7 us
    ppermute x8, waiting for transfers between devices, staged(): late[t - shared] = lax.ppermute(next(done), 'bus', swap_far)  15.6 us
    ppermute x12, starting transfers between devices, staged(): sent[t] = lax.ppermute(send, 'bus', swaps[t][0])  14.3 us
    all_to_all x1, waiting for transfers between devices, body(): lax.all_to_all(route(here, site_bus, site_values, groups, bus_dev), 'bus'...  13.6 us
    ppermute x8, starting transfers between devices, staged(): late[t - shared] = lax.ppermute(next(done), 'bus', swap_far)  13.2 us
    ppermute x12, starting transfers between devices, staged(): moved[t - summed] = lax.ppermute(next(done), 'bus', swaps[t - summed][1])  9.26 us
  transfers between devices with their start and end apart: 44, of which 25 were waited for; matrix products, arithmetic and copies ran while one was open for 3% of the time, Pallas kernels for 32%

profile of v4, /device:TPU:0, one launch (start us, length us, event | category | flops | bytes accessed | tf_op | source)
XLA Modules:
  0.0 236.4 jit_solution(9766546661174192940)
XLA Ops:
  0.6 1.6 copy-done.4
  3.1 7.5 %route.1 = bf16[8,128,512]{2,1,0:T(8,128)(2,1)} custom-call(s32[1]{0:T(128)} %bitcast.2.here_ref, s32[256,128]{1,0:T(8,128)S(1)} %bitcast.33, f32[128,4096]{1,0:T(8,128)S(1)} %copy-done.4), custom_call_target="tpu_custom_call" | custom-call | flops 8589934592 | bytes 2097152 | tf_op jit(solution)/shard_map/route/pallas_call | solution.py:94
  10.7 7.3 %all-to-all-start = ((bf16[8,128,512]{2,1,0:T(8,128)(2,1)}), bf16[8,128,512]{2,1,0:T(8,128)(2,1)S(1)}, u32[]{:S(2)}, u32[]{:S(2)}) async-start(bf16[8,128,512]{2,1,0:T(8,128)(2,1)} %route.1), calls=%async_computation | async-start | bytes 2097152 | tf_op jit(solution)/shard_map/all_to_all | solution.py:474
  17.9 6.3 %arrivals.1 = s32[8,1,512]{2,1,0:T(1,128)S(1)} custom-call(s32[1]{0:T(128)} %bitcast.2.here_ref, s32[256,128]{1,0:T(8,128)S(1)} %bitcast.34), custom_call_target="tpu_custom_call" | custom-call | flops 1073741824 | bytes 131072 | tf_op jit(solution)/shard_map/arrivals/pallas_call | solution.py:147
  24.3 5.8 %sort.14 = (s32[4096]{0:T(1024)S(1)}, s32[4096]{0:T(1024)}) sort(s32[4096]{0:T(1024)S(1)} %iota_add_fusion, s32[4096]{0:T(1024)S(1)} %iota.20), dimensions={0}, to_apply=%region_1.2 | sort | flops 49152 | bytes 65536 | tf_op jit(solution)/shard_map/sort | solution.py:479
  30.1 13.6 %all-to-all-done.runs_ref = bf16[8,128,512]{2,1,0:T(8,128)(2,1)S(1)} async-done(((bf16[8,128,512]{2,1,0:T(8,128)(2,1)}), bf16[8,128,512]{2,1,0:T(8,128)(2,1)S(1)}, u32[]{:S(2)}, u32[]{:S(2)}) %all-to-all-start) | async-done | bytes 1048608 | tf_op jit(solution)/shard_map/all_to_all | solution.py:474
  43.7 6.5 %merge.1.refs_0_ = bf16[32,128,128]{2,1,0:T(8,128)(2,1)} custom-call(s32[8,1,512]{2,1,0:T(1,128)S(1)} %bitcast.32, bf16[8,128,512]{2,1,0:T(8,128)(2,1)S(1)} %all-to-all-done.runs_ref), custom_call_target="tpu_custom_call" | custom-call | flops 8589934592 | bytes 2097152 | tf_op jit(solution)/shard_map/merge/pallas_call | solution.py:178
  50.2 1.5 collective-permute-start.1
  53.0 8.5 %inject.2.token_ref.refs_0_.refs_1_.refs_2_ = bf16[14,256,640]{2,1,0:T(8,128)(2,1)S(1)} custom-call(s32[14]{0:T(128)S(1)} %get-tuple-element.186.first_ref, s32[14]{0:T(128)S(1)} %get-tuple-element.185.windows_ref, s32[4]{0:T(128)S(1)} %pad_add_fusion.rows_ref, s32[32,1,128]{2,1,0:T(1,128)S(1)} %bitcast.17, bf16[32,128,128]{2,1,0:T(8,128)(2,1)} %merge.1.refs_0_, ...), custom_call_target="tpu_custom_call" | custom-call | flops 65536 | bytes 1024 | tf_op jit(solution)/shard_map/inject/pallas_call | solution.py:235
  61.6 6.9 %partial_flow.12 = (bf16[128,2048]{1,0:T(8,128)(2,1)}, bf16[64,2048]{1,0:T(8,128)(2,1)S(1)}, bf16[64,2048]{1,0:T(8,128)(2,1)S(1)}) custom-call(s32[22]{0:T(128)S(1)} %bitcast.20, s32[66]{0:T(128)S(1)} %reshape.46.zone_ref, s32[66]{0:T(128)S(1)} %reshape.47.last_ref, s32[1]{0:T(128)} %bitcast.1.near_ref, ...), custom_call_target="tpu_custom_call" | custom-call | flops 1006632960 | bytes 5898240 | tf_op jit(solution)/shard_map/partial_flow/pallas_call | solution.py:385
  69.2 5.8 %partial_flow.13 = (bf16[128,2048]{1,0:T(8,128)(2,1)}, bf16[64,2048]{1,0:T(8,128)(2,1)S(1)}, bf16[64,2048]{1,0:T(8,128)(2,1)S(1)}) custom-call(s32[22]{0:T(128)S(1)} %bitcast.21, s32[66]{0:T(128)S(1)} %reshape.46.zone_ref, s32[66]{0:T(128)S(1)} %reshape.47.last_ref, s32[1]{0:T(128)} %bitcast.1.near_ref, ...), custom_call_target="tpu_custom_call" | custom-call | flops 1006632960 | bytes 5898240 | tf_op jit(solution)/shard_map/partial_flow/pallas_call | solution.py:385
  75.0 0.9 collective-permute-done.1.values_ref
  76.2 1.5 collective-permute-start.3
  78.8 7.3 %inject.3.refs_0_.refs_1_.refs_2_.refs_3_.refs_4_.refs_5_ = bf16[14,256,640]{2,1,0:T(8,128)(2,1)S(1)} custom-call(s32[14]{0:T(128)S(1)} %get-tuple-element.186.first_ref, s32[14]{0:T(128)S(1)} %get-tuple-element.185.windows_ref, s32[4]{0:T(128)S(1)} %pad_add_fusion.1.rows_ref, s32[32,1,128]{2,1,0:T(1,128)S(1)} %bitcast.18, ...), custom_call_target="tpu_custom_call" | custom-call | flops 65536 | bytes 1024 | tf_op jit(solution)/shard_map/inject/pallas_call | solution.py:235
  86.1 5.2 %partial_flow.14 = (bf16[128,2048]{1,0:T(8,128)(2,1)S(1)}, bf16[64,2048]{1,0:T(8,128)(2,1)S(1)}, bf16[64,2048]{1,0:T(8,128)(2,1)S(1)}) custom-call(s32[22]{0:T(128)S(1)} %bitcast.22, s32[66]{0:T(128)S(1)} %reshape.46.zone_ref, s32[66]{0:T(128)S(1)} %reshape.47.last_ref, s32[1]{0:T(128)} %bitcast.1.near_ref, ...), custom_call_target="tpu_custom_call" | custom-call | flops 1006632960 | bytes 5898240 | tf_op jit(solution)/shard_map/partial_flow/pallas_call | solution.py:385
  91.7 5.8 %partial_flow.15 = (bf16[128,2048]{1,0:T(8,128)(2,1)S(1)}, bf16[64,2048]{1,0:T(8,128)(2,1)S(1)}, bf16[64,2048]{1,0:T(8,128)(2,1)S(1)}, bf16[64,2048]{1,0:T(8,128)(2,1)S(1)}, bf16[64,2048]{1,0:T(8,128)(2,1)S(1)}) custom-call(s32[22]{0:T(128)S(1)} %bitcast.23, s32[66]{0:T(128)S(1)} %reshape.46.zone_ref, s32[66]{0:T(128)S(1)} %reshape.47.last_ref, ...), custom_call_target="tpu_custom_call" | custom-call | flops 1006632960 | bytes 5898240 | tf_op jit(solution)/shard_map/partial_flow/pallas_call | solution.py:385
  97.8 1.6 collective-permute-start.6
  99.3 3.1 %collective-permute-done.4.refs_11_ = bf16[128,2048]{1,0:T(8,128)(2,1)S(1)} collective-permute-done((bf16[128,2048]{1,0:T(8,128)(2,1)}, bf16[128,2048]{1,0:T(8,128)(2,1)S(1)}, u32[]{:S(2)}, u32[]{:S(2)}) %collective-permute-start.4) | collective-permute-done | bytes 524320 | tf_op jit(solution)/shard_map/ppermute | solution.py:582
  102.4 5.0 %partial_flow.16 = (bf16[256,1024]{1,0:T(8,128)(2,1)S(1)}, bf16[128,1024]{1,0:T(8,128)(2,1)S(1)}, bf16[128,1024]{1,0:T(8,128)(2,1)S(1)}, bf16[64,2048]{1,0:T(8,128)(2,1)S(1)}, bf16[64,2048]{1,0:T(8,128)(2,1)S(1)}) custom-call(s32[22]{0:T(128)S(1)} %bitcast.24, s32[66]{0:T(128)S(1)} %reshape.46.zone_ref, s32[66]{0:T(128)S(1)} %reshape.47.last_ref, ...), custom_call_target="tpu_custom_call" | custom-call | flops 1006632960 | bytes 3932160 | tf_op jit(solution)/shard_map/partial_flow/pallas_call | solution.py:385
  108.0 5.7 %collective-permute-done.5.refs_11_ = bf16[128,2048]{1,0:T(8,128)(2,1)S(1)} collective-permute-done((bf16[128,2048]{1,0:T(8,128)(2,1)S(1)}, bf16[128,2048]{1,0:T(8,128)(2,1)S(1)}, u32[]{:S(2)}, u32[]{:S(2)}) %collective-permute-start.5) | collective-permute-done | bytes 524320 | tf_op jit(solution)/shard_map/ppermute | solution.py:582
  113.6 3.1 %partial_flow.17 = (bf16[256,1024]{1,0:T(8,128)(2,1)S(1)}, bf16[128,1024]{1,0:T(8,128)(2,1)S(1)}, bf16[128,1024]{1,0:T(8,128)(2,1)S(1)}, bf16[64,2048]{1,0:T(8,1...) custom-call(s32[22]{0:T(128)S(1)} %bitcast.25, ...), custom_call_target="tpu_custom_call" | custom-call | flops 1006632960 | bytes 3932160 | tf_op jit(solution)/shard_map/partial_flow/pallas_call | solution.py:385
  116.8 1.1 collective-permute-start.10
  117.9 1.3 collective-permute-start.11
  119.2 1.8 collective-permute-start.12
  121.0 3.8 %collective-permute-done.7.refs_11_ = bf16[128,2048]{1,0:T(8,128)(2,1)S(1)} collective-permute-done((bf16[128,2048]{1,0:T(8,128)(2,1)S(1)}, bf16[128,2048]{1,0:T(8,128)(2,1)S(1)}, u32[]{:S(2)}, u32[]{:S(2)}) %collective-permute-start.7) | collective-permute-done | bytes 524320 | tf_op jit(solution)/shard_map/ppermute | solution.py:582
  124.9 5.3 %partial_flow.18 = (bf16[256,1024]{1,0:T(8,128)(2,1)S(1)}, bf16[128,1024]{1,0:T(8,128)(2,1)S(1)}, bf16[128,1024]{1,0:T(8,128)(2,1)S(1)}, bf16[64,2048]{1,0:T(8,1...) custom-call(s32[22]{0:T(128)S(1)} %bitcast.26, ...), custom_call_target="tpu_custom_call" | custom-call | flops 1006632960 | bytes 3932160 | tf_op jit(solution)/shard_map/partial_flow/pallas_call | solution.py:385
  130.5 5.6 %collective-permute-done.9.refs_11_ = bf16[256,1024]{1,0:T(8,128)(2,1)S(1)} collective-permute-done((bf16[256,1024]{1,0:T(8,128)(2,1)S(1)}, bf16[256,1024]{1,0:T(8,128)(2,1)S(1)}, u32[]{:S(2)}, u32[]{:S(2)}) %collective-permute-start.9) | collective-permute-done | bytes 524320 | tf_op jit(solution)/shard_map/ppermute | solution.py:582
  136.1 1.3 collective-permute-start.14
  137.4 3.2 %partial_flow.19 = (bf16[256,1024]{1,0:T(8,128)(2,1)S(1)}, bf16[128,1024]{1,0:T(8,128)(2,1)S(1)}, bf16[128,1024]{1,0:T(8,128)(2,1)S(1)}, bf16[128,1024]{1,0:T(8,...) custom-call(s32[22]{0:T(128)S(1)} %bitcast.27, ...), custom_call_target="tpu_custom_call" | custom-call | flops 1006632960 | bytes 3932160 | tf_op jit(solution)/shard_map/partial_flow/pallas_call | solution.py:385
  140.6 2.9 %collective-permute-start.18 = (bf16[256,1024]{1,0:T(8,128)(2,1)S(1)}, bf16[256,1024]{1,0:T(8,128)(2,1)S(1)}, u32[]{:S(2)}, u32[]{:S(2)}) collective-permute-start(bf16[256,1024]{1,0:T(8,128)(2,1)S(1)} %get-tuple-element.138), channel_id=1, source_target_pairs={{0,1},{1,0},{2,3},{3,2},{4,5},{5,4},{6,7},{7,6},{8,9},{9,8},{10,11... | collective-permute-start | bytes 1572872 | tf_op jit(solution)/shard_map/ppermute | solution.py:582
  144.1 1.8 collective-permute-done.13.refs_13_
  145.9 6.2 %collective-permute-done.14.refs_15_ = bf16[64,2048]{1,0:T(8,128)(2,1)S(1)} collective-permute-done((bf16[64,2048]{1,0:T(8,128)(2,1)S(1)}, bf16[64,2048]{1,0:T(8,128)(2,1)S(1)}, u32[]{:S(2)}, u32[]{:S(2)}) %collective-permute-start.14) | collective-permute-done | bytes 262176 | tf_op jit(solution)/shard_map/ppermute | solution.py:599
  152.1 1.4 collective-permute-start.17
  153.5 3.8 %partial_flow.20 = (bf16[256,1024]{1,0:T(8,128)(2,1)S(1)}, bf16[128,1024]{1,0:T(8,128)(2,1)S(1)}, bf16[128,1024]{1,0:T(8,128)(2,1)S(1)}, bf16[128,1024]{1,0:T(8,...) custom-call(s32[22]{0:T(128)S(1)} %bitcast.28, ...), custom_call_target="tpu_custom_call" | custom-call | flops 1006632960 | bytes 3932160 | tf_op jit(solution)/shard_map/partial_flow/pallas_call | solution.py:385
  157.4 1.2 collective-permute-done.15.refs_11_
  158.6 1.6 collective-permute-start.20
  160.2 2.0 collective-permute-start.21
  162.2 3.8 %partial_flow.21 = (bf16[256,1024]{1,0:T(8,128)(2,1)S(1)}, bf16[128,1024]{1,0:T(8,128)(2,1)S(1)}, bf16[128,1024]{1,0:T(8,128)(2,1)S(1)}, bf16[128,1024]{1,0:T(8,...) custom-call(s32[22]{0:T(128)S(1)} %bitcast.29, ...), custom_call_target="tpu_custom_call" | custom-call | flops 1006632960 | bytes 3932160 | tf_op jit(solution)/shard_map/partial_flow/pallas_call | solution.py:385
  166.0 3.5 %collective-permute-start.22 = (bf16[128,1024]{1,0:T(8,128)(2,1)S(1)}, bf16[128,1024]{1,0:T(8,128)(2,1)S(1)}, u32[]{:S(2)}, u32[]{:S(2)}) collective-permute-start(bf16[128,1024]{1,0:T(8,128)(2,1)S(1)} %get-tuple-element.148), channel_id=1, source_target_pairs={{0,2},{1,3},{2,0},{3,1},{4,6},{5,7},{6,4},{7,5},{8,10},{9,11},{10,... | collective-permute-start | bytes 786440 | tf_op jit(solution)/shard_map/ppermute | solution.py:594
  169.8 1.6 collective-permute-start.26
  171.5 2.9 %partial_flow.22 = (bf16[256,512]{1,0:T(8,128)(2,1)S(1)}, bf16[128,512]{1,0:T(8,128)(2,1)S(1)}, bf16[128,512]{1,0:T(8,128)(2,1)S(1)}, bf16[128,1024]{1,0:T(8,128...) custom-call(s32[22]{0:T(128)S(1)} %bitcast.30, ...), custom_call_target="tpu_custom_call" | custom-call | flops 503316480 | bytes 1966080 | tf_op jit(solution)/shard_map/partial_flow/pallas_call | solution.py:385
  174.4 2.7 %collective-permute-start.27 = (bf16[128,1024]{1,0:T(8,128)(2,1)S(1)}, bf16[128,1024]{1,0:T(8,128)(2,1)S(1)}, u32[]{:S(2)}, u32[]{:S(2)}) collective-permute-start(bf16[128,1024]{1,0:T(8,128)(2,1)S(1)} %get-tuple-element.161), channel_id=1, source_target_pairs={{0,2},{1,3},{2,0},{3,1},{4,6},{5,7},{6,4},{7,5},{8,10},{9,11},{10,... | collective-permute-start | bytes 786440 | tf_op jit(solution)/shard_map/ppermute | solution.py:594
  177.3 1.7 collective-permute-done.23.refs_15_
  179.0 1.0 collective-permute-start.29
  180.1 3.4 %collective-permute-start.24 = (bf16[64,1024]{1,0:T(8,128)(2,1)S(1)}, bf16[64,1024]{1,0:T(8,128)(2,1)S(1)}, u32[]{:S(2)}, u32[]{:S(2)}) collective-permute-start(bf16[64,1024]{1,0:T(8,128)(2,1)S(1)} %get-tuple-element.153), channel_id=1, source_target_pairs={{0,4},{1,5},{2,6},{3,7},{4,0},{5,1},{6,2},{7,3},{8,12},{9,13},{10,... | collective-permute-start | bytes 393224 | tf_op jit(solution)/shard_map/ppermute | solution.py:601
  183.5 2.6 %partial_flow.23 = (bf16[256,512]{1,0:T(8,128)(2,1)S(1)}, bf16[128,512]{1,0:T(8,128)(2,1)S(1)}, bf16[128,512]{1,0:T(8,128)(2,1)S(1)}, bf16[128,1024]{1,0:T(8,128...) custom-call(s32[22]{0:T(128)S(1)} %bitcast.31, ...), custom_call_target="tpu_custom_call" | custom-call | flops 503316480 | bytes 1966080 | tf_op jit(solution)/shard_map/partial_flow/pallas_call | solution.py:385
  186.2 1.7 collective-permute-done.24
  187.9 2.9 %collective-permute-start.25 = (bf16[64,1024]{1,0:T(8,128)(2,1)S(1)}, bf16[64,1024]{1,0:T(8,128)(2,1)S(1)}, u32[]{:S(2)}, u32[]{:S(2)}) collective-permute-start(bf16[64,1024]{1,0:T(8,128)(2,1)S(1)} %get-tuple-element.155), channel_id=1, source_target_pairs={{0,4},{1,5},{2,6},{3,7},{4,0},{5,1},{6,2},{7,3},{8,12},{9,13},{10,... | collective-permute-start | bytes 393224 | tf_op jit(solution)/shard_map/ppermute | solution.py:601
  190.9 1.3 collective-permute-done.26.refs_2_
  192.3 1.4 collective-permute-start.32
  194.0 3.9 %collective-permute-done.29.refs_2_ = bf16[256,512]{1,0:T(8,128)(2,1)S(1)} collective-permute-done((bf16[256,512]{1,0:T(8,128)(2,1)S(1)}, bf16[256,512]{1,0:T(8,128)(2,1)S(1)}, u32[]{:S(2)}, u32[]{:S(2)}) %collective-permute-start.29) | collective-permute-done | bytes 262176 | tf_op jit(solution)/shard_map/ppermute | solution.py:582
  198.1 1.7 collective-permute-start.28
  199.9 3.2 %collective-permute-done.32.refs_2_ = bf16[256,512]{1,0:T(8,128)(2,1)S(1)} collective-permute-done((bf16[256,512]{1,0:T(8,128)(2,1)S(1)}, bf16[256,512]{1,0:T(8,128)(2,1)S(1)}, u32[]{:S(2)}, u32[]{:S(2)}) %collective-permute-start.32) | collective-permute-done | bytes 262176 | tf_op jit(solution)/shard_map/ppermute | solution.py:582
  203.2 1.7 collective-permute-start.31
  204.9 2.0 collective-permute-done.28
  207.1 3.0 %collective-permute-done.35.refs_1_ = bf16[128,512]{1,0:T(8,128)(2,1)S(1)} collective-permute-done((bf16[128,512]{1,0:T(8,128)(2,1)S(1)}, bf16[128,512]{1,0:T(8,128)(2,1)S(1)}, u32[]{:S(2)}, u32[]{:S(2)}) %collective-permute-start.35) | collective-permute-done | bytes 131104 | tf_op jit(solution)/shard_map/ppermute | solution.py:594
  210.6 2.5 %collective-permute-start.34 = (bf16[64,1024]{1,0:T(8,128)(2,1)S(1)}, bf16[64,1024]{1,0:T(8,128)(2,1)S(1)}, u32[]{:S(2)}, u32[]{:S(2)}) collective-permute-start(bf16[64,1024]{1,0:T(8,128)(2,1)S(1)} %get-tuple-element.176), channel_id=1, source_target_pairs={{0,4},{1,5},{2,6},{3,7},{4,0},{5,1},{6,2},{7,3},{8,12},{9,13},{10,... | collective-permute-start | bytes 393224 | tf_op jit(solution)/shard_map/ppermute | solution.py:601
  213.7 5.4 %collective-permute-done.31 = bf16[64,1024]{1,0:T(8,128)(2,1)S(1)} collective-permute-done((bf16[64,1024]{1,0:T(8,128)(2,1)S(1)}, bf16[64,1024]{1,0:T(8,128)(2,1)S(1)}, u32[]{:S(2)}, u32[]{:S(2)}) %collective-permute-start.31) | collective-permute-done | bytes 131104 | tf_op jit(solution)/shard_map/ppermute | solution.py:601
  219.1 4.1 %collective-permute-done.34 = bf16[64,1024]{1,0:T(8,128)(2,1)S(1)} collective-permute-done((bf16[64,1024]{1,0:T(8,128)(2,1)S(1)}, bf16[64,1024]{1,0:T(8,128)(2,1)S(1)}, u32[]{:S(2)}, u32[]{:S(2)}) %collective-permute-start.34) | collective-permute-done | bytes 131104 | tf_op jit(solution)/shard_map/ppermute | solution.py:601
  225.0 3.2 %collective-permute-done.39 = f32[11264]{0:T(1024)S(1)} collective-permute-done((f32[11264]{0:T(1024)S(1)}, f32[11264]{0:T(1024)S(1)}, u32[]{:S(2)}, u32[]{:S(2)}) %collective-permute-start.39) | collective-permute-done | bytes 45088 | tf_op jit(solution)/shard_map/ppermute | solution.py:456
  228.2 2.7 %collective-permute-start.42 = (f32[11264]{0:T(1024)S(1)}, f32[11264]{0:T(1024)S(1)}, u32[]{:S(2)}, u32[]{:S(2)}) collective-permute-start(f32[11264]{0:T(1024)S(1)} %max.12), channel_id=1, source_target_pairs={{0,6},{1,7},{2,4},{3,5},{4,2},{5,3},{6,0},{7,1},{8,14},{9,15},{10,... | collective-permute-start | bytes 135176 | tf_op jit(solution)/shard_map/ppermute | solution.py:456
  230.8 1.8 collective-permute-start.40
  232.6 1.8 collective-permute-done.42
  234.4 1.3 collective-permute-done.41
  (127 shorter events, 11.6 us)
Async XLA Ops:
  0.6 1.6 copy-start.4
  2.2 0.9 copy-start.5
  3.1 14.8 %copy-start.6 = (s32[32768]{0:T(1024)S(1)}, s32[32768]{0:T(1024)}, u32[]{:S(2)}) copy-start(s32[32768]{0:T(1024)} %param.7) | copy-start | bytes 393220
  10.7 33.0 %all-to-all-start = ((bf16[8,128,512]{2,1,0:T(8,128)(2,1)}), bf16[8,128,512]{2,1,0:T(8,128)(2,1)S(1)}, u32[]{:S(2)}, u32[]{:S(2)}) async-start(bf16[8,128,512]{2,1,0:T(8,128)(2,1)} %route.1), calls=%async_computation | async-start | bytes 2097152 | tf_op jit(solution)/shard_map/all_to_all | solution.py:474
  43.7 8.0 %copy-start.15 = (s32[22,3]{0,1:T(4,128)S(1)}, s32[22,3]{0,1:T(4,128)}, u32[]{:S(2)}) copy-start(s32[22,3]{0,1:T(4,128)} %param.9) | copy-start | bytes 796
  43.7 8.2 %copy-start.3 = (s32[22,1]{0,1:T(1,128)S(1)}, s32[22,1]{0,1:T(1,128)}, u32[]{:S(2)}) copy-start(s32[22,1]{0,1:T(1,128)} %param.8) | copy-start | bytes 268
  50.2 2.9 %collective-permute-start = (bf16[32,128,128]{2,1,0:T(8,128)(2,1)}, bf16[32,128,128]{2,1,0:T(8,128)(2,1)S(1)}, u32[]{:S(2)}, u32[]{:S(2)}) collective-permute-start(bf16[32,128,128]{2,1,0:T(8,128)(2,1)} %merge.1.refs_0_), channel_id=1, source_target_pairs={{0,8},{8,0},{16,24},{24,16},{1,9},{9,1},{17,25},{25,17},{2,10},{10... | collective-permute-start | bytes 3145736 | tf_op jit(solution)/shard_map/ppermute | solution.py:542
  50.2 25.8 %collective-permute-start.1 = (bf16[32,128,128]{2,1,0:T(8,128)(2,1)}, bf16[32,128,128]{2,1,0:T(8,128)(2,1)S(1)}, u32[]{:S(2)}, u32[]{:S(2)}) collective-permute-start(bf16[32,128,128]{2,1,0:T(8,128)(2,1)} %merge.1.refs_0_), channel_id=1, source_target_pairs={{0,16},{8,24},{16,0},{24,8},{1,17},{9,25},{17,1},{25,9},{2,18},{10... | collective-permute-start | bytes 3145736 | tf_op jit(solution)/shard_map/ppermute | solution.py:541
  61.5 7.7 %copy-start = (bf16[14,256,640]{2,1,0:T(8,128)(2,1)}, bf16[14,256,640]{2,1,0:T(8,128)(2,1)S(1)}, u32[]{:S(2)}) copy-start(bf16[14,256,640]{2,1,0:T(8,128)(2,1)S(1)} %inject.2.token_ref.refs_0_.refs_1_.refs_2_) | copy-start | bytes 13762564
  68.5 0.7 copy-start.1
  76.1 2.7 %collective-permute-start.2 = (bf16[32,128,128]{2,1,0:T(8,128)(2,1)S(1)}, bf16[32,128,128]{2,1,0:T(8,128)(2,1)S(1)}, u32[]{:S(2)}, u32[]{:S(2)}) collective-permute-start(bf16[32,128,128]{2,1,0:T(8,128)(2,1)S(1)} %copy_after.1.refs_0_), channel_id=1, source_target_pairs={{0,8},{8,0},{16,24},{24,16},{1,9},{9,1},{17,25},{25,17},{2,10},{10... | collective-permute-start | bytes 3145736 | tf_op jit(solution)/shard_map/ppermute | solution.py:569
  76.2 15.5 %collective-permute-start.3 = (bf16[128,2048]{1,0:T(8,128)(2,1)}, bf16[128,2048]{1,0:T(8,128)(2,1)}, u32[]{:S(2)}, u32[]{:S(2)}) collective-permute-start(bf16[128,2048]{1,0:T(8,128)(2,1)} %get-tuple-element.98), channel_id=1, source_target_pairs={{0,1},{1,0},{2,3},{3,2},{4,5},{5,4},{6,7},{7,6},{8,9},{9,8},{10,11... | collective-permute-start | bytes 1572872 | tf_op jit(solution)/shard_map/ppermute | solution.py:582
  77.7 24.7 %collective-permute-start.4 = (bf16[128,2048]{1,0:T(8,128)(2,1)}, bf16[128,2048]{1,0:T(8,128)(2,1)S(1)}, u32[]{:S(2)}, u32[]{:S(2)}) collective-permute-start(bf16[128,2048]{1,0:T(8,128)(2,1)} %get-tuple-element.101), channel_id=1, source_target_pairs={{0,1},{1,0},{2,3},{3,2},{4,5},{5,4},{6,7},{7,6},{8,9},{9,8},{10,11... | collective-permute-start | bytes 1572872 | tf_op jit(solution)/shard_map/ppermute | solution.py:582
  86.1 5.6 %copy-start.2 = (bf16[64,2048]{1,0:T(8,128)(2,1)S(1)}, bf16[64,2048]{1,0:T(8,128)(2,1)}, u32[]{:S(2)}) copy-start(bf16[64,2048]{1,0:T(8,128)(2,1)} %copy-done.1) | copy-start | bytes 786436
  91.3 22.3 %collective-permute-start.5 = (bf16[128,2048]{1,0:T(8,128)(2,1)S(1)}, bf16[128,2048]{1,0:T(8,128)(2,1)S(1)}, u32[]{:S(2)}, u32[]{:S(2)}) collective-permute-start(bf16[128,2048]{1,0:T(8,128)(2,1)S(1)} %get-tuple-element.104), channel_id=1, source_target_pairs={{0,1},{1,0},{2,3},{3,2},{4,5},{5,4},{6,7},{7,6},{8,9},{9,8},{10,11... | collective-permute-start | bytes 1572872 | tf_op jit(solution)/shard_map/ppermute | solution.py:582
  91.7 10.7 %slice-start = ((s8[4587520]{0:T(1024)(128)(4,1)}), s8[4194304]{0:T(1024)(128)(4,1)S(1)}, s32[]{:S(2)}) async-start(s8[4587520]{0:T(1024)(128)(4,1)} %bitcast.15), calls=%async_computation.1 | async-start | bytes 8388608
  91.7 10.7 %slice-start.1 = ((s8[4587520]{0:T(1024)(128)(4,1)}), s8[393216]{0:T(1024)(128)(4,1)S(1)}, s32[]{:S(2)}) async-start(s8[4587520]{0:T(1024)(128)(4,1)} %bitcast.15), calls=%async_computation.2 | async-start | bytes 786432
  97.5 27.4 %collective-permute-start.7 = (bf16[128,2048]{1,0:T(8,128)(2,1)S(1)}, bf16[128,2048]{1,0:T(8,128)(2,1)S(1)}, u32[]{:S(2)}, u32[]{:S(2)}) collective-permute-start(bf16[128,2048]{1,0:T(8,128)(2,1)S(1)} %get-tuple-element.109), channel_id=1, source_target_pairs={{0,1},{1,0},{2,3},{3,2},{4,5},{5,4},{6,7},{7,6},{8,9},{9,8},{10,11... | collective-permute-start | bytes 1572872 | tf_op jit(solution)/shard_map/ppermute | solution.py:582
  97.8 10.2 %collective-permute-start.6 = (bf16[64,2048]{1,0:T(8,128)(2,1)S(1)}, bf16[64,2048]{1,0:T(8,128)(2,1)S(1)}, u32[]{:S(2)}, u32[]{:S(2)}) collective-permute-start(bf16[64,2048]{1,0:T(8,128)(2,1)S(1)} %get-tuple-element.106), channel_id=1, source_target_pairs={{0,2},{1,3},{2,0},{3,1},{4,6},{5,7},{6,4},{7,5},{8,10},{9,11},{10,... | collective-permute-start | bytes 786440 | tf_op jit(solution)/shard_map/ppermute | solution.py:594
  107.4 28.7 %collective-permute-start.9 = (bf16[256,1024]{1,0:T(8,128)(2,1)S(1)}, bf16[256,1024]{1,0:T(8,128)(2,1)S(1)}, u32[]{:S(2)}, u32[]{:S(2)}) collective-permute-start(bf16[256,1024]{1,0:T(8,128)(2,1)S(1)} %get-tuple-element.114), channel_id=1, source_target_pairs={{0,1},{1,0},{2,3},{3,2},{4,5},{5,4},{6,7},{7,6},{8,9},{9,8},{10,11... | collective-permute-start | bytes 1572872 | tf_op jit(solution)/shard_map/ppermute | solution.py:582
  108.0 11.2 %collective-permute-start.8 = (bf16[64,2048]{1,0:T(8,128)(2,1)S(1)}, bf16[64,2048]{1,0:T(8,128)(2,1)S(1)}, u32[]{:S(2)}, u32[]{:S(2)}) collective-permute-start(bf16[64,2048]{1,0:T(8,128)(2,1)S(1)} %get-tuple-element.111), channel_id=1, source_target_pairs={{0,2},{1,3},{2,0},{3,1},{4,6},{5,7},{6,4},{7,5},{8,10},{9,11},{10,... | collective-permute-start | bytes 786440 | tf_op jit(solution)/shard_map/ppermute | solution.py:594
  116.8 19.3 %collective-permute-start.10 = (bf16[64,2048]{1,0:T(8,128)(2,1)S(1)}, bf16[64,2048]{1,0:T(8,128)(2,1)S(1)}, u32[]{:S(2)}, u32[]{:S(2)}) collective-permute-start(bf16[64,2048]{1,0:T(8,128)(2,1)S(1)} %get-tuple-element.116), channel_id=1, source_target_pairs={{0,2},{1,3},{2,0},{3,1},{4,6},{5,7},{6,4},{7,5},{8,10},{9,11},{10,... | collective-permute-start | bytes 786440 | tf_op jit(solution)/shard_map/ppermute | solution.py:594
  117.9 19.5 %collective-permute-start.11 = (bf16[64,2048]{1,0:T(8,128)(2,1)S(1)}, bf16[64,2048]{1,0:T(8,128)(2,1)S(1)}, u32[]{:S(2)}, u32[]{:S(2)}) collective-permute-start(bf16[64,2048]{1,0:T(8,128)(2,1)S(1)} %get-tuple-element.118), channel_id=1, source_target_pairs={{4,0},{5,1},{6,2},{7,3},{12,8},{13,9},{14,10},{15,11},{16,20},{17,... | collective-permute-start | bytes 786440 | tf_op jit(solution)/shard_map/ppermute | solution.py:599
  119.2 34.3 %collective-permute-start.12 = (bf16[256,1024]{1,0:T(8,128)(2,1)S(1)}, bf16[256,1024]{1,0:T(8,128)(2,1)S(1)}, u32[]{:S(2)}, u32[]{:S(2)}) collective-permute-start(bf16[256,1024]{1,0:T(8,128)(2,1)S(1)} %get-tuple-element.122), channel_id=1, source_target_pairs={{0,1},{1,0},{2,3},{3,2},{4,5},{5,4},{6,7},{7,6},{8,9},{9,8},{10,11... | collective-permute-start | bytes 1572872 | tf_op jit(solution)/shard_map/ppermute | solution.py:582
  130.2 28.4 %collective-permute-start.15 = (bf16[256,1024]{1,0:T(8,128)(2,1)S(1)}, bf16[256,1024]{1,0:T(8,128)(2,1)S(1)}, u32[]{:S(2)}, u32[]{:S(2)}) collective-permute-start(bf16[256,1024]{1,0:T(8,128)(2,1)S(1)} %get-tuple-element.130), channel_id=1, source_target_pairs={{0,1},{1,0},{2,3},{3,2},{4,5},{5,4},{6,7},{7,6},{8,9},{9,8},{10,11... | collective-permute-start | bytes 1572872 | tf_op jit(solution)/shard_map/ppermute | solution.py:582
  136.1 9.8 %collective-permute-start.13 = (bf16[64,2048]{1,0:T(8,128)(2,1)S(1)}, bf16[64,2048]{1,0:T(8,128)(2,1)S(1)}, u32[]{:S(2)}, u32[]{:S(2)}) collective-permute-start(bf16[64,2048]{1,0:T(8,128)(2,1)S(1)} %get-tuple-element.124), channel_id=1, source_target_pairs={{0,2},{1,3},{2,0},{3,1},{4,6},{5,7},{6,4},{7,5},{8,10},{9,11},{10,... | collective-permute-start | bytes 786440 | tf_op jit(solution)/shard_map/ppermute | solution.py:594
  136.1 16.0 %collective-permute-start.14 = (bf16[64,2048]{1,0:T(8,128)(2,1)S(1)}, bf16[64,2048]{1,0:T(8,128)(2,1)S(1)}, u32[]{:S(2)}, u32[]{:S(2)}) collective-permute-start(bf16[64,2048]{1,0:T(8,128)(2,1)S(1)} %get-tuple-element.126), channel_id=1, source_target_pairs={{4,0},{5,1},{6,2},{7,3},{12,8},{13,9},{14,10},{15,11},{16,20},{17,... | collective-permute-start | bytes 786440 | tf_op jit(solution)/shard_map/ppermute | solution.py:599
  137.4 6.1 %copy-start.8 = (f32[11264]{0:T(1024)S(1)}, f32[11264]{0:T(1024)}, u32[]{:S(2)}) copy-start(f32[11264]{0:T(1024)} %param.11) | copy-start | bytes 135172
  140.6 29.2 %collective-permute-start.18 = (bf16[256,1024]{1,0:T(8,128)(2,1)S(1)}, bf16[256,1024]{1,0:T(8,128)(2,1)S(1)}, u32[]{:S(2)}, u32[]{:S(2)}) collective-permute-start(bf16[256,1024]{1,0:T(8,128)(2,1)S(1)} %get-tuple-element.138), channel_id=1, source_target_pairs={{0,1},{1,0},{2,3},{3,2},{4,5},{5,4},{6,7},{7,6},{8,9},{9,8},{10,11... | collective-permute-start | bytes 1572872 | tf_op jit(solution)/shard_map/ppermute | solution.py:582
  145.9 14.4 %collective-permute-start.16 = (bf16[128,1024]{1,0:T(8,128)(2,1)S(1)}, bf16[128,1024]{1,0:T(8,128)(2,1)S(1)}, u32[]{:S(2)}, u32[]{:S(2)}) collective-permute-start(bf16[128,1024]{1,0:T(8,128)(2,1)S(1)} %get-tuple-element.132), channel_id=1, source_target_pairs={{0,2},{1,3},{2,0},{3,1},{4,6},{5,7},{6,4},{7,5},{8,10},{9,11},{10,... | collective-permute-start | bytes 786440 | tf_op jit(solution)/shard_map/ppermute | solution.py:594
  152.1 10.1 %collective-permute-start.17 = (bf16[64,2048]{1,0:T(8,128)(2,1)S(1)}, bf16[64,2048]{1,0:T(8,128)(2,1)S(1)}, u32[]{:S(2)}, u32[]{:S(2)}) collective-permute-start(bf16[64,2048]{1,0:T(8,128)(2,1)S(1)} %get-tuple-element.134), channel_id=1, source_target_pairs={{0,4},{1,5},{2,6},{3,7},{8,12},{9,13},{10,14},{11,15},{20,16},{21,... | collective-permute-start | bytes 786440 | tf_op jit(solution)/shard_map/ppermute | solution.py:599
  157.3 12.5 %collective-permute-start.19 = (bf16[128,1024]{1,0:T(8,128)(2,1)S(1)}, bf16[128,1024]{1,0:T(8,128)(2,1)S(1)}, u32[]{:S(2)}, u32[]{:S(2)}) collective-permute-start(bf16[128,1024]{1,0:T(8,128)(2,1)S(1)} %get-tuple-element.140), channel_id=1, source_target_pairs={{0,2},{1,3},{2,0},{3,1},{4,6},{5,7},{6,4},{7,5},{8,10},{9,11},{10,... | collective-permute-start | bytes 786440 | tf_op jit(solution)/shard_map/ppermute | solution.py:594
  158.6 12.9 %collective-permute-start.20 = (bf16[64,2048]{1,0:T(8,128)(2,1)S(1)}, bf16[64,2048]{1,0:T(8,128)(2,1)S(1)}, u32[]{:S(2)}, u32[]{:S(2)}) collective-permute-start(bf16[64,2048]{1,0:T(8,128)(2,1)S(1)} %get-tuple-element.142), channel_id=1, source_target_pairs={{0,4},{1,5},{2,6},{3,7},{8,12},{9,13},{10,14},{11,15},{20,16},{21,... | collective-permute-start | bytes 786440 | tf_op jit(solution)/shard_map/ppermute | solution.py:599
  160.2 23.2 %collective-permute-start.21 = (bf16[256,1024]{1,0:T(8,128)(2,1)S(1)}, bf16[256,1024]{1,0:T(8,128)(2,1)S(1)}, u32[]{:S(2)}, u32[]{:S(2)}) collective-permute-start(bf16[256,1024]{1,0:T(8,128)(2,1)S(1)} %get-tuple-element.146), channel_id=1, source_target_pairs={{0,1},{1,0},{2,3},{3,2},{4,5},{5,4},{6,7},{7,6},{8,9},{9,8},{10,11... | collective-permute-start | bytes 1572872 | tf_op jit(solution)/shard_map/ppermute | solution.py:582
  166.0 14.1 %collective-permute-start.22 = (bf16[128,1024]{1,0:T(8,128)(2,1)S(1)}, bf16[128,1024]{1,0:T(8,128)(2,1)S(1)}, u32[]{:S(2)}, u32[]{:S(2)}) collective-permute-start(bf16[128,1024]{1,0:T(8,128)(2,1)S(1)} %get-tuple-element.148), channel_id=1, source_target_pairs={{0,2},{1,3},{2,0},{3,1},{4,6},{5,7},{6,4},{7,5},{8,10},{9,11},{10,... | collective-permute-start | bytes 786440 | tf_op jit(solution)/shard_map/ppermute | solution.py:594
  169.8 9.2 %collective-permute-start.23 = (bf16[64,1024]{1,0:T(8,128)(2,1)S(1)}, bf16[64,1024]{1,0:T(8,128)(2,1)S(1)}, u32[]{:S(2)}, u32[]{:S(2)}) collective-permute-start(bf16[64,1024]{1,0:T(8,128)(2,1)S(1)} %get-tuple-element.150), channel_id=1, source_target_pairs={{0,4},{1,5},{2,6},{3,7},{4,0},{5,1},{6,2},{7,3},{8,12},{9,13},{10,... | collective-permute-start | bytes 393224 | tf_op jit(solution)/shard_map/ppermute | solution.py:601
  169.8 22.5 %collective-permute-start.26 = (bf16[256,1024]{1,0:T(8,128)(2,1)S(1)}, bf16[256,1024]{1,0:T(8,128)(2,1)S(1)}, u32[]{:S(2)}, u32[]{:S(2)}) collective-permute-start(bf16[256,1024]{1,0:T(8,128)(2,1)S(1)} %get-tuple-element.158), channel_id=1, source_target_pairs={{0,1},{1,0},{2,3},{3,2},{4,5},{5,4},{6,7},{7,6},{8,9},{9,8},{10,11... | collective-permute-start | bytes 1572872 | tf_op jit(solution)/shard_map/ppermute | solution.py:582
  171.5 5.6 %slice-start.2 = ((f32[11264]{0:T(1024)}), f32[4096]{0:T(1024)S(1)}, s32[]{:S(2)}) async-start(f32[11264]{0:T(1024)} %param.11), calls=%async_computation.3 | async-start | bytes 32768 | tf_op jit(solution)/shard_map/slice | solution.py:510
  174.4 19.5 %collective-permute-start.27 = (bf16[128,1024]{1,0:T(8,128)(2,1)S(1)}, bf16[128,1024]{1,0:T(8,128)(2,1)S(1)}, u32[]{:S(2)}, u32[]{:S(2)}) collective-permute-start(bf16[128,1024]{1,0:T(8,128)(2,1)S(1)} %get-tuple-element.161), channel_id=1, source_target_pairs={{0,2},{1,3},{2,0},{3,1},{4,6},{5,7},{6,4},{7,5},{8,10},{9,11},{10,... | collective-permute-start | bytes 786440 | tf_op jit(solution)/shard_map/ppermute | solution.py:594
  179.0 18.8 %collective-permute-start.29 = (bf16[256,512]{1,0:T(8,128)(2,1)S(1)}, bf16[256,512]{1,0:T(8,128)(2,1)S(1)}, u32[]{:S(2)}, u32[]{:S(2)}) collective-permute-start(bf16[256,512]{1,0:T(8,128)(2,1)S(1)} %get-tuple-element.165), channel_id=1, source_target_pairs={{0,1},{1,0},{2,3},{3,2},{4,5},{5,4},{6,7},{7,6},{8,9},{9,8},{10,11... | collective-permute-start | bytes 786440 | tf_op jit(solution)/shard_map/ppermute | solution.py:582
  180.1 7.8 %collective-permute-start.24 = (bf16[64,1024]{1,0:T(8,128)(2,1)S(1)}, bf16[64,1024]{1,0:T(8,128)(2,1)S(1)}, u32[]{:S(2)}, u32[]{:S(2)}) collective-permute-start(bf16[64,1024]{1,0:T(8,128)(2,1)S(1)} %get-tuple-element.153), channel_id=1, source_target_pairs={{0,4},{1,5},{2,6},{3,7},{4,0},{5,1},{6,2},{7,3},{8,12},{9,13},{10,... | collective-permute-start | bytes 393224 | tf_op jit(solution)/shard_map/ppermute | solution.py:601
  183.5 2.7 %copy-start.14 = (f32[1024]{0:T(1024)S(1)}, f32[1024]{0:T(1024)}, u32[]{:S(2)}) copy-start(f32[1024]{0:T(1024)} %get-tuple-element.210) | copy-start | bytes 12292
  183.5 7.4 %copy-start.13 = (f32[1024]{0:T(1024)S(1)}, f32[1024]{0:T(1024)}, u32[]{:S(2)}) copy-start(f32[1024]{0:T(1024)} %get-tuple-element.209) | copy-start | bytes 12292
  186.0 13.7 %copy-start.12 = (f32[1024]{0:T(1024)S(1)}, f32[1024]{0:T(1024)}, u32[]{:S(2)}) copy-start(f32[1024]{0:T(1024)} %get-tuple-element.208) | copy-start | bytes 12292
  186.1 20.9 %copy-start.11 = (f32[1024]{0:T(1024)S(1)}, f32[1024]{0:T(1024)}, u32[]{:S(2)}) copy-start(f32[1024]{0:T(1024)} %get-tuple-element.207) | copy-start | bytes 12292
  186.1 13.7 %collective-permute-start.30 = (bf16[128,1024]{1,0:T(8,128)(2,1)S(1)}, bf16[128,1024]{1,0:T(8,128)(2,1)S(1)}, u32[]{:S(2)}, u32[]{:S(2)}) collective-permute-start(bf16[128,1024]{1,0:T(8,128)(2,1)S(1)} %get-tuple-element.168), channel_id=1, source_target_pairs={{0,2},{1,3},{2,0},{3,1},{4,6},{5,7},{6,4},{7,5},{8,10},{9,11},{10,... | collective-permute-start | bytes 786440 | tf_op jit(solution)/shard_map/ppermute | solution.py:594
  187.9 10.1 %collective-permute-start.25 = (bf16[64,1024]{1,0:T(8,128)(2,1)S(1)}, bf16[64,1024]{1,0:T(8,128)(2,1)S(1)}, u32[]{:S(2)}, u32[]{:S(2)}) collective-permute-start(bf16[64,1024]{1,0:T(8,128)(2,1)S(1)} %get-tuple-element.155), channel_id=1, source_target_pairs={{0,4},{1,5},{2,6},{3,7},{4,0},{5,1},{6,2},{7,3},{8,12},{9,13},{10,... | collective-permute-start | bytes 393224 | tf_op jit(solution)/shard_map/ppermute | solution.py:601
  192.3 10.8 %collective-permute-start.32 = (bf16[256,512]{1,0:T(8,128)(2,1)S(1)}, bf16[256,512]{1,0:T(8,128)(2,1)S(1)}, u32[]{:S(2)}, u32[]{:S(2)}) collective-permute-start(bf16[256,512]{1,0:T(8,128)(2,1)S(1)} %get-tuple-element.172), channel_id=1, source_target_pairs={{0,1},{1,0},{2,3},{3,2},{4,5},{5,4},{6,7},{7,6},{8,9},{9,8},{10,11... | collective-permute-start | bytes 786440 | tf_op jit(solution)/shard_map/ppermute | solution.py:582
  193.8 25.2 %copy-start.10 = (f32[1024]{0:T(1024)S(1)}, f32[1024]{0:T(1024)}, u32[]{:S(2)}) copy-start(f32[1024]{0:T(1024)} %get-tuple-element.206) | copy-start | bytes 12292
  193.9 13.2 %collective-permute-start.33 = (bf16[128,1024]{1,0:T(8,128)(2,1)S(1)}, bf16[128,1024]{1,0:T(8,128)(2,1)S(1)}, u32[]{:S(2)}, u32[]{:S(2)}) collective-permute-start(bf16[128,1024]{1,0:T(8,128)(2,1)S(1)} %get-tuple-element.174), channel_id=1, source_target_pairs={{0,2},{1,3},{2,0},{3,1},{4,6},{5,7},{6,4},{7,5},{8,10},{9,11},{10,... | collective-permute-start | bytes 786440 | tf_op jit(solution)/shard_map/ppermute | solution.py:594
  193.9 29.3 %copy-start.9 = (f32[1024]{0:T(1024)S(1)}, f32[1024]{0:T(1024)}, u32[]{:S(2)}) copy-start(f32[1024]{0:T(1024)} %get-tuple-element.205) | copy-start | bytes 12292
  198.0 12.1 %collective-permute-start.35 = (bf16[128,512]{1,0:T(8,128)(2,1)S(1)}, bf16[128,512]{1,0:T(8,128)(2,1)S(1)}, u32[]{:S(2)}, u32[]{:S(2)}) collective-permute-start(bf16[128,512]{1,0:T(8,128)(2,1)S(1)} %get-tuple-element.177), channel_id=1, source_target_pairs={{0,2},{1,3},{2,0},{3,1},{4,6},{5,7},{6,4},{7,5},{8,10},{9,11},{10,... | collective-permute-start | bytes 393224 | tf_op jit(solution)/shard_map/ppermute | solution.py:594
  198.1 8.9 %collective-permute-start.28 = (bf16[64,1024]{1,0:T(8,128)(2,1)S(1)}, bf16[64,1024]{1,0:T(8,128)(2,1)S(1)}, u32[]{:S(2)}, u32[]{:S(2)}) collective-permute-start(bf16[64,1024]{1,0:T(8,128)(2,1)S(1)} %get-tuple-element.163), channel_id=1, source_target_pairs={{0,4},{1,5},{2,6},{3,7},{4,0},{5,1},{6,2},{7,3},{8,12},{9,13},{10,... | collective-permute-start | bytes 393224 | tf_op jit(solution)/shard_map/ppermute | solution.py:601
  203.1 10.0 %collective-permute-start.37 = (bf16[128,512]{1,0:T(8,128)(2,1)S(1)}, bf16[128,512]{1,0:T(8,128)(2,1)S(1)}, u32[]{:S(2)}, u32[]{:S(2)}) collective-permute-start(bf16[128,512]{1,0:T(8,128)(2,1)S(1)} %get-tuple-element.180), channel_id=1, source_target_pairs={{0,2},{1,3},{2,0},{3,1},{4,6},{5,7},{6,4},{7,5},{8,10},{9,11},{10,... | collective-permute-start | bytes 393224 | tf_op jit(solution)/shard_map/ppermute | solution.py:594
  203.2 15.8 %collective-permute-start.31 = (bf16[64,1024]{1,0:T(8,128)(2,1)S(1)}, bf16[64,1024]{1,0:T(8,128)(2,1)S(1)}, u32[]{:S(2)}, u32[]{:S(2)}) collective-permute-start(bf16[64,1024]{1,0:T(8,128)(2,1)S(1)} %get-tuple-element.170), channel_id=1, source_target_pairs={{0,4},{1,5},{2,6},{3,7},{4,0},{5,1},{6,2},{7,3},{8,12},{9,13},{10,... | collective-permute-start | bytes 393224 | tf_op jit(solution)/shard_map/ppermute | solution.py:601
  210.1 13.2 %collective-permute-start.36 = (bf16[64,512]{1,0:T(8,128)(2,1)S(1)}, bf16[64,512]{1,0:T(8,128)(2,1)S(1)}, u32[]{:S(2)}, u32[]{:S(2)}) collective-permute-start(bf16[64,512]{1,0:T(8,128)(2,1)S(1)} %get-tuple-element.179), channel_id=1, source_target_pairs={{0,4},{1,5},{2,6},{3,7},{4,0},{5,1},{6,2},{7,3},{8,12},{9,13},{10,... | collective-permute-start | bytes 196616 | tf_op jit(solution)/shard_map/ppermute | solution.py:601
  210.6 12.6 %collective-permute-start.34 = (bf16[64,1024]{1,0:T(8,128)(2,1)S(1)}, bf16[64,1024]{1,0:T(8,128)(2,1)S(1)}, u32[]{:S(2)}, u32[]{:S(2)}) collective-permute-start(bf16[64,1024]{1,0:T(8,128)(2,1)S(1)} %get-tuple-element.176), channel_id=1, source_target_pairs={{0,4},{1,5},{2,6},{3,7},{4,0},{5,1},{6,2},{7,3},{8,12},{9,13},{10,... | collective-permute-start | bytes 393224 | tf_op jit(solution)/shard_map/ppermute | solution.py:601
  213.2 10.8 %collective-permute-start.38 = (bf16[64,512]{1,0:T(8,128)(2,1)S(1)}, bf16[64,512]{1,0:T(8,128)(2,1)S(1)}, u32[]{:S(2)}, u32[]{:S(2)}) collective-permute-start(bf16[64,512]{1,0:T(8,128)(2,1)S(1)} %get-tuple-element.182), channel_id=1, source_target_pairs={{0,4},{1,5},{2,6},{3,7},{4,0},{5,1},{6,2},{7,3},{8,12},{9,13},{10,... | collective-permute-start | bytes 196616 | tf_op jit(solution)/shard_map/ppermute | solution.py:601
  224.0 12.4 %copy-start.7 = (f32[64,11264]{1,0:T(8,128)}, f32[64,11264]{1,0:T(8,128)S(1)}, u32[]{:S(2)}) copy-start(f32[64,11264]{1,0:T(8,128)S(1)} %get-tuple-element.200) | copy-start | bytes 8650756
  224.0 4.1 %collective-permute-start.39 = (f32[11264]{0:T(1024)S(1)}, f32[11264]{0:T(1024)S(1)}, u32[]{:S(2)}, u32[]{:S(2)}) collective-permute-start(f32[11264]{0:T(1024)S(1)} %constant_dynamic-update-slice_fusion.2), channel_id=1, source_target_pairs={{0,1},{1,0},{2,3},{3,2},{4,5},{5,4},{6,7},{7,6},{8,9},{9,8},{10,11... | collective-permute-start | bytes 135176 | tf_op jit(solution)/shard_map/ppermute | solution.py:456
  228.2 6.3 %collective-permute-start.42 = (f32[11264]{0:T(1024)S(1)}, f32[11264]{0:T(1024)S(1)}, u32[]{:S(2)}, u32[]{:S(2)}) collective-permute-start(f32[11264]{0:T(1024)S(1)} %max.12), channel_id=1, source_target_pairs={{0,6},{1,7},{2,4},{3,5},{4,2},{5,3},{6,0},{7,1},{8,14},{9,15},{10,... | collective-permute-start | bytes 135176 | tf_op jit(solution)/shard_map/ppermute | solution.py:456
  230.8 4.9 %collective-permute-start.41 = (f32[11264]{0:T(1024)S(1)}, f32[11264]{0:T(1024)S(1)}, u32[]{:S(2)}, u32[]{:S(2)}) collective-permute-start(f32[11264]{0:T(1024)S(1)} %max.12), channel_id=1, source_target_pairs={{0,4},{1,5},{2,6},{3,7},{4,0},{5,1},{6,2},{7,3},{8,12},{9,13},{10,... | collective-permute-start | bytes 135176 | tf_op jit(solution)/shard_map/ppermute | solution.py:456
  230.8 4.9 %collective-permute-start.40 = (f32[11264]{0:T(1024)S(1)}, f32[11264]{0:T(1024)S(1)}, u32[]{:S(2)}, u32[]{:S(2)}) collective-permute-start(f32[11264]{0:T(1024)S(1)} %max.12), channel_id=1, source_target_pairs={{0,2},{1,3},{2,0},{3,1},{4,6},{5,7},{6,4},{7,5},{8,10},{9,11},{10,... | collective-permute-start | bytes 135176 | tf_op jit(solution)/shard_map/ppermute | solution.py:456
